TPU v7x, 32 devices: a whole 2x2x4 slice. The times are simulated.
32 devices in a mesh: var: 8 (over z, y), seg: 4 (over x, core).
Axes of the slice: x: 2, y: 2, z: 4, core: 2. Of those that a mesh axis runs over, the one named last changes fastest.
Arguments:
- tokens: bfloat16 [32, 32, 64, 256], P('seg', 'var'), may hold values from -6 to 6
- domain: int32 [32], P('seg'), may hold values from 0 to 3, as said below
- counts: int32 [4], replicated, may hold values from 1 to 32, as said below
- domain_mean: float32 [4, 256], replicated, may hold values from -3 to 3
- domain_scale: float32 [4, 256], replicated, may hold values from 0.5 to 2
- attn_inner: bfloat16 [3, 3, 256, 256], replicated, may hold values from -0.375 to 0.375
- attn_outer: bfloat16 [3, 256, 256], replicated, may hold values from -1 to 1
- attn_bias: float32 [3, 3, 256], replicated, may hold values from -1.2 to 1.2
- mlp_in: bfloat16 [2, 256, 512], replicated, may hold values from -0.375 to 0.375
- mlp_in_bias: float32 [2, 512], replicated, may hold values from -1.2 to 1.2
- mlp_out: bfloat16 [2, 512, 256], replicated, may hold values from -0.375 to 0.375
- mlp_out_bias: float32 [2, 256], replicated, may hold values from -1.2 to 1.2
- norm_gain: float32 [4, 256], replicated, may hold values from 0.5 to 1.5
- norm_bias: float32 [4, 256], replicated, may hold values from -1.2 to 1.2
- router: bfloat16 [64, 10, 256], replicated, may hold values from -6 to 6
- cotangent: bfloat16 [32, 32, 64, 256], P('seg', 'var'), may hold values from -6 to 6
Outputs:
- output: float32 [32, 32, 64, 256], P('seg', 'var')
- input_grad: float32 [32, 32, 64, 256], P('seg', 'var')
- grad_attn_inner: float32 [3, 3, 256, 256], replicated
- grad_attn_outer: float32 [3, 256, 256], replicated
- grad_attn_bias: float32 [3, 3, 256], replicated
- grad_mlp_in: float32 [2, 256, 512], replicated
- grad_mlp_in_bias: float32 [2, 512], replicated
- grad_mlp_out: float32 [2, 512, 256], replicated
- grad_mlp_out_bias: float32 [2, 256], replicated
- grad_norm_gain: float32 [4, 256], replicated
- grad_norm_bias: float32 [4, 256], replicated
- grad_router: float32 [64, 10, 256], replicated
Inputs may be any that keep to these rules, and one draw needn't show every extreme that they name: The 8 series of one index of seg include one whose domain has 32 variables. Variables numbered counts[domain] and above are padding.
All inputs are finite; a program needn't handle non-finite values.
Results may differ from a plain program's by a relative error of at most 0.035.
The roundings to bfloat16 on the way count: a program that leaves them out, or rounds other values in their place, can miss the bound.
Values may be sent and summed in bfloat16 or wider, within the bound.
A program may use at most 320 MiB of HBM per device.

v0:
```python
import jax
import jax.numpy as jnp
from jax import lax
from jax.sharding import PartitionSpec as P

HEADS = 8


highest = lax.Precision.HIGHEST
epsilon = 1e-05
masked_score = -1e30


def layer_norm(values, gain, shift):
    center = values - jnp.mean(values, axis=-1, keepdims=True)
    spread = jnp.mean(center * center, axis=-1, keepdims=True)
    return center * lax.rsqrt(spread + epsilon) * gain + shift


def dense(values, weight):
    flat = values.reshape(-1, values.shape[-1])
    result = jnp.dot(flat, weight, preferred_element_type=jnp.float32)
    return result.reshape(values.shape[:-1] + (weight.shape[1],))


def weight_term(values, grads):
    flat_values = values.reshape(-1, values.shape[-1])
    flat_grads = grads.reshape(-1, grads.shape[-1])
    return jnp.einsum("nk,nm->km", flat_values, flat_grads, preferred_element_type=jnp.float32)


def back_term(grads, weight):
    flat = grads.reshape(-1, grads.shape[-1])
    result = jnp.einsum("nm,km->nk", flat, weight, preferred_element_type=jnp.float32)
    return result.reshape(grads.shape[:-1] + (weight.shape[0],))


def column_sums(grads):
    return jnp.sum(grads.reshape(-1, grads.shape[-1]).astype(jnp.float32), axis=0)


def split_heads(values):
    return values.reshape(values.shape[:-1] + (HEADS, values.shape[-1] // HEADS))


def on_device(
    tokens,
    domain,
    counts,
    domain_mean,
    domain_scale,
    attn_inner,
    attn_outer,
    attn_bias,
    mlp_in,
    mlp_in_bias,
    mlp_out,
    mlp_out_bias,
    norm_gain,
    norm_bias,
    router,
    cotangent,
):
    batch, local_vars, segs, width = tokens.shape
    routers = router.shape[1]
    domains = counts.shape[0]
    scale = (width // HEADS) ** (-0.5)
    picks = domain[:, None] == jnp.arange(domains, dtype=jnp.int32)[None, :]
    offset = jnp.sum(jnp.where(picks[:, :, None], domain_mean[None], 0.0), axis=1)
    factor = jnp.sum(jnp.where(picks[:, :, None], domain_scale[None], 0.0), axis=1)
    limit = jnp.sum(jnp.where(picks, counts[None, :], 0), axis=1)
    first_var = lax.axis_index("var") * local_vars
    valid = (first_var + jnp.arange(local_vars, dtype=jnp.int32))[None, :] < limit[:, None]
    start = (tokens.astype(jnp.float32) - offset[:, None, None, :]) * factor[:, None, None, :]
    start_low = start.astype(jnp.bfloat16)
    time_query = (dense(start_low, attn_inner[0, 0]) + attn_bias[0, 0]).astype(jnp.bfloat16)
    time_key = dense(start_low, attn_inner[0, 1]).astype(jnp.bfloat16)
    time_value = (dense(start_low, attn_inner[0, 2]) + attn_bias[0, 1]).astype(jnp.bfloat16)

    def time_scores():
        return (
            jnp.einsum(
                "bvshe,bvthe->bvhst",
                split_heads(time_query),
                split_heads(time_key),
                preferred_element_type=jnp.float32,
            )
            * scale
        )

    scores = time_scores()
    time_top = jnp.max(scores, axis=-1, keepdims=True)
    expo = jnp.exp(scores - time_top)
    time_total = jnp.sum(expo, axis=-1, keepdims=True)
    time_prob = (expo / time_total).astype(jnp.bfloat16)
    context = jnp.einsum(
        "bvhst,bvthe->bvshe", time_prob, split_heads(time_value), preferred_element_type=jnp.float32
    )
    context = context.reshape(tokens.shape).astype(jnp.bfloat16)
    branch_one = dense(context, attn_outer[0]) + attn_bias[0, 2]
    norm_one, pull_one = jax.vjp(layer_norm, start + branch_one, norm_gain[0], norm_bias[0])

    def feed_forward(values, index):
        values_low = values.astype(jnp.bfloat16)
        inner = dense(values_low, mlp_in[index]) + mlp_in_bias[index]
        active, pull_gelu = jax.vjp(jax.nn.gelu, inner)
        active_low = active.astype(jnp.bfloat16)
        outer = dense(active_low, mlp_out[index]) + mlp_out_bias[index]
        return (outer, (values_low, active_low, pull_gelu))

    def feed_back(grad_out, kept, index):
        values_low, active_low, pull_gelu = kept
        out_low = grad_out.astype(jnp.bfloat16)
        grad_second = weight_term(active_low, out_low)
        grad_second_bias = column_sums(out_low)
        (inner_grad,) = pull_gelu(back_term(out_low, mlp_out[index]))
        inner_low = inner_grad.astype(jnp.bfloat16)
        grad_first = weight_term(values_low, inner_low)
        grad_first_bias = column_sums(inner_low)
        return (
            back_term(inner_low, mlp_in[index]),
            (grad_first, grad_first_bias, grad_second, grad_second_bias),
        )

    mlp_first, kept_first = feed_forward(norm_one, 0)
    norm_two, pull_two = jax.vjp(layer_norm, norm_one + mlp_first, norm_gain[1], norm_bias[1])
    series_low = norm_two.astype(jnp.bfloat16)
    send_query = (dense(router, attn_inner[1, 0]) + attn_bias[1, 0]).astype(jnp.bfloat16)
    query_heads = split_heads(send_query)
    send_key = dense(series_low, attn_inner[1, 1]).astype(jnp.bfloat16)
    send_value = (dense(series_low, attn_inner[1, 2]) + attn_bias[1, 1]).astype(jnp.bfloat16)

    def send_scores(keys, rows_valid):
        raw = (
            jnp.einsum(
                "srhe,bvshe->bsrhv",
                query_heads,
                split_heads(keys),
                preferred_element_type=jnp.float32,
            )
            * scale
        )
        return jnp.where(rows_valid[:, None, None, None, :], raw, masked_score)

    local_top = jnp.max(send_scores(send_key, valid), axis=-1)
    top = lax.pmax(local_top, "var")
    weights = jnp.exp(send_scores(send_key, valid) - top[..., None]) * valid[
        :, None, None, None, :
    ].astype(jnp.float32)
    total = jnp.sum(weights, axis=-1)
    summed = jnp.einsum(
        "bsrhv,bvshe->bsrhe",
        weights,
        split_heads(send_value).astype(jnp.float32),
        precision=highest,
    )
    part_total = total
    part_summed = summed
    total, summed = lax.psum((part_total, part_summed), "var")
    gathered = summed / total[..., None]
    gathered_low = gathered.reshape(batch, segs, routers, width).astype(jnp.bfloat16)
    buffer = (dense(gathered_low, attn_outer[1]) + attn_bias[1, 2]).astype(jnp.bfloat16)
    recv_query = (dense(series_low, attn_inner[2, 0]) + attn_bias[2, 0]).astype(jnp.bfloat16)
    recv_key = dense(buffer, attn_inner[2, 1]).astype(jnp.bfloat16)
    recv_value = (dense(buffer, attn_inner[2, 2]) + attn_bias[2, 1]).astype(jnp.bfloat16)
    recv_scores = (
        jnp.einsum(
            "bvshe,bsrhe->bvshr",
            split_heads(recv_query),
            split_heads(recv_key),
            preferred_element_type=jnp.float32,
        )
        * scale
    )
    recv_prob, pull_soft = jax.vjp(lambda values: jax.nn.softmax(values, axis=-1), recv_scores)
    recv_out = jnp.einsum(
        "bvshr,bsrhe->bvshe",
        recv_prob,
        split_heads(recv_value).astype(jnp.float32),
        precision=highest,
    )
    recv_out = recv_out.reshape(tokens.shape).astype(jnp.bfloat16)
    branch_three = dense(recv_out, attn_outer[2]) + attn_bias[2, 2]
    norm_three, pull_three = jax.vjp(
        layer_norm, norm_two + branch_three, norm_gain[2], norm_bias[2]
    )
    mlp_second, kept_second = feed_forward(norm_three, 1)
    output, pull_four = jax.vjp(layer_norm, norm_three + mlp_second, norm_gain[3], norm_bias[3])
    grad_four, gain_four, shift_four = pull_four(cotangent.astype(jnp.float32))
    back_second, grads_second = feed_back(grad_four, kept_second, 1)
    grad_three, gain_three, shift_three = pull_three(grad_four + back_second)
    recv_low = grad_three.astype(jnp.bfloat16)
    grad_outer_recv = weight_term(recv_out, recv_low)
    grad_obias_recv = column_sums(recv_low)
    recv_grad_full = back_term(recv_low, attn_outer[2]).astype(jnp.bfloat16)
    recv_grad = split_heads(recv_grad_full)
    prob_grad = jnp.einsum(
        "bvshe,bsrhe->bvshr", recv_grad, split_heads(recv_value), preferred_element_type=jnp.float32
    )
    (score_grad,) = pull_soft(prob_grad)
    score_grad = score_grad * scale
    value_part = jnp.einsum(
        "bvshr,bvshe->bsrhe", recv_prob, recv_grad.astype(jnp.float32), precision=highest
    )
    key_part = jnp.einsum(
        "bvshr,bvshe->bsrhe",
        score_grad,
        split_heads(recv_query).astype(jnp.float32),
        precision=highest,
    )
    query_recv = jnp.einsum(
        "bvshr,bsrhe->bvshe",
        score_grad,
        split_heads(recv_key).astype(jnp.float32),
        precision=highest,
    )
    query_recv = query_recv.reshape(tokens.shape).astype(jnp.bfloat16)
    key_sum, value_sum = lax.psum((key_part, value_part), "var")
    share = (lax.axis_index("var") == 0).astype(jnp.float32)
    key_low = key_sum.reshape(batch, segs, routers, width).astype(jnp.bfloat16)
    value_low = value_sum.reshape(batch, segs, routers, width).astype(jnp.bfloat16)
    grad_inner_rq = weight_term(series_low, query_recv)
    grad_bias_rq = column_sums(query_recv)
    grad_inner_rk = weight_term(buffer, key_low) * share
    grad_inner_rv = weight_term(buffer, value_low) * share
    grad_bias_rv = column_sums(value_low) * share
    buffer_grad = (
        back_term(key_low, attn_inner[2, 1]) + back_term(value_low, attn_inner[2, 2])
    ).astype(jnp.bfloat16)
    grad_outer_send = weight_term(gathered_low, buffer_grad) * share
    grad_obias_send = column_sums(buffer_grad) * share
    pre_grad = split_heads(back_term(buffer_grad, attn_outer[1]).astype(jnp.bfloat16)).astype(
        jnp.float32
    )
    valid_float = valid[:, None, None, None, :].astype(jnp.float32)
    prob_send = (
        jnp.exp(send_scores(send_key, valid) - top[..., None]) * valid_float / total[..., None]
    )
    value_dot = jnp.einsum(
        "bsrhe,bvshe->bsrhv",
        pre_grad,
        split_heads(send_value).astype(jnp.float32),
        precision=highest,
    )
    center = jnp.sum(pre_grad * gathered, axis=-1)
    send_grad = prob_send * (value_dot - center[..., None]) * scale
    value_send = (
        jnp.einsum("bsrhv,bsrhe->bvshe", prob_send, pre_grad, precision=highest)
        .reshape(tokens.shape)
        .astype(jnp.bfloat16)
    )
    key_send = (
        jnp.einsum(
            "bsrhv,srhe->bvshe", send_grad, query_heads.astype(jnp.float32), precision=highest
        )
        .reshape(tokens.shape)
        .astype(jnp.bfloat16)
    )
    query_send = jnp.einsum(
        "bsrhv,bvshe->srhe", send_grad, split_heads(send_key).astype(jnp.float32), precision=highest
    ).reshape(segs, routers, width)
    grad_inner_sk = weight_term(series_low, key_send)
    grad_inner_sv = weight_term(series_low, value_send)
    grad_bias_sv = column_sums(value_send)
    grad_inner_sq = jnp.einsum(
        "srd,srf->df", router.astype(jnp.float32), query_send, precision=highest
    )
    grad_bias_sq = jnp.sum(query_send, axis=(0, 1))
    grad_router = jnp.einsum(
        "srf,df->srd", query_send, attn_inner[1, 0].astype(jnp.float32), precision=highest
    )
    grad_series = (
        grad_three
        + back_term(query_recv, attn_inner[2, 0])
        + back_term(key_send, attn_inner[1, 1])
        + back_term(value_send, attn_inner[1, 2])
    )
    grad_two, gain_two, shift_two = pull_two(grad_series)
    back_first, grads_first = feed_back(grad_two, kept_first, 0)
    grad_one, gain_one, shift_one = pull_one(grad_two + back_first)
    time_low = grad_one.astype(jnp.bfloat16)
    grad_outer_time = weight_term(context, time_low)
    grad_obias_time = column_sums(time_low)
    context_grad = split_heads(back_term(time_low, attn_outer[0]).astype(jnp.bfloat16))
    again = jnp.exp(time_scores() - time_top) / time_total
    again_grad = jnp.einsum(
        "bvshe,bvthe->bvhst",
        context_grad,
        split_heads(time_value),
        preferred_element_type=jnp.float32,
    )
    value_time = jnp.einsum(
        "bvhst,bvshe->bvthe",
        again.astype(jnp.bfloat16),
        context_grad,
        preferred_element_type=jnp.float32,
    )
    value_time = value_time.reshape(tokens.shape).astype(jnp.bfloat16)
    score_low = (again * (again_grad - jnp.sum(again * again_grad, axis=-1, keepdims=True))).astype(
        jnp.bfloat16
    )
    query_time = (
        jnp.einsum(
            "bvhst,bvthe->bvshe",
            score_low,
            split_heads(time_key),
            preferred_element_type=jnp.float32,
        )
        * scale
    )
    query_time = query_time.reshape(tokens.shape).astype(jnp.bfloat16)
    key_time = (
        jnp.einsum(
            "bvhst,bvshe->bvthe",
            score_low,
            split_heads(time_query),
            preferred_element_type=jnp.float32,
        )
        * scale
    )
    key_time = key_time.reshape(tokens.shape).astype(jnp.bfloat16)
    grad_inner_tq = weight_term(start_low, query_time)
    grad_inner_tk = weight_term(start_low, key_time)
    grad_inner_tv = weight_term(start_low, value_time)
    grad_bias_tq = column_sums(query_time)
    grad_bias_tv = column_sums(value_time)
    grad_start = (
        grad_one
        + back_term(query_time, attn_inner[0, 0])
        + back_term(key_time, attn_inner[0, 1])
        + back_term(value_time, attn_inner[0, 2])
    )
    input_grad = grad_start * factor[:, None, None, :]
    grad_inner = jnp.stack(
        [
            jnp.stack([grad_inner_tq, grad_inner_tk, grad_inner_tv]),
            jnp.stack([grad_inner_sq, grad_inner_sk, grad_inner_sv]),
            jnp.stack([grad_inner_rq, grad_inner_rk, grad_inner_rv]),
        ]
    )
    grad_outer = jnp.stack([grad_outer_time, grad_outer_send, grad_outer_recv])
    grad_bias = jnp.stack(
        [
            jnp.stack([grad_bias_tq, grad_bias_tv, grad_obias_time]),
            jnp.stack([grad_bias_sq, grad_bias_sv, grad_obias_send]),
            jnp.stack([grad_bias_rq, grad_bias_rv, grad_obias_recv]),
        ]
    )
    grad_up = jnp.stack([grads_first[0], grads_second[0]])
    grad_up_bias = jnp.stack([grads_first[1], grads_second[1]])
    grad_down = jnp.stack([grads_first[2], grads_second[2]])
    grad_down_bias = jnp.stack([grads_first[3], grads_second[3]])
    grad_gain = jnp.stack([gain_one, gain_two, gain_three, gain_four])
    grad_shift = jnp.stack([shift_one, shift_two, shift_three, shift_four])
    totals = lax.psum(
        (
            grad_inner,
            grad_outer,
            grad_bias,
            grad_up,
            grad_up_bias,
            grad_down,
            grad_down_bias,
            grad_gain,
            grad_shift,
            grad_router,
        ),
        ("var", "seg"),
    )
    return (
        output,
        input_grad,
        totals[0],
        totals[1],
        totals[2],
        totals[3],
        totals[4],
        totals[5],
        totals[6],
        totals[7],
        totals[8],
        totals[9],
    )


def solution(mesh):
    in_specs = (
        P("seg", "var", None, None),
        P("seg"),
        P(),
        P(),
        P(),
        P(),
        P(),
        P(),
        P(),
        P(),
        P(),
        P(),
        P(),
        P(),
        P(),
        P("seg", "var", None, None),
    )
    out_specs = (
        P("seg", "var", None, None),
        P("seg", "var", None, None),
        P(),
        P(),
        P(),
        P(),
        P(),
        P(),
        P(),
        P(),
        P(),
        P(),
    )
    return jax.shard_map(
        on_device, mesh=mesh, in_specs=in_specs, out_specs=out_specs, check_vma=False
    )
```

profile of v0, /device:TPU:29, one launch (start us, length us, event | category | flops | bytes accessed | tf_op | source)
XLA Modules:
  0.0 2197.6 jit_solution(2666842778561737390)
XLA Ops:
  92.4 88.0 %all-reduce.9.cloned.1.call-done = f32[8,64,10,8]{2,0,3,1:T(8,128)} async-done(((f32[8,64,10,8]{2,0,3,1:T(8,128)}), f32[8,64,10,8]{2,0,3,1:T(8,128)}) %all-reduce.9.cloned.1.call-update) | async-done | bytes 163856 | tf_op jit(solution)/shard_map/pmax | solution.py:146
  191.0 30.2 %fusion.12 = f32[8,64,8,32,10]{3,4,2,1,0:T(8,128)} fusion(bf16[8,4,64,8,32]{4,1,3,2,0:T(4,128)(2,1)S(1)} %copy-done.10, f32[8,64,10,8,4]{2,0,4,3,1:T(8,128)S(1)} %get-tuple-element.57), kind=kOutput, calls=%fused_computation.21 | convolution fusion | flops 62914560 | bytes 6946816 | tf_op jit(solution)/shard_map/bsrhv,bvshe->bsrhe/dot_general | solution.py:151
  221.2 23.4 %copy.362 = f32[8,64,8,32,10]{1,3,2,4,0:T(8,128)} copy(f32[8,64,8,32,10]{3,4,2,1,0:T(8,128)} %fusion.12) | data formatting | bytes 10485760 | tf_op jit(solution)/shard_map/bsrhv,bvshe->bsrhe/dot_general | solution.py:151
  258.7 383.1 %all-reduce.13.cloned.1.call-done = (f32[8,64,10,8,32]{1,4,3,2,0:T(8,128)}, f32[8,64,10,8]{2,0,3,1:T(8,128)}) async-done(((f32[8,64,10,8,32]{1,4,3,2,0:T(8,128)}, f32[8,64,10,8]{2,0,3,1:T(8,128)}), (f32[8,64,10,8,32]{1,4,3,2,0:T(8,128)}, f32[8,64,10,8]{2,0,3,1:T(8,128)})) %all-reduce.13.cloned.1.call-update) | async-done | bytes 5406736 | tf_op jit(solution)/shard_map/psum | solution.py:159
  680.6 25.2 %copy.368 = bf16[8,64,10,8,32]{4,2,3,1,0:T(8,128)(2,1)} copy(bf16[8,64,10,8,32]{1,4,3,2,0:T(8,128)(2,1)} %bitcast.518) | data formatting | bytes 5242880 | tf_op jit(solution)/shard_map/reshape | solution.py:43
  705.8 16.9 bitcast_reduce_fusion
  722.7 11.3 fusion.164
  736.1 25.2 %copy.370 = bf16[8,64,10,8,32]{4,2,3,1,0:T(8,128)(2,1)} copy(bf16[8,64,10,8,32]{1,4,3,2,0:T(8,128)(2,1)} %bitcast.517) | data formatting | bytes 5242880 | tf_op jit(solution)/shard_map/reshape | solution.py:43
  761.3 22.0 %fusion.40 = bf16[8,4,64,8,32]{4,1,3,2,0:T(4,128)(2,1)} fusion(bf16[8,64,10,8,32]{4,2,3,1,0:T(8,128)(2,1)} %copy.370, f32[8,4,64,8]{1,3,2,0:T(8,128)} %copy-done.20, f32[8,64,8,10,4]{3,4,2,1,0:T(4,128)} %get-tuple-element.93, f32[8,4,64,8]{1,3,2,0:T(8,128)} %get-tuple-element.92), kind=kOutput, calls=%fused_computation.73 | convolution fusion | flops 63930368 | bytes 4456448 | tf_op jit(solution)/shard_map/bvshr,bsrhe->bvshe/dot_general | solution.py:176
  833.4 18.5 fusion.6
  852.1 18.0 fusion.14
  870.2 16.3 convert_reduce_fusion.1
  898.2 42.7 %fusion.161 = f32[8,64,8,32,10]{3,4,2,1,0:T(8,128)} fusion(bf16[8,4,64,8,32]{4,1,3,2,0:T(4,128)(2,1)} %copy.375, f32[8,4,64,8]{1,3,2,0:T(8,128)} %copy-done.20, f32[8,64,8,10,4]{3,4,2,1,0:T(4,128)} %get-tuple-element.93, f32[8,4,64,8]{1,3,2,0:T(8,128)} %get-tuple-element.92), kind=kOutput, calls=%fused_computation.283 | convolution fusion | flops 63406080 | bytes 7077888 | tf_op jit(solution)/shard_map/bvshr,bvshe->bsrhe/dot_general | solution.py:202
  940.9 30.3 %fusion.182 = f32[8,64,8,32,10]{3,4,2,1,0:T(8,128)} fusion(bf16[8,4,64,8,32]{4,1,3,2,0:T(4,128)(2,1)S(1)} %copy-done.9, f32[8,4,64,8,10]{4,1,3,2,0:T(4,128)S(1)} %bitcast.506), kind=kOutput, calls=%fused_computation.301 | convolution fusion | flops 62914560 | bytes 6946816 | tf_op jit(solution)/shard_map/bvshr,bvshe->bsrhe/dot_general | solution.py:205
  971.2 23.4 %copy.383 = f32[8,64,8,32,10]{1,3,2,4,0:T(8,128)} copy(f32[8,64,8,32,10]{3,4,2,1,0:T(8,128)} %fusion.161) | data formatting | bytes 10485760 | tf_op jit(solution)/shard_map/bvshr,bvshe->bsrhe/dot_general | solution.py:202
  994.6 23.4 %copy.380 = f32[8,64,8,32,10]{1,3,2,4,0:T(8,128)} copy(f32[8,64,8,32,10]{3,4,2,1,0:T(8,128)} %fusion.182) | data formatting | bytes 10485760 | tf_op jit(solution)/shard_map/bvshr,bvshe->bsrhe/dot_general | solution.py:205
  1018.0 803.0 %all-reduce.14 = (bf16[8,64,10,8,32]{1,4,3,2,0:T(8,128)(2,1)}, bf16[8,64,10,8,32]{1,4,3,2,0:T(8,128)(2,1)}) all-reduce(f32[8,64,10,8,32]{1,4,3,2,0:T(8,128)} %bitcast.512, f32[8,64,10,8,32]{1,4,3,2,0:T(8,128)} %bitcast.511), channel_id=1, replica_groups=mesh['var'=8,'seg'=4] {'var'}, use_global_device_ids=true, to_apply=%region_25.26 | all-reduce | flops 2621440 | bytes 15728640 | tf_op jit(solution)/shard_map/psum | solution.py:218
  1852.2 25.2 %copy.387 = bf16[8,64,10,8,32]{4,2,3,1,0:T(8,128)(2,1)} copy(bf16[8,64,10,8,32]{1,4,3,2,0:T(8,128)(2,1)} %bitcast.509) | data formatting | bytes 5242880 | tf_op jit(solution)/shard_map/reshape | solution.py:43
  1877.4 12.4 fusion.183
  1889.8 23.0 %convert_reduce_fusion.2 = (f32[8,32]{1,0:T(8,128)S(1)}, bf16[8,4,64,8,32]{4,1,3,2,0:T(4,128)(2,1)}) fusion(bf16[8,64,10,8,32]{4,2,3,1,0:T(8,128)(2,1)} %copy.387, f32[8,64,10,8,4]{2,0,4,3,1:T(8,128)} %broadcast_divide_fusion.1), kind=kOutput, calls=%fused_computation.24 | convolution fusion | flops 64487168 | bytes 4326400 | tf_op jit(solution)/shard_map/bsrhv,bsrhe->bvshe/dot_general | solution.py:248
  1912.8 14.1 fusion.181
  1926.9 15.4 convert_bitcast_fusion
  2033.5 41.1 %all-reduce = (f32[3,3,256]{2,1,0:T(4,128)}, f32[2,512]{1,0:T(2,128)}, f32[2,256]{1,0:T(2,128)}, f32[4,256]{1,0:T(4,128)}, f32[4,256]{1,0:T(4,128)}) all-reduce(f32[3,3,256]{2,1,0:T(4,128)S(1)} %pad_maximum_fusion.4, f32[2,512]{1,0:T(2,128)S(1)} %pad_maximum_fusion.5, ...), channel_id=1, replica_groups=mesh['var'=8,'seg'=4] {'var','seg'}, use_global_device_ids=true, to_apply=%region_44.45 | all-reduce | flops 5888 | bytes 47104 | tf_op jit(solution)/shard_map/psum | solution.py:355
  2082.3 101.6 %all-reduce.11.cloned.1.call-done = (f32[3,3,256,256]{3,2,1,0:T(8,128)}, f32[3,256,256]{2,1,0:T(8,128)}, f32[2,256,512]{2,1,0:T(8,128)}, f32[2,512,256]{2,1,0:T(8,128)}, f32[64,10,256]{2,0,1:T(8,128)}) async-done(((f32[3,3,256,256]{3,2,1,0:T(8,128)}, f32[3,256,256]{2,1,0:T(8,128)}, f32[2,256,512]{2,1,0:T(8,128)}, f32[2,512,256]{2,1,0:T(8,128)}, f32[64,10,256]{2,0,1:T(8,128)}), ...) | async-done | bytes 5898256 | tf_op jit(solution)/shard_map/psum | solution.py:355
  (404 shorter events, 348.4 us)
Async XLA Ops:
  7.2 173.2 %all-reduce.9.cloned.1.call-start = ((), (), s32[]{:S(2)}) async-start(), calls=%async_computation | async-start | bytes 4194304 | tf_op jit(solution)/shard_map/pmax | solution.py:146
  11.4 40.0 %copy-start.84 = (f32[1,256]{1,0:T(1,128)}, f32[1,256]{1,0:T(1,128)S(1)}, u32[]{:S(2)}) copy-start(f32[1,256]{1,0:T(1,128)S(1)} %get-tuple-element.74) | copy-start | bytes 3076
  11.4 779.8 %copy-start.88 = (f32[1,256]{1,0:T(1,128)}, f32[1,256]{1,0:T(1,128)S(1)}, u32[]{:S(2)}) copy-start(f32[1,256]{1,0:T(1,128)S(1)} %get-tuple-element.73) | copy-start | bytes 3076
  12.9 38.6 %copy-start.91 = (f32[1,256]{1,0:T(1,128)}, f32[1,256]{1,0:T(1,128)S(1)}, u32[]{:S(2)}) copy-start(f32[1,256]{1,0:T(1,128)S(1)} %get-tuple-element.78) | copy-start | bytes 3076
  14.2 37.2 %copy-start.102 = (f32[1,512]{1,0:T(1,128)}, f32[1,512]{1,0:T(1,128)S(1)}, u32[]{:S(2)}) copy-start(f32[1,512]{1,0:T(1,128)S(1)} %get-tuple-element.81) | copy-start | bytes 6148
  18.0 29.1 %copy-start.82 = (f32[8,256]{1,0:T(8,128)}, f32[8,256]{1,0:T(8,128)S(1)}, u32[]{:S(2)}) copy-start(f32[8,256]{1,0:T(8,128)S(1)} %get-tuple-element.27) | copy-start | bytes 24580
  18.0 29.1 %copy-start.86 = (f32[8,256]{1,0:T(8,128)}, f32[8,256]{1,0:T(8,128)S(1)}, u32[]{:S(2)}) copy-start(f32[8,256]{1,0:T(8,128)S(1)} %get-tuple-element.26) | copy-start | bytes 24580
  54.0 737.3 %copy-start.6 = (f32[8,4,64,256]{3,2,1,0:T(8,128)}, f32[8,4,64,256]{3,2,1,0:T(8,128)S(1)}, u32[]{:S(2)}) copy-start(f32[8,4,64,256]{3,2,1,0:T(8,128)S(1)} %get-tuple-element.89) | copy-start | bytes 6291460
  54.0 737.3 %copy-start.60 = (f32[8,4,64]{2,1,0:T(4,128)}, f32[8,4,64]{2,1,0:T(4,128)S(1)}, u32[]{:S(2)}) copy-start(f32[8,4,64]{2,1,0:T(4,128)S(1)} %broadcast_multiply_fusion.2) | copy-start | bytes 24580
  54.7 736.6 %copy-start.64 = (f32[8,4,64]{2,1,0:T(4,128)}, f32[8,4,64]{2,1,0:T(4,128)S(1)}, u32[]{:S(2)}) copy-start(f32[8,4,64]{2,1,0:T(4,128)S(1)} %fusion.144) | copy-start | bytes 24580
  56.0 188.6 %copy-start.21 = (bf16[8,4,64,256]{3,2,1,0:T(8,128)(2,1)}, bf16[8,4,64,256]{3,2,1,0:T(8,128)(2,1)S(1)}, u32[]{:S(2)}) copy-start(bf16[8,4,64,256]{3,2,1,0:T(8,128)(2,1)S(1)} %fusion.58) | copy-start | bytes 3145732
  78.5 563.4 %all-reduce.13.cloned.1.call-start = ((), (), s32[]{:S(2)}) async-start(), calls=%async_computation.2 | async-start | bytes 25165824 | tf_op jit(solution)/shard_map/psum | solution.py:159
  244.6 1939.3 %all-reduce.11.cloned.1.call-start = ((), (), s32[]{:S(2)}) async-start(), calls=%async_computation.1 | async-start | bytes 11796480 | tf_op jit(solution)/shard_map/psum | solution.py:355
  833.4 18.7 copy-start.19
  851.9 18.2 slice-start
  852.1 18.1 slice-start.1
  852.1 18.1 slice-start.2
  852.1 18.1 slice-start.3
  870.2 16.3 copy-start.5
  895.1 45.8 %slice-start.4 = ((s8[8388608]{0:T(1024)(128)(4,1)}), s8[4194304]{0:T(1024)(128)(4,1)S(1)}, s32[]{:S(2)}) async-start(s8[8388608]{0:T(1024)(128)(4,1)} %bitcast.505), calls=%async_computation.7 | async-start | bytes 8388608
  898.2 42.7 %slice-start.5 = ((s8[8388608]{0:T(1024)(128)(4,1)}), s8[4194304]{0:T(1024)(128)(4,1)S(1)}, s32[]{:S(2)}) async-start(s8[8388608]{0:T(1024)(128)(4,1)} %bitcast.505), calls=%async_computation.8 | async-start | bytes 8388608
  898.2 42.7 %copy-start.9 = (bf16[8,4,64,8,32]{4,1,3,2,0:T(4,128)(2,1)S(1)}, bf16[8,4,64,8,32]{4,1,3,2,0:T(4,128)(2,1)}, u32[]{:S(2)}) copy-start(bf16[8,4,64,8,32]{4,1,3,2,0:T(4,128)(2,1)} %copy.369) | copy-start | bytes 3145732
  1889.8 23.0 %copy-start.1 = (f32[8,64,8,4,10]{4,3,2,1,0:T(4,128)}, f32[8,64,8,4,10]{4,3,2,1,0:T(4,128)S(1)}, u32[]{:S(2)}) copy-start(f32[8,64,8,4,10]{4,3,2,1,0:T(4,128)S(1)} %fusion.183) | copy-start | bytes 1966084
  1889.8 23.0 %copy-start.11 = (bf16[8,4,64,8,32]{4,0,1,3,2:T(8,128)(2,1)S(1)}, bf16[8,4,64,8,32]{4,0,1,3,2:T(8,128)(2,1)}, u32[]{:S(2)}) copy-start(bf16[8,4,64,8,32]{4,0,1,3,2:T(8,128)(2,1)} %copy.358) | copy-start | bytes 3145732
  (101 other events, 358.6 us)
Sparse Core Ops, SparseCore 0:
  78.6 101.7 all-reduce.8
  244.7 397.1 all-reduce.12
  2028.6 155.1 all-reduce.10
where the time goes:
time: 2210 us; the launch traced here: 2200 us
  blocking collectives  844 us (38%)
  waiting for transfers between devices  573 us (26%)
  matrix products  388 us (18%)
  local copies, waits for them, and re-layouts  285 us (13%)
  other arithmetic  91.7 us (4%)
    psum x1, blocking collectives, on_device(): key_sum, value_sum = lax.psum((key_part, value_part), 'var')  803 us
    psum x1, waiting for transfers between devices, on_device(): total, summed = lax.psum((part_total, part_summed), 'var')  383 us
    reshape x8, local copies, waits for them, and re-layouts, split_heads(): values.reshape(values.shape[:-1] + (HEADS, values.shape[-1] // HEADS))  115 us
    psum x1, waiting for transfers between devices, on_device(): lax.psum((grad_inner, grad_outer, grad_bias, grad_up, grad_up_bias, grad_...  102 us
    pmax x1, waiting for transfers between devices, on_device(): top = lax.pmax(local_top, 'var')  88 us
  transfers between devices with their start and end apart: 3, of which 3 were waited for; matrix products, arithmetic and copies ran while one was open for 2% of the time, Pallas kernels for 0%

commit v1 on v0

v1 whole, which is shorter than its diff:
```python
import functools

import jax
import jax.numpy as jnp
import numpy as np
from jax import lax
from jax.experimental import pallas as pl
from jax.experimental.pallas import tpu as pltpu
from jax.sharding import PartitionSpec as P

HEADS = 8
SLOTS = 16
EPS = 1e-05
MASKED = -1e30
MESH = pl.DeviceIdType.MESH
F32 = jnp.float32
LOW = jnp.bfloat16
VMEM_LIMIT = 56 * 1024 * 1024


def mm(a, b):
    return jnp.dot(a, b, preferred_element_type=F32)


def mm_nt(a, b):
    return lax.dot_general(a, b, (((1,), (1,)), ((), ())), preferred_element_type=F32)


def mm_tn(a, b):
    return lax.dot_general(a, b, (((0,), (0,)), ((), ())), preferred_element_type=F32)


def ln_stats(a):
    mean = jnp.mean(a, axis=1, keepdims=True)
    center = a - mean
    var = jnp.mean(center * center, axis=1, keepdims=True)
    rstd = lax.rsqrt(var + EPS)
    return center * rstd, rstd


def ln_back(g, xhat, rstd, gain):
    gy = g * gain
    first = jnp.mean(gy, axis=1, keepdims=True)
    second = jnp.mean(gy * xhat, axis=1, keepdims=True)
    return rstd * (gy - first - xhat * second)


def gelu_both(z):
    k0 = np.float32(np.sqrt(2.0 / np.pi))
    k1 = np.float32(0.044715)
    square = z * z
    t = jnp.tanh(k0 * z * (1.0 + k1 * square))
    half = 0.5 * (1.0 + t)
    slope = half + 0.5 * z * (1.0 - t * t) * (k0 * (1.0 + 3.0 * k1 * square))
    return z * half, slope


def col_sum(x):
    return jnp.sum(x.astype(F32), axis=0, keepdims=True)


def spread_heads(x, heads_ref):
    return jnp.concatenate([x * heads_ref[h : h + 1, :] for h in range(HEADS)], axis=0)


def gather_heads(x, headsf_ref, rows):
    total = x[:rows] * headsf_ref[0:1, :]
    for h in range(1, HEADS):
        total = total + x[h * rows : (h + 1) * rows] * headsf_ref[h : h + 1, :]
    return total


def first_kernel(
    segs, lvars,
    tok_ref, cot_ref, off_ref, fac_ref, wi_ref, wo_ref, ab_ref, win_ref, bin_ref, wout_ref, bout_ref,
    gain_ref, shift_ref, heads_ref, headsf_ref, perm_ref,
    t2_ref, cots_ref, q_ref, k_ref, v_ref, p_ref, tc_ref, x1_ref, r1_ref, f1_ref, s1_ref, x2_ref, r2_ref,
):
    rows = lvars * segs
    width = tok_ref.shape[-1]
    scale = np.float32((width // HEADS) ** (-0.5))
    cots_ref[0] = mm(perm_ref[...], cot_ref[0].reshape(rows, width)).astype(LOW)
    tok = tok_ref[0].reshape(rows, width).astype(F32)
    start = (tok - off_ref[0]) * fac_ref[0]
    low = start.astype(LOW)
    q_ref[0] = (mm(low, wi_ref[0, 0]) + ab_ref[0, 0:1, :]).astype(LOW)
    k_ref[0] = mm(low, wi_ref[0, 1]).astype(LOW)
    v_ref[0] = (mm(low, wi_ref[0, 2]) + ab_ref[0, 1:2, :]).astype(LOW)
    for v in range(lvars):
        part = slice(v * segs, (v + 1) * segs)
        spread = spread_heads(q_ref[0, part, :], heads_ref)
        scores = mm_nt(k_ref[0, part, :], spread)
        top = jnp.max(scores, axis=0, keepdims=True)
        expo = jnp.exp((scores - top) * scale)
        prob = (expo / jnp.sum(expo, axis=0, keepdims=True)).astype(LOW)
        p_ref[0, part, :] = prob
        tc_ref[0, part, :] = gather_heads(mm_tn(prob, v_ref[0, part, :]), headsf_ref, segs).astype(LOW)
    a1 = start + mm(tc_ref[0], wo_ref[0]) + ab_ref[0, 2:3, :]
    x1, r1 = ln_stats(a1)
    x1_ref[0] = x1.astype(LOW)
    r1_ref[0] = jnp.broadcast_to(r1, (rows, 128))
    t1 = x1 * gain_ref[0:1, :] + shift_ref[0:1, :]
    act, slope = gelu_both(mm(t1.astype(LOW), win_ref[0]) + bin_ref[0:1, :])
    f1_ref[0] = act.astype(LOW)
    s1_ref[0] = slope.astype(LOW)
    a2 = t1 + mm(f1_ref[0], wout_ref[0]) + bout_ref[0:1, :]
    x2, r2 = ln_stats(a2)
    x2_ref[0] = x2.astype(LOW)
    r2_ref[0] = jnp.broadcast_to(r2, (rows, 128))
    t2 = (x2 * gain_ref[1:2, :] + shift_ref[1:2, :]).astype(LOW)
    t2_ref[0] = mm(perm_ref[...], t2).astype(LOW)


B_SQ, B_SK, B_SV, B_RQ, B_RK, B_RV, B_O1, B_O2, B_IN, B_OUT, B_SMALL = [256 * i for i in (0, 1, 2, 3, 4, 5, 6, 7, 8, 10, 12)]
B_ROWS = B_SMALL + 16
C_Q, C_K, C_V, C_O, C_IN, C_OUT, C_SMALL = [256 * i for i in (0, 1, 2, 3, 4, 6, 8)]
C_ROWS = C_SMALL + 16


def second_kernel(
    lsegs, nvars, routers, steps,
    t2_ref, cot_ref, lim_ref, router_ref, wi1_ref, wi2_ref, wo_ref, ab_ref, win_ref, bin_ref, wout_ref, bout_ref,
    gain_ref, shift_ref, mask_ref, grow_ref, shrink_ref, sumr_ref, perm_ref, back_ref,
    out_ref, g_ref, grads_ref, groute_ref,
    qx_ref, kq_ref,
):
    step = pl.program_id(0)
    rows, width = t2_ref.shape[1:]
    lanes = SLOTS * HEADS
    scale = np.float32((width // HEADS) ** (-0.5))

    def expand(x):
        return (mm(grow_ref[...], x).astype(LOW).reshape(-1, 16, width) * mask_ref[...][None]).reshape(-1, width)

    def contract(x):
        return mm(shrink_ref[...], (x.astype(LOW).reshape(-1, 16, width) * mask_ref[...][None]).reshape(-1, width))

    @pl.when(step == 0)
    def _():
        grads_ref[...] = jnp.zeros_like(grads_ref)
        kq_ref[...] = jnp.zeros_like(kq_ref)
        sq = (mm(router_ref[...], wi1_ref[0, 0]) + ab_ref[1, 0:1, :]).astype(LOW)
        qx_ref[...] = expand(sq)

    def per_segment(f):
        return [f(slice(s * nvars, (s + 1) * nvars), slice(s * lanes, (s + 1) * lanes)) for s in range(lsegs)]

    t2 = mm(perm_ref[...], t2_ref[0]).astype(LOW)
    sk = mm(t2, wi1_ref[0, 1]).astype(LOW)
    sv = (mm(t2, wi1_ref[0, 2]) + ab_ref[1, 1:2, :]).astype(LOW)
    rq = (mm(t2, wi2_ref[0, 0]) + ab_ref[2, 0:1, :]).astype(LOW)
    valid = lax.broadcasted_iota(jnp.int32, (nvars, lanes), 0).astype(F32) < lim_ref[0]

    def send_prob(n, l):
        scores = jnp.where(valid, mm_nt(sk[n], qx_ref[l, :]), MASKED)
        top = jnp.max(scores, axis=0, keepdims=True)
        expo = jnp.where(valid, jnp.exp((scores - top) * scale), 0.0)
        return expo / jnp.sum(expo, axis=0, keepdims=True)

    sp = per_segment(send_prob)
    sp_low = [x.astype(LOW) for x in sp]
    pre = contract(jnp.concatenate([mm_tn(sp_low[s], sv[s * nvars : (s + 1) * nvars]) for s in range(lsegs)], axis=0))
    pre_low = pre.astype(LOW)
    buffer = (mm(pre_low, wo_ref[1]) + ab_ref[1, 2:3, :]).astype(LOW)
    rkx = expand(mm(buffer, wi2_ref[0, 1]).astype(LOW))
    rvx = expand((mm(buffer, wi2_ref[0, 2]) + ab_ref[2, 1:2, :]).astype(LOW))
    scores = jnp.concatenate(per_segment(lambda n, l: mm_nt(rq[n], rkx[l])), axis=0)
    real = lax.broadcasted_iota(jnp.int32, (rows, lanes), 1) < routers * HEADS
    scores = jnp.where(real, scores, MASKED)
    top = scores
    shift = lanes // 2
    while shift >= HEADS:
        top = jnp.maximum(top, pltpu.roll(top, shift, 1))
        shift //= 2
    expo = jnp.where(real, jnp.exp((scores - top) * scale), 0.0)
    rp = expo / mm(expo.astype(LOW), sumr_ref[...])
    rp_low = rp.astype(LOW)
    rc = jnp.concatenate(per_segment(lambda n, l: mm(rp_low[n], rvx[l])), axis=0).astype(LOW)
    a3 = t2.astype(F32) + mm(rc, wo_ref[2]) + ab_ref[2, 2:3, :]
    x3, r3 = ln_stats(a3)
    t3 = x3 * gain_ref[2:3, :] + shift_ref[2:3, :]
    t3_low = t3.astype(LOW)
    act, slope = gelu_both(mm(t3_low, win_ref[0]) + bin_ref[1:2, :])
    f2 = act.astype(LOW)
    a4 = t3 + mm(f2, wout_ref[0]) + bout_ref[1:2, :]
    x4, r4 = ln_stats(a4)
    out = (x4 * gain_ref[3:4, :] + shift_ref[3:4, :]).astype(LOW)
    out_ref[0] = mm(back_ref[...], out).astype(LOW)

    def add(row, value):
        grads_ref[row : row + value.shape[0], :] += value

    small = {}
    cot = mm(perm_ref[...], cot_ref[0])
    small[10] = col_sum(cot * x4)
    small[12] = col_sum(cot)
    g4 = ln_back(cot, x4, r4, gain_ref[3:4, :])
    e4 = g4.astype(LOW)
    add(B_OUT, mm_tn(f2, e4))
    small[8] = col_sum(e4)
    e3 = (slope * mm_nt(e4, wout_ref[0])).astype(LOW)
    add(B_IN, mm_tn(t3_low, e3[:, :width]))
    add(B_IN + width, mm_tn(t3_low, e3[:, width:]))
    e3_sum = col_sum(e3)
    small[6] = e3_sum[:, :width]
    small[7] = e3_sum[:, width:]
    g3 = g4 + mm_nt(e3, win_ref[0])
    small[9] = col_sum(g3 * x3)
    small[11] = col_sum(g3)
    g3 = ln_back(g3, x3, r3, gain_ref[2:3, :])
    eo = g3.astype(LOW)
    add(B_O2, mm_tn(rc, eo))
    small[5] = col_sum(eo)
    ec = mm_nt(eo, wo_ref[2]).astype(LOW)
    dp = jnp.concatenate(per_segment(lambda n, l: mm_nt(ec[n], rvx[l])), axis=0)
    ds = (scale * rp * (dp - mm((rp * dp).astype(LOW), sumr_ref[...]))).astype(LOW)
    erq = jnp.concatenate(per_segment(lambda n, l: mm(ds[n], rkx[l])), axis=0).astype(LOW)
    erk = contract(jnp.concatenate(per_segment(lambda n, l: mm_tn(ds[n], rq[n])), axis=0)).astype(LOW)
    erv = contract(jnp.concatenate(per_segment(lambda n, l: mm_tn(rp_low[n], ec[n])), axis=0)).astype(LOW)
    add(B_RQ, mm_tn(t2, erq))
    small[3] = col_sum(erq)
    add(B_RK, mm_tn(buffer, erk))
    add(B_RV, mm_tn(buffer, erv))
    small[4] = col_sum(erv)
    eb = (mm_nt(erk, wi2_ref[0, 1]) + mm_nt(erv, wi2_ref[0, 2])).astype(LOW)
    add(B_O1, mm_tn(pre_low, eb))
    small[2] = col_sum(eb)
    epx = expand(mm_nt(eb, wo_ref[1]).astype(LOW))
    dss = []
    for s in range(lsegs):
        dps = mm_nt(sv[s * nvars : (s + 1) * nvars], epx[s * lanes : (s + 1) * lanes])
        weighted = sp[s] * dps
        center = jnp.sum(weighted, axis=0, keepdims=True)
        dss.append((scale * (weighted - sp[s] * center)).astype(LOW))
    esv = jnp.concatenate([mm(sp_low[s], epx[s * lanes : (s + 1) * lanes]) for s in range(lsegs)], axis=0).astype(LOW)
    esk = jnp.concatenate([mm(dss[s], qx_ref[s * lanes : (s + 1) * lanes, :]) for s in range(lsegs)], axis=0).astype(LOW)
    for s in range(lsegs):
        kq_ref[s * lanes : (s + 1) * lanes, :] += mm_tn(dss[s], sk[s * nvars : (s + 1) * nvars])
    add(B_SK, mm_tn(t2, esk))
    add(B_SV, mm_tn(t2, esv))
    small[1] = col_sum(esv)
    g2 = g3 + mm_nt(erq, wi2_ref[0, 0]) + mm_nt(esk, wi1_ref[0, 1]) + mm_nt(esv, wi1_ref[0, 2])
    g_ref[0] = mm(back_ref[...], g2.astype(LOW)).astype(LOW)
    for row in range(1, 13):
        add(B_SMALL + row, small[row])

    @pl.when(step == steps - 1)
    def _():
        kq = contract(kq_ref[...])
        kq_low = kq.astype(LOW)
        grads_ref[B_SQ : B_SQ + width, :] = mm_tn(router_ref[...], kq_low)
        grads_ref[B_SMALL : B_SMALL + 1, :] = col_sum(kq)
        groute_ref[...] = mm_nt(kq_low, wi1_ref[0, 0])


def third_kernel(
    segs, lvars,
    out_ref, g_ref, tok_ref, off_ref, fac_ref, wi_ref, wo_ref, win_ref, wout_ref, gain_ref, shift_ref,
    heads_ref, headsf_ref, perm_ref,
    q_ref, k_ref, v_ref, p_ref, tc_ref, x1_ref, r1_ref, f1_ref, s1_ref, x2_ref, r2_ref,
    full_ref, gin_ref, grads_ref,
    gq_ref, gk_ref, gv_ref,
):
    step = pl.program_id(0)
    rows, width = g_ref.shape[1:]
    scale = np.float32((width // HEADS) ** (-0.5))

    @pl.when(step == 0)
    def _():
        grads_ref[...] = jnp.zeros_like(grads_ref)

    def add(row, value):
        grads_ref[row : row + value.shape[0], :] += value

    def wide(ref):
        return jnp.concatenate([ref[0]] * (width // 128), axis=1)

    full_ref[0] = mm(perm_ref[...], out_ref[0]).reshape(lvars, segs, width)
    g2 = mm(perm_ref[...], g_ref[0])
    x2 = x2_ref[0].astype(F32)
    add(C_SMALL + 7, col_sum(g2 * x2))
    add(C_SMALL + 9, col_sum(g2))
    g2 = ln_back(g2, x2, wide(r2_ref), gain_ref[1:2, :])
    e2 = g2.astype(LOW)
    add(C_OUT, mm_tn(f1_ref[0], e2))
    add(C_SMALL + 5, col_sum(e2))
    e1 = (s1_ref[0].astype(F32) * mm_nt(e2, wout_ref[0])).astype(LOW)
    x1 = x1_ref[0].astype(F32)
    t1 = (x1 * gain_ref[0:1, :] + shift_ref[0:1, :]).astype(LOW)
    add(C_IN, mm_tn(t1, e1[:, :width]))
    add(C_IN + width, mm_tn(t1, e1[:, width:]))
    e1_sum = col_sum(e1)
    add(C_SMALL + 3, e1_sum[:, :width])
    add(C_SMALL + 4, e1_sum[:, width:])
    g1 = g2 + mm_nt(e1, win_ref[0])
    add(C_SMALL + 6, col_sum(g1 * x1))
    add(C_SMALL + 8, col_sum(g1))
    g1 = ln_back(g1, x1, wide(r1_ref), gain_ref[0:1, :])
    et = g1.astype(LOW)
    add(C_O, mm_tn(tc_ref[0], et))
    add(C_SMALL + 2, col_sum(et))
    etc = mm_nt(et, wo_ref[0]).astype(LOW)
    for v in range(lvars):
        part = slice(v * segs, (v + 1) * segs)
        ex = spread_heads(etc[part], heads_ref)
        prob_low = p_ref[0, part, :]
        prob = prob_low.astype(F32)
        weighted = prob * mm_nt(v_ref[0, part, :], ex)
        ets = (weighted - prob * jnp.sum(weighted, axis=0, keepdims=True)).astype(LOW)
        gv_ref[part, :] = mm(prob_low, ex).astype(LOW)
        gk_ref[part, :] = (scale * mm(ets, spread_heads(q_ref[0, part, :], heads_ref))).astype(LOW)
        gq_ref[part, :] = (scale * gather_heads(mm_tn(ets, k_ref[0, part, :]), headsf_ref, segs)).astype(LOW)
    factor = fac_ref[0]
    low = ((tok_ref[0].reshape(rows, width).astype(F32) - off_ref[0]) * factor).astype(LOW)
    gq = gq_ref[...]
    gk = gk_ref[...]
    gv = gv_ref[...]
    add(C_Q, mm_tn(low, gq))
    add(C_K, mm_tn(low, gk))
    add(C_V, mm_tn(low, gv))
    add(C_SMALL, col_sum(gq))
    add(C_SMALL + 1, col_sum(gv))
    gs = g1 + mm_nt(gq, wi_ref[0, 0]) + mm_nt(gk, wi_ref[0, 1]) + mm_nt(gv, wi_ref[0, 2])
    gin_ref[0] = (gs * factor).reshape(lvars, segs, width)


def reduce_kernel(axes, x_ref, o_ref, acc_ref, send_ref, *scratch):
    recv_refs, sems = scratch[:-4], scratch[-4:]
    scatter_send, scatter_recv, gather_send, gather_recv = sems
    position = {name: index for name, (index, _, _) in axes.items()}
    members = {name: count for name, (_, count, _) in axes.items()}
    total = x_ref.shape[0]
    half = total // 2
    barrier = pltpu.get_barrier_semaphore()
    greeted = 0
    for name, (index, count, target) in axes.items():
        for k in range(1, count):
            pl.semaphore_signal(barrier, inc=1, device_id=target(lax.rem(index + k, count)), device_id_type=MESH)
            greeted += 1
    pl.semaphore_wait(barrier, greeted)
    acc_ref[...] = x_ref[...]
    names = [name for name in axes if members[name] > 1]
    orders = [names, names[:1] + [names[2], names[1]] + names[3:]] if len(names) == 4 else [names, names]
    starts = [jnp.int32(0), jnp.int32(half)]
    sizes = [half, half]
    slot = 0
    plan = [[], []]
    counter = 0
    for level in range(len(names)):
        waits = [[], []]
        for part in range(2):
            name = orders[part][level]
            index, count, target = axes[name]
            size = sizes[part] // count
            recv = recv_refs[part * len(names) + level]
            for k in range(1, count):
                peer = lax.rem(index + k, count)
                begin = pl.multiple_of(starts[part] + peer * size, 16)
                send_ref[pl.ds(begin, size), :] = acc_ref[pl.ds(begin, size), :].astype(LOW)
                copy = pltpu.make_async_remote_copy(
                    src_ref=send_ref.at[pl.ds(begin, size), :],
                    dst_ref=recv.at[k - 1],
                    send_sem=scatter_send.at[counter],
                    recv_sem=scatter_recv.at[counter],
                    device_id=target(peer),
                    device_id_type=MESH,
                )
                copy.start()
                waits[part].append(copy)
                counter += 1
        for part in range(2):
            name = orders[part][level]
            index, count, target = axes[name]
            size = sizes[part] // count
            recv = recv_refs[part * len(names) + level]
            mine = pl.multiple_of(starts[part] + index * size, 16)
            for copy in waits[part]:
                copy.wait()
            value = acc_ref[pl.ds(mine, size), :]
            for k in range(1, count):
                value = value + recv[k - 1].astype(F32)
            acc_ref[pl.ds(mine, size), :] = value
            plan[part].append((name, starts[part], size))
            starts[part] = mine
            sizes[part] = size
    for part in range(2):
        own = pl.ds(pl.multiple_of(starts[part], 16), sizes[part])
        o_ref[own, :] = acc_ref[own, :].astype(LOW)
    counter = 0
    for level in reversed(range(len(names))):
        copies = []
        for part in range(2):
            name, base, size = plan[part][level]
            index, count, target = axes[name]
            own = pl.ds(pl.multiple_of(base + index * size, 16), size)
            for k in range(1, count):
                copy = pltpu.make_async_remote_copy(
                    src_ref=o_ref.at[own, :],
                    dst_ref=o_ref.at[own, :],
                    send_sem=gather_send.at[counter],
                    recv_sem=gather_recv.at[counter],
                    device_id=target(lax.rem(index + k, count)),
                    device_id_type=MESH,
                )
                copy.start()
                copies.append(copy)
                counter += 1
        for copy in copies:
            copy.wait()


def all_reduce(x, var_size, seg_size, collective_id):
    cores = 2 if seg_size % 2 == 0 else 1
    xs = seg_size // cores
    ys = xs if var_size % xs == 0 else 1
    zs = var_size // ys
    devices = var_size * seg_size
    rows, width = x.shape
    quantum = 2 * 16 * devices
    padded = -(-rows // quantum) * quantum
    x = jnp.pad(x, ((0, padded - rows), (0, 0)))
    counts = {"core": cores, "x": xs, "y": ys, "z": zs}

    def kernel(*refs):
        var = lax.axis_index("var")
        seg = lax.axis_index("seg")
        core, xi = lax.rem(seg, cores), lax.div(seg, cores)
        yi, zi = lax.rem(var, ys), lax.div(var, ys)
        axes = {
            "core": (core, cores, lambda i: {"seg": xi * cores + i}),
            "x": (xi, xs, lambda i: {"seg": i * cores + core}),
            "y": (yi, ys, lambda i: {"var": zi * ys + i}),
            "z": (zi, zs, lambda i: {"var": i * ys + yi}),
        }
        reduce_kernel(axes, *refs)

    names = [name for name in counts if counts[name] > 1]
    orders = [names, names[:1] + [names[2], names[1]] + names[3:]] if len(names) == 4 else [names, names]
    recv = []
    for part in range(2):
        size = padded // 2
        for name in orders[part]:
            size //= counts[name]
            recv.append(pltpu.VMEM((counts[name] - 1, size, width), LOW))
    copies = 2 * sum(counts[name] - 1 for name in names)
    out = pl.pallas_call(
        kernel,
        out_shape=jax.ShapeDtypeStruct((padded, width), LOW),
        in_specs=[pl.BlockSpec(memory_space=pltpu.VMEM)],
        out_specs=pl.BlockSpec(memory_space=pltpu.VMEM),
        scratch_shapes=[pltpu.VMEM((padded, width), F32), pltpu.VMEM((padded, width), LOW)]
        + recv
        + [pltpu.SemaphoreType.DMA((copies,))] * 4,
        compiler_params=pltpu.CompilerParams(
            collective_id=collective_id, has_side_effects=True, vmem_limit_bytes=VMEM_LIMIT
        ),
        name="reduce",
    )(x)
    return out[:rows]


def fixed(shape, index=None):
    index = (0,) * len(shape) if index is None else index
    return pl.BlockSpec(shape, lambda b: index)


def stepped(shape):
    return pl.BlockSpec((1,) + shape, lambda b: (b,) + (0,) * len(shape))


def on_device(
    var_size, seg_size,
    tokens, domain, counts, domain_mean, domain_scale, attn_inner, attn_outer, attn_bias,
    mlp_in, mlp_in_bias, mlp_out, mlp_out_bias, norm_gain, norm_bias, router, cotangent,
):
    batch, lvars, segs, width = tokens.shape
    routers = router.shape[1]
    hidden = mlp_in.shape[2]
    lsegs = segs // var_size
    nvars = lvars * var_size
    rows = lvars * segs
    lanes = SLOTS * HEADS
    domains = counts.shape[0]
    me = lax.axis_index("var")

    picks = domain[:, None] == jnp.arange(domains, dtype=jnp.int32)[None, :]
    offset = jnp.sum(jnp.where(picks[:, :, None], domain_mean[None], 0.0), axis=1)[:, None, :]
    factor = jnp.sum(jnp.where(picks[:, :, None], domain_scale[None], 0.0), axis=1)[:, None, :]
    limit = jnp.sum(jnp.where(picks, counts[None, :], 0), axis=1).astype(F32)
    limit = jnp.broadcast_to(limit[:, None, None], (batch, 1, lanes))

    heads = (np.arange(width)[None, :] // (width // HEADS) == np.arange(HEADS)[:, None]).astype(np.float32)
    heads_low = jnp.asarray(heads, LOW)
    heads_f = jnp.asarray(heads, F32)
    mask = jnp.asarray(np.concatenate([heads, heads], axis=0), LOW)
    order = np.arange(rows).reshape(lvars, var_size, lsegs).transpose(1, 0, 2).reshape(-1)
    split = np.eye(rows, dtype=np.float32)[order]
    order = np.arange(rows).reshape(nvars, lsegs).transpose(1, 0).reshape(-1)
    swap = np.eye(rows, dtype=np.float32)[order]
    group = np.arange(lsegs * lanes) // HEADS
    grow = (group[:, None] == np.arange(lsegs * SLOTS)[None, :]).astype(np.float32)
    sumr = (np.arange(lanes)[:, None] % HEADS == np.arange(lanes)[None, :] % HEADS).astype(np.float32)

    params = pltpu.CompilerParams(dimension_semantics=("arbitrary",), vmem_limit_bytes=VMEM_LIMIT)
    kept = [
        ((rows, width), LOW), ((rows, width), LOW), ((rows, width), LOW), ((rows, HEADS * segs), LOW),
        ((rows, width), LOW), ((rows, width), LOW), ((rows, 128), F32), ((rows, hidden), LOW),
        ((rows, hidden), LOW), ((rows, width), LOW), ((rows, 128), F32),
    ]
    whole = lambda x: fixed(x.shape)
    series = stepped((lvars, segs, width))
    plane = stepped((rows, width))
    inner0 = fixed((1,) + attn_inner.shape[1:])
    outer0 = fixed((1,) + attn_outer.shape[1:])
    up0 = fixed((1,) + mlp_in.shape[1:])
    down0 = fixed((1,) + mlp_out.shape[1:])
    row_spec = stepped((1, width))
    split_low = jnp.asarray(split, LOW)
    t2, cot, *residuals = pl.pallas_call(
        functools.partial(first_kernel, segs, lvars),
        grid=(batch,),
        in_specs=[
            series, series, row_spec, row_spec, inner0, outer0, whole(attn_bias), up0, whole(mlp_in_bias), down0,
            whole(mlp_out_bias), whole(norm_gain), whole(norm_bias), whole(heads_low), whole(heads_f), whole(split_low),
        ],
        out_specs=[plane, plane] + [stepped(shape) for shape, _ in kept],
        out_shape=[jax.ShapeDtypeStruct((batch, rows, width), LOW)] * 2
        + [jax.ShapeDtypeStruct((batch,) + shape, dtype) for shape, dtype in kept],
        compiler_params=params,
        name="time_forward",
    )(
        tokens, cotangent, offset, factor, attn_inner, attn_outer, attn_bias, mlp_in, mlp_in_bias, mlp_out,
        mlp_out_bias, norm_gain, norm_bias, heads_low, heads_f, split_low,
    )

    def exchange(x):
        parts = x.reshape(batch, var_size, rows // var_size, width)
        return lax.all_to_all(parts, "var", 1, 1, tiled=True).reshape(batch, rows, width)

    t2 = exchange(t2)
    cot = exchange(cot)
    mine = lax.dynamic_slice_in_dim(router, me * lsegs, lsegs, 0)
    mine = jnp.pad(mine, ((0, 0), (0, SLOTS - routers), (0, 0))).reshape(lsegs * SLOTS, width)
    inner1 = fixed((1,) + attn_inner.shape[1:], (1, 0, 0, 0))
    inner2 = fixed((1,) + attn_inner.shape[1:], (2, 0, 0, 0))
    up1 = fixed((1,) + mlp_in.shape[1:], (1, 0, 0))
    down1 = fixed((1,) + mlp_out.shape[1:], (1, 0, 0))
    consts = [mask, jnp.asarray(grow, LOW), jnp.asarray(grow.T, LOW), jnp.asarray(sumr, LOW), jnp.asarray(swap, LOW), jnp.asarray(swap.T, LOW)]
    out, g2, grads_b, groute = pl.pallas_call(
        functools.partial(second_kernel, lsegs, nvars, routers, batch),
        grid=(batch,),
        in_specs=[
            plane, plane, stepped((1, lanes)), whole(mine), inner1, inner2, whole(attn_outer), whole(attn_bias), up1,
            whole(mlp_in_bias), down1, whole(mlp_out_bias), whole(norm_gain), whole(norm_bias),
        ]
        + [whole(c) for c in consts],
        out_specs=[plane, plane, fixed((B_ROWS, width)), fixed((lsegs * SLOTS, width))],
        out_shape=[
            jax.ShapeDtypeStruct((batch, rows, width), LOW),
            jax.ShapeDtypeStruct((batch, rows, width), LOW),
            jax.ShapeDtypeStruct((B_ROWS, width), F32),
            jax.ShapeDtypeStruct((lsegs * SLOTS, width), F32),
        ],
        scratch_shapes=[pltpu.VMEM((lsegs * lanes, width), LOW), pltpu.VMEM((lsegs * lanes, width), F32)],
        compiler_params=params,
        name="router_part",
    )(
        t2, cot, limit, mine, attn_inner, attn_inner, attn_outer, attn_bias, mlp_in, mlp_in_bias, mlp_out,
        mlp_out_bias, norm_gain, norm_bias, *consts,
    )
    g2 = exchange(g2)
    out = exchange(out)
    join_low = jnp.asarray(split.T, LOW)
    output, input_grad, grads_c = pl.pallas_call(
        functools.partial(third_kernel, segs, lvars),
        grid=(batch,),
        in_specs=[
            plane, plane, series, row_spec, row_spec, inner0, outer0, up0, down0, whole(norm_gain), whole(norm_bias),
            whole(heads_low), whole(heads_f), whole(join_low),
        ]
        + [stepped(shape) for shape, _ in kept],
        out_specs=[series, series, fixed((C_ROWS, width))],
        out_shape=[
            jax.ShapeDtypeStruct(tokens.shape, F32),
            jax.ShapeDtypeStruct(tokens.shape, F32),
            jax.ShapeDtypeStruct((C_ROWS, width), F32),
        ],
        scratch_shapes=[pltpu.VMEM((rows, width), LOW)] * 3,
        compiler_params=params,
        name="time_backward",
    )(
        out, g2, tokens, offset, factor, attn_inner, attn_outer, mlp_in, mlp_out, norm_gain, norm_bias,
        heads_low, heads_f, join_low, *residuals,
    )

    groute = groute.reshape(lsegs, SLOTS, width)[:, :routers]
    routes = lax.dynamic_update_slice_in_dim(jnp.zeros(router.shape, F32), groute, me * lsegs, 0)
    routes = routes.reshape(-1, width)
    sums = all_reduce(jnp.concatenate([grads_b, grads_c, routes], axis=0), var_size, seg_size, 1).astype(F32)
    gb, gc, gr = sums[:B_ROWS], sums[B_ROWS : B_ROWS + C_ROWS], sums[B_ROWS + C_ROWS :]
    grad_inner = jnp.concatenate([gc[: 3 * width], gb[: 6 * width]], axis=0).reshape(attn_inner.shape)
    grad_outer = jnp.concatenate([gc[C_O : C_O + width], gb[B_O1 : B_O1 + 2 * width]], axis=0).reshape(attn_outer.shape)
    bs, cs = gb[B_SMALL:], gc[C_SMALL:]
    grad_bias = jnp.concatenate([cs[0:3], bs[0:6]], axis=0).reshape(attn_bias.shape)

    def up(x):
        return jnp.concatenate([x[:width], x[width : 2 * width]], axis=1)

    grad_up = jnp.stack([up(gc[C_IN:]), up(gb[B_IN:])])
    grad_up_bias = jnp.stack([cs[3:5].reshape(-1), bs[6:8].reshape(-1)])
    grad_down = jnp.stack([gc[C_OUT : C_OUT + hidden], gb[B_OUT : B_OUT + hidden]])
    grad_down_bias = jnp.stack([cs[5], bs[8]])
    grad_gain = jnp.concatenate([cs[6:8], bs[9:11]], axis=0)
    grad_shift = jnp.concatenate([cs[8:10], bs[11:13]], axis=0)
    return (
        output, input_grad, grad_inner, grad_outer, grad_bias, grad_up, grad_up_bias, grad_down, grad_down_bias,
        grad_gain, grad_shift, gr.reshape(router.shape),
    )


def solution(mesh):
    split = P("seg", "var", None, None)
    in_specs = (split, P("seg")) + (P(),) * 13 + (split,)
    out_specs = (split, split) + (P(),) * 10
    var_size, seg_size = mesh.shape["var"], mesh.shape["seg"]
    return jax.shard_map(
        functools.partial(on_device, var_size, seg_size),
        mesh=mesh, in_specs=in_specs, out_specs=out_specs, check_vma=False,
    )
```

time: 2210 us -> 326 us (0.15)
  blocking collectives: 844 us -> 0 us
  waiting for transfers between devices: 573 us -> 90.4 us
  matrix products: 388 us -> 0 us
  local copies, waits for them, and re-layouts: 285 us -> 19.6 us
  Pallas kernels: 0 us -> 173 us
  other arithmetic: 91.7 us -> 17.2 us
    psum x2 -> x0, blocking collectives: 844 us -> none  [the longest x1 803 us: on_device(): key_sum, value_sum = lax.psum((key_part, value_part), 'var')]
    psum x2 -> x0, waiting for transfers between devices: 485 us -> none  [the longest x1 383 us: on_device(): total, summed = lax.psum((part_total, part_summed), 'var')]
    dot_general x65 -> x0, matrix products: 380 us -> none  [the longest x1 42.7 us: on_device(): jnp.einsum('bvshr,bvshe->bsrhe', recv_prob, recv_grad.astype(jnp.float32)...]
    pallas_call x0 -> x4, Pallas kernels: none -> 173 us  [the longest x1 63.1 us: all_reduce(): pl.pallas_call(kernel, out_shape=jax.ShapeDtypeStruct((padded, width), LO...]
    reshape x8 -> x7, local copies, waits for them, and re-layouts: 115 us -> 8.5 us  [the longest x4 6.87 us: exchange(): parts = x.reshape(batch, var_size, rows // var_size, width)]
    all_to_all x0 -> x4, waiting for transfers between devices: none -> 90.4 us  [exchange(): lax.all_to_all(parts, 'var', 1, 1, tiled=True).reshape(batch, rows, width)]
    pmax x1 -> x0, waiting for transfers between devices: 88 us -> none  [on_device(): top = lax.pmax(local_top, 'var')]
    dot_general x3 -> x0, local copies, waits for them, and re-layouts: 70.2 us -> none  [the longest x1 23.4 us: on_device(): jnp.einsum('bsrhv,bvshe->bsrhe', weights, split_heads(send_value).astype(...]
  transfers between devices with their start and end apart: 3 -> 4, of which waited for: 3 -> 4; matrix products, arithmetic and copies ran while one was open for 2% -> 2% of each run, Pallas kernels for 0% -> 0%
where the time goes in v1:
time: 326 us; the launch traced here: 323 us
  Pallas kernels  173 us (53%)
  waiting for transfers between devices  90.4 us (28%)
  starting transfers between devices  22 us (7%)
  local copies, waits for them, and re-layouts  19.6 us (6%)
  other arithmetic  17.2 us (5%)
    all_to_all x4, waiting for transfers between devices, exchange(): lax.all_to_all(parts, 'var', 1, 1, tiled=True).reshape(batch, rows, width)  90.4 us
    pallas_call x1, Pallas kernels, all_reduce(): pl.pallas_call(kernel, out_shape=jax.ShapeDtypeStruct((padded, width), LO...  63.1 us
    pallas_call x1, Pallas kernels, on_device(): pl.pallas_call(functools.partial(second_kernel, lsegs, nvars, routers, ba...  60.5 us
    pallas_call x1, Pallas kernels, on_device(): pl.pallas_call(functools.partial(third_kernel, segs, lvars), grid=(batch,...  27.9 us
    all_to_all x4, starting transfers between devices, exchange(): lax.all_to_all(parts, 'var', 1, 1, tiled=True).reshape(batch, rows, width)  22 us
    pallas_call x1, Pallas kernels, on_device(): pl.pallas_call(functools.partial(first_kernel, segs, lvars), grid=(batch,...  21.7 us
    reshape x4, local copies, waits for them, and re-layouts, exchange(): parts = x.reshape(batch, var_size, rows // var_size, width)  6.87 us
  transfers between devices with their start and end apart: 4, of which 4 were waited for; matrix products, arithmetic and copies ran while one was open for 2% of the time, Pallas kernels for 0%

profile of v1, /device:TPU:29, one launch (start us, length us, event | category | flops | bytes accessed | tf_op | source)
XLA Modules:
  0.0 323.3 jit_solution(10373830499430322672)
XLA Ops:
  3.4 21.7 %time_forward.1 = (bf16[8,256,256]{2,1,0:T(8,128)(2,1)}, bf16[8,256,256]{2,1,0:T(8,128)(2,1)}, bf16[8,256,256]{2,1,0:T(8,128)(2,1)}, bf16[8,256,256]{2,1,0:T(8,1...) custom-call(bf16[8,4,64,256]{3,2,1,0:T(8,128)(2,1)} %tok_ref.3, ...), custom_call_target="tpu_custom_call" | custom-call | tf_op jit(solution)/shard_map/time_forward/pallas_call | solution.py:519
  25.1 2.4 copy.52
  27.5 5.6 %all-to-all-start = ((bf16[8,8,32,256]{3,2,0,1:T(8,128)(2,1)}), bf16[8,8,32,256]{3,2,0,1:T(8,128)(2,1)S(1)}, u32[]{:S(2)}, u32[]{:S(2)}) async-start(bf16[8,8,32,256]{3,2,0,1:T(8,128)(2,1)} %copy.52), calls=%async_computation | async-start | bytes 2097152 | tf_op jit(solution)/shard_map/all_to_all | solution.py:538
  33.0 1.1 copy.54
  34.1 23.0 %all-to-all-done = bf16[8,8,32,256]{3,2,0,1:T(8,128)(2,1)S(1)} async-done(((bf16[8,8,32,256]{3,2,0,1:T(8,128)(2,1)}), bf16[8,8,32,256]{3,2,0,1:T(8,128)(2,1)S(1)}, u32[]{:S(2)}, u32[]{:S(2)}) %all-to-all-start) | async-done | bytes 1048608 | tf_op jit(solution)/shard_map/all_to_all | solution.py:538
  57.1 5.4 %all-to-all-start.1 = ((bf16[8,8,32,256]{3,2,0,1:T(8,128)(2,1)}), bf16[8,8,32,256]{3,2,0,1:T(8,128)(2,1)S(1)}, u32[]{:S(2)}, u32[]{:S(2)}) async-start(bf16[8,8,32,256]{3,2,0,1:T(8,128)(2,1)} %copy.54), calls=%async_computation.1 | async-start | bytes 2097152 | tf_op jit(solution)/shard_map/all_to_all | solution.py:538
  64.4 22.3 %all-to-all-done.1 = bf16[8,8,32,256]{3,2,0,1:T(8,128)(2,1)S(1)} async-done(((bf16[8,8,32,256]{3,2,0,1:T(8,128)(2,1)}), bf16[8,8,32,256]{3,2,0,1:T(8,128)(2,1)S(1)}, u32[]{:S(2)}, u32[]{:S(2)}) %all-to-all-start.1) | async-done | bytes 1048608 | tf_op jit(solution)/shard_map/all_to_all | solution.py:538
  86.7 1.1 copy.55
  88.5 60.5 %router_part.1 = (bf16[8,256,256]{2,1,0:T(8,128)(2,1)}, bf16[8,256,256]{2,1,0:T(8,128)(2,1)}, f32[3088,256]{1,0:T(8,128)}, f32[128,256]{1,0:T(8,128)}) custom-call(bf16[8,256,256]{2,1,0:T(8,128)(2,1)} %bitcast.30, bf16[8,256,256]{2,1,0:T(8,128)(2,1)} %bitcast.31, f32[8,1,128]{2,1,0:T(1,128)} %broadcast_in_dim.71.lim_ref, bf16[128,256]{1,0:T(8,128)(2,1)} %bitcast.38, ...), custom_call_target="tpu_custom_call" | custom-call | tf_op jit(solution)/shard_map/router_part/pallas_call | solution.py:549
  148.9 2.4 copy.57
  151.3 5.6 %all-to-all-start.2 = ((bf16[8,8,32,256]{3,2,0,1:T(8,128)(2,1)}), bf16[8,8,32,256]{3,2,0,1:T(8,128)(2,1)S(1)}, u32[]{:S(2)}, u32[]{:S(2)}) async-start(bf16[8,8,32,256]{3,2,0,1:T(8,128)(2,1)} %copy.57), calls=%async_computation.2 | async-start | bytes 2097152 | tf_op jit(solution)/shard_map/all_to_all | solution.py:538
  156.9 1.1 copy.59
  158.0 23.1 %all-to-all-done.2 = bf16[8,8,32,256]{3,2,0,1:T(8,128)(2,1)S(1)} async-done(((bf16[8,8,32,256]{3,2,0,1:T(8,128)(2,1)}), bf16[8,8,32,256]{3,2,0,1:T(8,128)(2,1)S(1)}, u32[]{:S(2)}, u32[]{:S(2)}) %all-to-all-start.2) | async-done | bytes 1048608 | tf_op jit(solution)/shard_map/all_to_all | solution.py:538
  181.0 5.4 %all-to-all-start.3 = ((bf16[8,8,32,256]{3,2,0,1:T(8,128)(2,1)}), bf16[8,8,32,256]{3,2,0,1:T(8,128)(2,1)S(1)}, u32[]{:S(2)}, u32[]{:S(2)}) async-start(bf16[8,8,32,256]{3,2,0,1:T(8,128)(2,1)} %copy.59), calls=%async_computation.3 | async-start | bytes 2097152 | tf_op jit(solution)/shard_map/all_to_all | solution.py:538
  188.6 22.0 %all-to-all-done.3 = bf16[8,8,32,256]{3,2,0,1:T(8,128)(2,1)S(1)} async-done(((bf16[8,8,32,256]{3,2,0,1:T(8,128)(2,1)}), bf16[8,8,32,256]{3,2,0,1:T(8,128)(2,1)S(1)}, u32[]{:S(2)}, u32[]{:S(2)}) %all-to-all-start.3) | async-done | bytes 1048608 | tf_op jit(solution)/shard_map/all_to_all | solution.py:538
  210.6 1.1 copy.60
  211.7 27.9 %time_backward.1 = (f32[8,4,64,256]{3,2,1,0:T(8,128)}, f32[8,4,64,256]{3,2,1,0:T(8,128)}, f32[2064,256]{1,0:T(8,128)}) custom-call(bf16[8,256,256]{2,1,0:T(8,128)(2,1)} %bitcast.28, bf16[8,256,256]{2,1,0:T(8,128)(2,1)} %bitcast.29, bf16[8,4,64,256]{3,2,1,0:T(8,128)(2,1)} %tok_ref.3, f32[8,1,256]{2,1,0:T(1,128)} %broadcast_in_dim.66.off_ref, ...), custom_call_target="tpu_custom_call" | custom-call | tf_op jit(solution)/shard_map/time_backward/pallas_call | solution.py:574
  239.6 6.1 %select_maximum_fusion.refs_0_ = f32[6144,256]{1,0:T(8,128)} fusion(f32[640,256]{1,0:T(8,128)S(1)} %copy-done.4, f32[2064,256]{1,0:T(8,128)} %get-tuple-element.50, f32[3088,256]{1,0:T(8,128)S(1)} %copy-done.3), kind=kLoop, calls=%fused_computation | loop fusion | flops 9437184 | bytes 12222464 | tf_op jit(solution)/shard_map/concatenate | solution.py:599
  245.7 63.1 %reduce.1 = bf16[6144,256]{1,0:T(8,128)(2,1)} custom-call(f32[6144,256]{1,0:T(8,128)} %select_maximum_fusion.refs_0_), custom_call_target="tpu_custom_call" | custom-call | tf_op jit(solution)/shard_map/reduce/pallas_call | solution.py:446
  308.8 2.3 slice_convert_fusion
  312.8 1.1 fusion.2
  314.8 1.2 copy.61
  316.0 1.3 pad_maximum_fusion.8
  321.1 1.6 pad_maximum_fusion
  (68 shorter events, 14.2 us)
Async XLA Ops:
  0.6 61.9 %copy-start = (bf16[64,10,256]{2,0,1:T(8,128)(2,1)S(1)}, bf16[64,10,256]{2,0,1:T(8,128)(2,1)}, u32[]{:S(2)}) copy-start(bf16[64,10,256]{2,0,1:T(8,128)(2,1)} %param.40) | copy-start | bytes 983044
  25.1 8.0 %copy-start.5 = (bf16[8,256,256]{2,1,0:T(8,128)(2,1)S(1)}, bf16[8,256,256]{2,1,0:T(8,128)(2,1)}, u32[]{:S(2)}) copy-start(bf16[8,256,256]{2,1,0:T(8,128)(2,1)} %get-tuple-element.33) | copy-start | bytes 3145732
  27.5 35.1 %copy-start.14 = (s32[8]{0:T(128)S(1)}, s32[8]{0:T(128)}, u32[]{:S(2)}) copy-start(s32[8]{0:T(128)} %param.27) | copy-start | bytes 100
  27.5 35.2 %copy-start.15 = (s32[4]{0:T(128)S(1)}, s32[4]{0:T(128)}, u32[]{:S(2)}) copy-start(s32[4]{0:T(128)} %param.28) | copy-start | bytes 52
  27.5 29.7 %all-to-all-start = ((bf16[8,8,32,256]{3,2,0,1:T(8,128)(2,1)}), bf16[8,8,32,256]{3,2,0,1:T(8,128)(2,1)S(1)}, u32[]{:S(2)}, u32[]{:S(2)}) async-start(bf16[8,8,32,256]{3,2,0,1:T(8,128)(2,1)} %copy.52), calls=%async_computation | async-start | bytes 2097152 | tf_op jit(solution)/shard_map/all_to_all | solution.py:538
  57.1 29.6 %all-to-all-start.1 = ((bf16[8,8,32,256]{3,2,0,1:T(8,128)(2,1)}), bf16[8,8,32,256]{3,2,0,1:T(8,128)(2,1)S(1)}, u32[]{:S(2)}, u32[]{:S(2)}) async-start(bf16[8,8,32,256]{3,2,0,1:T(8,128)(2,1)} %copy.54), calls=%async_computation.1 | async-start | bytes 2097152 | tf_op jit(solution)/shard_map/all_to_all | solution.py:538
  148.9 8.0 %copy-start.6 = (bf16[8,256,256]{2,1,0:T(8,128)(2,1)S(1)}, bf16[8,256,256]{2,1,0:T(8,128)(2,1)}, u32[]{:S(2)}) copy-start(bf16[8,256,256]{2,1,0:T(8,128)(2,1)} %get-tuple-element.35) | copy-start | bytes 3145732
  151.3 35.3 %copy-start.11 = (f32[128,256]{1,0:T(8,128)S(1)}, f32[128,256]{1,0:T(8,128)}, u32[]{:S(2)}) copy-start(f32[128,256]{1,0:T(8,128)} %get-tuple-element.51) | copy-start | bytes 393220
  151.3 29.7 %all-to-all-start.2 = ((bf16[8,8,32,256]{3,2,0,1:T(8,128)(2,1)}), bf16[8,8,32,256]{3,2,0,1:T(8,128)(2,1)S(1)}, u32[]{:S(2)}, u32[]{:S(2)}) async-start(bf16[8,8,32,256]{3,2,0,1:T(8,128)(2,1)} %copy.57), calls=%async_computation.2 | async-start | bytes 2097152 | tf_op jit(solution)/shard_map/all_to_all | solution.py:538
  181.0 29.6 %all-to-all-start.3 = ((bf16[8,8,32,256]{3,2,0,1:T(8,128)(2,1)}), bf16[8,8,32,256]{3,2,0,1:T(8,128)(2,1)S(1)}, u32[]{:S(2)}, u32[]{:S(2)}) async-start(bf16[8,8,32,256]{3,2,0,1:T(8,128)(2,1)} %copy.59), calls=%async_computation.3 | async-start | bytes 2097152 | tf_op jit(solution)/shard_map/all_to_all | solution.py:538
  211.7 27.9 %copy-start.3 = (f32[3088,256]{1,0:T(8,128)S(1)}, f32[3088,256]{1,0:T(8,128)}, u32[]{:S(2)}) copy-start(f32[3088,256]{1,0:T(8,128)} %get-tuple-element.49) | copy-start | bytes 9486340
  211.7 27.9 %copy-start.4 = (f32[640,256]{1,0:T(8,128)S(1)}, f32[640,256]{1,0:T(8,128)}, u32[]{:S(2)}) copy-start(f32[640,256]{1,0:T(8,128)} %reshape.108) | copy-start | bytes 1966084
  311.1 2.9 copy-start.2
  314.8 4.2 %copy-start.7 = (f32[256,256]{1,0:T(8,128)S(1)}, f32[256,256]{1,0:T(8,128)}, u32[]{:S(2)}) copy-start(f32[256,256]{1,0:T(8,128)} %get-tuple-element.113) | copy-start | bytes 786436
  314.8 4.2 %copy-start.8 = (f32[256,256]{1,0:T(8,128)S(1)}, f32[256,256]{1,0:T(8,128)}, u32[]{:S(2)}) copy-start(f32[256,256]{1,0:T(8,128)} %get-tuple-element.114) | copy-start | bytes 786436
  314.8 4.2 %copy-start.9 = (f32[256,256]{1,0:T(8,128)S(1)}, f32[256,256]{1,0:T(8,128)}, u32[]{:S(2)}) copy-start(f32[256,256]{1,0:T(8,128)} %get-tuple-element.115) | copy-start | bytes 786436
  314.8 4.2 %copy-start.10 = (f32[256,256]{1,0:T(8,128)S(1)}, f32[256,256]{1,0:T(8,128)}, u32[]{:S(2)}) copy-start(f32[256,256]{1,0:T(8,128)} %get-tuple-element.116) | copy-start | bytes 786436
  318.4 2.8 slice-start
  318.4 2.8 slice-start.1
  320.2 2.5 copy-start.12
  320.2 2.5 copy-start.13
  320.2 3.1 copy-start.1

commit v2 on v1

--- a/solution.py
+++ b/solution.py
@@ -70,45 +70,42 @@
     return total
 
 
-def first_kernel(
-    segs, lvars,
-    tok_ref, cot_ref, off_ref, fac_ref, wi_ref, wo_ref, ab_ref, win_ref, bin_ref, wout_ref, bout_ref,
-    gain_ref, shift_ref, heads_ref, headsf_ref, perm_ref,
-    t2_ref, cots_ref, q_ref, k_ref, v_ref, p_ref, tc_ref, x1_ref, r1_ref, f1_ref, s1_ref, x2_ref, r2_ref,
+def time_forward(
+    lvars, b, tok_ref, off_ref, fac_ref, wi_ref, wo_ref, ab_ref, win_ref, bin_ref, wout_ref, bout_ref,
+    gain_ref, shift_ref, heads_ref, headsf_ref, kept,
 ):
+    q_ref, k_ref, v_ref, p_ref, tc_ref, x1_ref, r1_ref, f1_ref, s1_ref, x2_ref, r2_ref = kept
+    segs, width = tok_ref.shape[2:]
     rows = lvars * segs
-    width = tok_ref.shape[-1]
     scale = np.float32((width // HEADS) ** (-0.5))
-    cots_ref[0] = mm(perm_ref[...], cot_ref[0].reshape(rows, width)).astype(LOW)
     tok = tok_ref[0].reshape(rows, width).astype(F32)
     start = (tok - off_ref[0]) * fac_ref[0]
     low = start.astype(LOW)
-    q_ref[0] = (mm(low, wi_ref[0, 0]) + ab_ref[0, 0:1, :]).astype(LOW)
-    k_ref[0] = mm(low, wi_ref[0, 1]).astype(LOW)
-    v_ref[0] = (mm(low, wi_ref[0, 2]) + ab_ref[0, 1:2, :]).astype(LOW)
+    q_ref[b] = (mm(low, wi_ref[0, 0]) + ab_ref[0, 0:1, :]).astype(LOW)
+    k_ref[b] = mm(low, wi_ref[0, 1]).astype(LOW)
+    v_ref[b] = (mm(low, wi_ref[0, 2]) + ab_ref[0, 1:2, :]).astype(LOW)
     for v in range(lvars):
         part = slice(v * segs, (v + 1) * segs)
-        spread = spread_heads(q_ref[0, part, :], heads_ref)
-        scores = mm_nt(k_ref[0, part, :], spread)
+        spread = spread_heads(q_ref[b, part, :], heads_ref)
+        scores = mm_nt(k_ref[b, part, :], spread)
         top = jnp.max(scores, axis=0, keepdims=True)
         expo = jnp.exp((scores - top) * scale)
         prob = (expo / jnp.sum(expo, axis=0, keepdims=True)).astype(LOW)
-        p_ref[0, part, :] = prob
-        tc_ref[0, part, :] = gather_heads(mm_tn(prob, v_ref[0, part, :]), headsf_ref, segs).astype(LOW)
-    a1 = start + mm(tc_ref[0], wo_ref[0]) + ab_ref[0, 2:3, :]
+        p_ref[b, part, :] = prob
+        tc_ref[b, part, :] = gather_heads(mm_tn(prob, v_ref[b, part, :]), headsf_ref, segs).astype(LOW)
+    a1 = start + mm(tc_ref[b], wo_ref[0]) + ab_ref[0, 2:3, :]
     x1, r1 = ln_stats(a1)
-    x1_ref[0] = x1.astype(LOW)
-    r1_ref[0] = jnp.broadcast_to(r1, (rows, 128))
+    x1_ref[b] = x1.astype(LOW)
+    r1_ref[b] = jnp.broadcast_to(r1, (rows, 128))
     t1 = x1 * gain_ref[0:1, :] + shift_ref[0:1, :]
     act, slope = gelu_both(mm(t1.astype(LOW), win_ref[0]) + bin_ref[0:1, :])
-    f1_ref[0] = act.astype(LOW)
-    s1_ref[0] = slope.astype(LOW)
-    a2 = t1 + mm(f1_ref[0], wout_ref[0]) + bout_ref[0:1, :]
+    f1_ref[b] = act.astype(LOW)
+    s1_ref[b] = slope.astype(LOW)
+    a2 = t1 + mm(f1_ref[b], wout_ref[0]) + bout_ref[0:1, :]
     x2, r2 = ln_stats(a2)
-    x2_ref[0] = x2.astype(LOW)
-    r2_ref[0] = jnp.broadcast_to(r2, (rows, 128))
-    t2 = (x2 * gain_ref[1:2, :] + shift_ref[1:2, :]).astype(LOW)
-    t2_ref[0] = mm(perm_ref[...], t2).astype(LOW)
+    x2_ref[b] = x2.astype(LOW)
+    r2_ref[b] = jnp.broadcast_to(r2, (rows, 128))
+    return (x2 * gain_ref[1:2, :] + shift_ref[1:2, :]).astype(LOW)
 
 
 B_SQ, B_SK, B_SV, B_RQ, B_RK, B_RV, B_O1, B_O2, B_IN, B_OUT, B_SMALL = [256 * i for i in (0, 1, 2, 3, 4, 5, 6, 7, 8, 10, 12)]
@@ -117,15 +114,13 @@
 C_ROWS = C_SMALL + 16
 
 
-def second_kernel(
-    lsegs, nvars, routers, steps,
-    t2_ref, cot_ref, lim_ref, router_ref, wi1_ref, wi2_ref, wo_ref, ab_ref, win_ref, bin_ref, wout_ref, bout_ref,
+def router_part(
+    lsegs, nvars, routers, steps, b, arrived, leaving,
+    lim_ref, router_ref, wi1_ref, wi2_ref, wo_ref, ab_ref, win_ref, bin_ref, wout_ref, bout_ref,
     gain_ref, shift_ref, mask_ref, grow_ref, shrink_ref, sumr_ref, perm_ref, back_ref,
-    out_ref, g_ref, grads_ref, groute_ref,
-    qx_ref, kq_ref,
+    grads_ref, groute_ref, qx_ref, kq_ref,
 ):
-    step = pl.program_id(0)
-    rows, width = t2_ref.shape[1:]
+    rows, width = perm_ref.shape[0], wo_ref.shape[1]
     lanes = SLOTS * HEADS
     scale = np.float32((width // HEADS) ** (-0.5))
 
@@ -135,7 +130,7 @@
     def contract(x):
         return mm(shrink_ref[...], (x.astype(LOW).reshape(-1, 16, width) * mask_ref[...][None]).reshape(-1, width))
 
-    @pl.when(step == 0)
+    @pl.when(b == 0)
     def _():
         grads_ref[...] = jnp.zeros_like(grads_ref)
         kq_ref[...] = jnp.zeros_like(kq_ref)
@@ -145,11 +140,11 @@
     def per_segment(f):
         return [f(slice(s * nvars, (s + 1) * nvars), slice(s * lanes, (s + 1) * lanes)) for s in range(lsegs)]
 
-    t2 = mm(perm_ref[...], t2_ref[0]).astype(LOW)
+    t2 = mm(perm_ref[...], arrived(0).reshape(rows, width)).astype(LOW)
     sk = mm(t2, wi1_ref[0, 1]).astype(LOW)
     sv = (mm(t2, wi1_ref[0, 2]) + ab_ref[1, 1:2, :]).astype(LOW)
     rq = (mm(t2, wi2_ref[0, 0]) + ab_ref[2, 0:1, :]).astype(LOW)
-    valid = lax.broadcasted_iota(jnp.int32, (nvars, lanes), 0).astype(F32) < lim_ref[0]
+    valid = lax.broadcasted_iota(jnp.int32, (nvars, lanes), 0).astype(F32) < lim_ref[b]
 
     def send_prob(n, l):
         scores = jnp.where(valid, mm_nt(sk[n], qx_ref[l, :]), MASKED)
@@ -185,13 +180,13 @@
     a4 = t3 + mm(f2, wout_ref[0]) + bout_ref[1:2, :]
     x4, r4 = ln_stats(a4)
     out = (x4 * gain_ref[3:4, :] + shift_ref[3:4, :]).astype(LOW)
-    out_ref[0] = mm(back_ref[...], out).astype(LOW)
+    leaving(3, mm(back_ref[...], out).astype(LOW))
 
     def add(row, value):
         grads_ref[row : row + value.shape[0], :] += value
 
     small = {}
-    cot = mm(perm_ref[...], cot_ref[0])
+    cot = mm(perm_ref[...], arrived(1).reshape(rows, width))
     small[10] = col_sum(cot * x4)
     small[12] = col_sum(cot)
     g4 = ln_back(cot, x4, r4, gain_ref[3:4, :])
@@ -240,11 +235,11 @@
     add(B_SV, mm_tn(t2, esv))
     small[1] = col_sum(esv)
     g2 = g3 + mm_nt(erq, wi2_ref[0, 0]) + mm_nt(esk, wi1_ref[0, 1]) + mm_nt(esv, wi1_ref[0, 2])
-    g_ref[0] = mm(back_ref[...], g2.astype(LOW)).astype(LOW)
+    leaving(2, mm(back_ref[...], g2.astype(LOW)).astype(LOW))
     for row in range(1, 13):
         add(B_SMALL + row, small[row])
 
-    @pl.when(step == steps - 1)
+    @pl.when(b == steps - 1)
     def _():
         kq = contract(kq_ref[...])
         kq_low = kq.astype(LOW)
@@ -253,19 +248,16 @@
         groute_ref[...] = mm_nt(kq_low, wi1_ref[0, 0])
 
 
-def third_kernel(
-    segs, lvars,
-    out_ref, g_ref, tok_ref, off_ref, fac_ref, wi_ref, wo_ref, win_ref, wout_ref, gain_ref, shift_ref,
-    heads_ref, headsf_ref, perm_ref,
-    q_ref, k_ref, v_ref, p_ref, tc_ref, x1_ref, r1_ref, f1_ref, s1_ref, x2_ref, r2_ref,
-    full_ref, gin_ref, grads_ref,
-    gq_ref, gk_ref, gv_ref,
+def time_backward(
+    lvars, b, arrived, tok_ref, off_ref, fac_ref, wi_ref, wo_ref, win_ref, wout_ref, gain_ref, shift_ref,
+    heads_ref, headsf_ref, perm_ref, kept, gin_ref, grads_ref, gq_ref, gk_ref, gv_ref,
 ):
-    step = pl.program_id(0)
-    rows, width = g_ref.shape[1:]
+    q_ref, k_ref, v_ref, p_ref, tc_ref, x1_ref, r1_ref, f1_ref, s1_ref, x2_ref, r2_ref = kept
+    segs, width = tok_ref.shape[2:]
+    rows = lvars * segs
     scale = np.float32((width // HEADS) ** (-0.5))
 
-    @pl.when(step == 0)
+    @pl.when(b == 0)
     def _():
         grads_ref[...] = jnp.zeros_like(grads_ref)
 
@@ -273,19 +265,18 @@
         grads_ref[row : row + value.shape[0], :] += value
 
     def wide(ref):
-        return jnp.concatenate([ref[0]] * (width // 128), axis=1)
-
-    full_ref[0] = mm(perm_ref[...], out_ref[0]).reshape(lvars, segs, width)
-    g2 = mm(perm_ref[...], g_ref[0])
-    x2 = x2_ref[0].astype(F32)
+        return jnp.concatenate([ref[b]] * (width // 128), axis=1)
+
+    g2 = mm(perm_ref[...], arrived(2).reshape(rows, width))
+    x2 = x2_ref[b].astype(F32)
     add(C_SMALL + 7, col_sum(g2 * x2))
     add(C_SMALL + 9, col_sum(g2))
     g2 = ln_back(g2, x2, wide(r2_ref), gain_ref[1:2, :])
     e2 = g2.astype(LOW)
-    add(C_OUT, mm_tn(f1_ref[0], e2))
+    add(C_OUT, mm_tn(f1_ref[b], e2))
     add(C_SMALL + 5, col_sum(e2))
-    e1 = (s1_ref[0].astype(F32) * mm_nt(e2, wout_ref[0])).astype(LOW)
-    x1 = x1_ref[0].astype(F32)
+    e1 = (s1_ref[b].astype(F32) * mm_nt(e2, wout_ref[0])).astype(LOW)
+    x1 = x1_ref[b].astype(F32)
     t1 = (x1 * gain_ref[0:1, :] + shift_ref[0:1, :]).astype(LOW)
     add(C_IN, mm_tn(t1, e1[:, :width]))
     add(C_IN + width, mm_tn(t1, e1[:, width:]))
@@ -297,19 +288,19 @@
     add(C_SMALL + 8, col_sum(g1))
     g1 = ln_back(g1, x1, wide(r1_ref), gain_ref[0:1, :])
     et = g1.astype(LOW)
-    add(C_O, mm_tn(tc_ref[0], et))
+    add(C_O, mm_tn(tc_ref[b], et))
     add(C_SMALL + 2, col_sum(et))
     etc = mm_nt(et, wo_ref[0]).astype(LOW)
     for v in range(lvars):
         part = slice(v * segs, (v + 1) * segs)
         ex = spread_heads(etc[part], heads_ref)
-        prob_low = p_ref[0, part, :]
+        prob_low = p_ref[b, part, :]
         prob = prob_low.astype(F32)
-        weighted = prob * mm_nt(v_ref[0, part, :], ex)
+        weighted = prob * mm_nt(v_ref[b, part, :], ex)
         ets = (weighted - prob * jnp.sum(weighted, axis=0, keepdims=True)).astype(LOW)
         gv_ref[part, :] = mm(prob_low, ex).astype(LOW)
-        gk_ref[part, :] = (scale * mm(ets, spread_heads(q_ref[0, part, :], heads_ref))).astype(LOW)
-        gq_ref[part, :] = (scale * gather_heads(mm_tn(ets, k_ref[0, part, :]), headsf_ref, segs)).astype(LOW)
+        gk_ref[part, :] = (scale * mm(ets, spread_heads(q_ref[b, part, :], heads_ref))).astype(LOW)
+        gq_ref[part, :] = (scale * gather_heads(mm_tn(ets, k_ref[b, part, :]), headsf_ref, segs)).astype(LOW)
     factor = fac_ref[0]
     low = ((tok_ref[0].reshape(rows, width).astype(F32) - off_ref[0]) * factor).astype(LOW)
     gq = gq_ref[...]
@@ -322,6 +313,121 @@
     add(C_SMALL + 1, col_sum(gv))
     gs = g1 + mm_nt(gq, wi_ref[0, 0]) + mm_nt(gk, wi_ref[0, 1]) + mm_nt(gv, wi_ref[0, 2])
     gin_ref[0] = (gs * factor).reshape(lvars, segs, width)
+
+
+def layer_kernel(
+    lvars, lsegs, nvars, routers, steps, var_size,
+    tok_ref, cot_ref, off_ref, fac_ref, lim_ref, router_ref, wi0_ref, wi1_ref, wi2_ref, wo_ref, ab_ref,
+    win0_ref, win1_ref, bin_ref, wout0_ref, wout1_ref, bout_ref, gain_ref, shift_ref,
+    heads_ref, headsf_ref, split_ref, join_ref, mask_ref, grow_ref, shrink_ref, sumr_ref, swap_ref, back_ref,
+    out_ref, gin_ref, gradsb_ref, gradsc_ref, groute_ref,
+    sent_ref, came_ref, qx_ref, kq_ref, gq_ref, gk_ref, gv_ref, send_sem, recv_sem, *kept,
+):
+    step = pl.program_id(0)
+    me = lax.axis_index("var")
+    width = tok_ref.shape[3]
+    rows = lvars * tok_ref.shape[2]
+    block = rows // var_size
+
+    def place(kind, b, u):
+        return came_ref.at[kind, b, u]
+
+    def copy(kind, b, k):
+        target = lax.rem(me + k, var_size)
+        return pltpu.make_async_remote_copy(
+            src_ref=sent_ref.at[kind, b, target],
+            dst_ref=place(kind, b, me),
+            send_sem=send_sem.at[kind, b],
+            recv_sem=recv_sem.at[kind, b],
+            device_id={"var": target},
+            device_id_type=MESH,
+        )
+
+    def whole(kind, b):
+        others = pl.ds(0, var_size - 1)
+        return pltpu.make_async_remote_copy(
+            src_ref=sent_ref.at[kind, b, others],
+            dst_ref=came_ref.at[kind, b, others],
+            send_sem=send_sem.at[kind, b],
+            recv_sem=recv_sem.at[kind, b],
+            device_id={"var": lax.rem(me + 1, var_size)},
+            device_id_type=MESH,
+        )
+
+    def store(kind, b, value):
+        value = value.reshape(var_size, block, width)
+        sent_ref[kind, b] = value
+        place(kind, b, me)[...] = sent_ref[kind, b, me]
+
+    def send(kind, b):
+        for k in range(1, var_size):
+            copy(kind, b, k).start()
+
+    @pl.when(step < steps)
+    def _():
+        b = step
+
+        @pl.when(b == 0)
+        def _():
+            barrier = pltpu.get_barrier_semaphore()
+            for k in range(1, var_size):
+                pl.semaphore_signal(barrier, inc=1, device_id={"var": lax.rem(me + k, var_size)}, device_id_type=MESH)
+
+        store(1, b, mm(split_ref[...], cot_ref[0].reshape(rows, width)).astype(LOW))
+        t2 = time_forward(
+            lvars, b, tok_ref, off_ref, fac_ref, wi0_ref, wo_ref, ab_ref, win0_ref, bin_ref, wout0_ref, bout_ref,
+            gain_ref, shift_ref, heads_ref, headsf_ref, kept,
+        )
+        store(0, b, mm(split_ref[...], t2).astype(LOW))
+
+        @pl.when(b == 0)
+        def _():
+            pl.semaphore_wait(pltpu.get_barrier_semaphore(), var_size - 1)
+
+        send(0, b)
+        send(1, b)
+
+    @pl.when((step >= steps) & (step < 2 * steps))
+    def _():
+        b = step - steps
+
+        def arrived(kind):
+            whole(kind, b).wait_recv()
+            return came_ref[kind, b]
+
+        def leaving(kind, value):
+            store(kind, b, value)
+            if kind == 2:
+                send(kind, b)
+
+        router_part(
+            lsegs, nvars, routers, steps, b, arrived, leaving,
+            lim_ref, router_ref, wi1_ref, wi2_ref, wo_ref, ab_ref, win1_ref, bin_ref, wout1_ref, bout_ref,
+            gain_ref, shift_ref, mask_ref, grow_ref, shrink_ref, sumr_ref, swap_ref, back_ref,
+            gradsb_ref, groute_ref, qx_ref, kq_ref,
+        )
+
+    @pl.when(step >= 2 * steps)
+    def _():
+        b = step - 2 * steps
+        send(3, b)
+
+        def arrived(kind):
+            whole(kind, b).wait_recv()
+            return came_ref[kind, b]
+
+        time_backward(
+            lvars, b, arrived, tok_ref, off_ref, fac_ref, wi0_ref, wo_ref, win0_ref, wout0_ref, gain_ref, shift_ref,
+            heads_ref, headsf_ref, join_ref, kept, gin_ref, gradsc_ref, gq_ref, gk_ref, gv_ref,
+        )
+
+    @pl.when(step == 3 * steps - 1)
+    def _():
+        for b in range(steps):
+            whole(3, b).wait_recv()
+            for kind in range(4):
+                whole(kind, b).wait_send()
+        out_ref[...] = came_ref[3]
 
 
 def reduce_kernel(axes, x_ref, o_ref, acc_ref, send_ref, *scratch):
@@ -464,10 +570,6 @@
     return pl.BlockSpec(shape, lambda b: index)
 
 
-def stepped(shape):
-    return pl.BlockSpec((1,) + shape, lambda b: (b,) + (0,) * len(shape))
-
-
 def on_device(
     var_size, seg_size,
     tokens, domain, counts, domain_mean, domain_scale, attn_inner, attn_outer, attn_bias,
@@ -501,97 +603,73 @@
     grow = (group[:, None] == np.arange(lsegs * SLOTS)[None, :]).astype(np.float32)
     sumr = (np.arange(lanes)[:, None] % HEADS == np.arange(lanes)[None, :] % HEADS).astype(np.float32)
 
-    params = pltpu.CompilerParams(dimension_semantics=("arbitrary",), vmem_limit_bytes=VMEM_LIMIT)
     kept = [
         ((rows, width), LOW), ((rows, width), LOW), ((rows, width), LOW), ((rows, HEADS * segs), LOW),
         ((rows, width), LOW), ((rows, width), LOW), ((rows, 128), F32), ((rows, hidden), LOW),
         ((rows, hidden), LOW), ((rows, width), LOW), ((rows, 128), F32),
     ]
-    whole = lambda x: fixed(x.shape)
-    series = stepped((lvars, segs, width))
-    plane = stepped((rows, width))
-    inner0 = fixed((1,) + attn_inner.shape[1:])
-    outer0 = fixed((1,) + attn_outer.shape[1:])
-    up0 = fixed((1,) + mlp_in.shape[1:])
-    down0 = fixed((1,) + mlp_out.shape[1:])
-    row_spec = stepped((1, width))
-    split_low = jnp.asarray(split, LOW)
-    t2, cot, *residuals = pl.pallas_call(
-        functools.partial(first_kernel, segs, lvars),
-        grid=(batch,),
-        in_specs=[
-            series, series, row_spec, row_spec, inner0, outer0, whole(attn_bias), up0, whole(mlp_in_bias), down0,
-            whole(mlp_out_bias), whole(norm_gain), whole(norm_bias), whole(heads_low), whole(heads_f), whole(split_low),
-        ],
-        out_specs=[plane, plane] + [stepped(shape) for shape, _ in kept],
-        out_shape=[jax.ShapeDtypeStruct((batch, rows, width), LOW)] * 2
-        + [jax.ShapeDtypeStruct((batch,) + shape, dtype) for shape, dtype in kept],
-        compiler_params=params,
-        name="time_forward",
-    )(
-        tokens, cotangent, offset, factor, attn_inner, attn_outer, attn_bias, mlp_in, mlp_in_bias, mlp_out,
-        mlp_out_bias, norm_gain, norm_bias, heads_low, heads_f, split_low,
-    )
-
-    def exchange(x):
-        parts = x.reshape(batch, var_size, rows // var_size, width)
-        return lax.all_to_all(parts, "var", 1, 1, tiled=True).reshape(batch, rows, width)
-
-    t2 = exchange(t2)
-    cot = exchange(cot)
     mine = lax.dynamic_slice_in_dim(router, me * lsegs, lsegs, 0)
     mine = jnp.pad(mine, ((0, 0), (0, SLOTS - routers), (0, 0))).reshape(lsegs * SLOTS, width)
-    inner1 = fixed((1,) + attn_inner.shape[1:], (1, 0, 0, 0))
-    inner2 = fixed((1,) + attn_inner.shape[1:], (2, 0, 0, 0))
-    up1 = fixed((1,) + mlp_in.shape[1:], (1, 0, 0))
-    down1 = fixed((1,) + mlp_out.shape[1:], (1, 0, 0))
-    consts = [mask, jnp.asarray(grow, LOW), jnp.asarray(grow.T, LOW), jnp.asarray(sumr, LOW), jnp.asarray(swap, LOW), jnp.asarray(swap.T, LOW)]
-    out, g2, grads_b, groute = pl.pallas_call(
-        functools.partial(second_kernel, lsegs, nvars, routers, batch),
-        grid=(batch,),
+    inner = [fixed((1,) + attn_inner.shape[1:], (i, 0, 0, 0)) for i in range(3)]
+    up0, up1 = [fixed((1,) + mlp_in.shape[1:], (i, 0, 0)) for i in range(2)]
+    down0, down1 = [fixed((1,) + mlp_out.shape[1:], (i, 0, 0)) for i in range(2)]
+    consts = [jnp.asarray(x, LOW) for x in (split, split.T)] + [mask]
+    consts += [jnp.asarray(x, LOW) for x in (grow, grow.T, sumr, swap, swap.T)]
+
+    def first_last(i):
+        return jnp.where(i < batch, i, jnp.maximum(i - 2 * batch, 0))
+
+    def first(i):
+        return jnp.minimum(i, batch - 1)
+
+    def last(i):
+        return jnp.maximum(i - 2 * batch, 0)
+
+    whole = lambda x: fixed(x.shape)
+    block = (1, lvars, segs, width)
+    row_spec = pl.BlockSpec((1, 1, width), lambda i: (first_last(i), 0, 0))
+    arrived, input_grad, grads_b, grads_c, groute = pl.pallas_call(
+        functools.partial(layer_kernel, lvars, lsegs, nvars, routers, batch, var_size),
+        grid=(3 * batch,),
         in_specs=[
-            plane, plane, stepped((1, lanes)), whole(mine), inner1, inner2, whole(attn_outer), whole(attn_bias), up1,
-            whole(mlp_in_bias), down1, whole(mlp_out_bias), whole(norm_gain), whole(norm_bias),
+            pl.BlockSpec(block, lambda i: (first_last(i), 0, 0, 0)),
+            pl.BlockSpec(block, lambda i: (first(i), 0, 0, 0)),
+            row_spec, row_spec, whole(limit), whole(mine), *inner, whole(attn_outer), whole(attn_bias),
+            up0, up1, whole(mlp_in_bias), down0, down1, whole(mlp_out_bias), whole(norm_gain), whole(norm_bias),
+            whole(heads_low), whole(heads_f),
         ]
         + [whole(c) for c in consts],
-        out_specs=[plane, plane, fixed((B_ROWS, width)), fixed((lsegs * SLOTS, width))],
+        out_specs=[
+            fixed((batch, var_size, rows // var_size, width)),
+            pl.BlockSpec(block, lambda i: (last(i), 0, 0, 0)),
+            fixed((B_ROWS, width)), fixed((C_ROWS, width)), fixed((lsegs * SLOTS, width)),
+        ],
         out_shape=[
-            jax.ShapeDtypeStruct((batch, rows, width), LOW),
-            jax.ShapeDtypeStruct((batch, rows, width), LOW),
+            jax.ShapeDtypeStruct((batch, var_size, rows // var_size, width), LOW),
+            jax.ShapeDtypeStruct(tokens.shape, F32),
             jax.ShapeDtypeStruct((B_ROWS, width), F32),
+            jax.ShapeDtypeStruct((C_ROWS, width), F32),
             jax.ShapeDtypeStruct((lsegs * SLOTS, width), F32),
         ],
-        scratch_shapes=[pltpu.VMEM((lsegs * lanes, width), LOW), pltpu.VMEM((lsegs * lanes, width), F32)],
-        compiler_params=params,
-        name="router_part",
+        scratch_shapes=[
+            pltpu.VMEM((4, batch, var_size, rows // var_size, width), LOW),
+            pltpu.VMEM((4, batch, var_size, rows // var_size, width), LOW),
+            pltpu.VMEM((lsegs * lanes, width), LOW),
+            pltpu.VMEM((lsegs * lanes, width), F32),
+            *[pltpu.VMEM((rows, width), LOW)] * 3,
+            pltpu.SemaphoreType.DMA((4, batch)),
+            pltpu.SemaphoreType.DMA((4, batch)),
+        ]
+        + [pltpu.VMEM((batch,) + shape, dtype) for shape, dtype in kept],
+        compiler_params=pltpu.CompilerParams(
+            dimension_semantics=("arbitrary",), vmem_limit_bytes=VMEM_LIMIT, collective_id=0, has_side_effects=True
+        ),
+        name="layer",
     )(
-        t2, cot, limit, mine, attn_inner, attn_inner, attn_outer, attn_bias, mlp_in, mlp_in_bias, mlp_out,
-        mlp_out_bias, norm_gain, norm_bias, *consts,
+        tokens, cotangent, offset, factor, limit, mine, attn_inner, attn_inner, attn_inner, attn_outer, attn_bias,
+        mlp_in, mlp_in, mlp_in_bias, mlp_out, mlp_out, mlp_out_bias, norm_gain, norm_bias, heads_low, heads_f, *consts,
     )
-    g2 = exchange(g2)
-    out = exchange(out)
-    join_low = jnp.asarray(split.T, LOW)
-    output, input_grad, grads_c = pl.pallas_call(
-        functools.partial(third_kernel, segs, lvars),
-        grid=(batch,),
-        in_specs=[
-            plane, plane, series, row_spec, row_spec, inner0, outer0, up0, down0, whole(norm_gain), whole(norm_bias),
-            whole(heads_low), whole(heads_f), whole(join_low),
-        ]
-        + [stepped(shape) for shape, _ in kept],
-        out_specs=[series, series, fixed((C_ROWS, width))],
-        out_shape=[
-            jax.ShapeDtypeStruct(tokens.shape, F32),
-            jax.ShapeDtypeStruct(tokens.shape, F32),
-            jax.ShapeDtypeStruct((C_ROWS, width), F32),
-        ],
-        scratch_shapes=[pltpu.VMEM((rows, width), LOW)] * 3,
-        compiler_params=params,
-        name="time_backward",
-    )(
-        out, g2, tokens, offset, factor, attn_inner, attn_outer, mlp_in, mlp_out, norm_gain, norm_bias,
-        heads_low, heads_f, join_low, *residuals,
-    )
+    output = arrived.reshape(batch, var_size, lvars, lsegs, width).transpose(0, 2, 1, 3, 4).reshape(tokens.shape).astype(F32)
 
     groute = groute.reshape(lsegs, SLOTS, width)[:, :routers]
     routes = lax.dynamic_update_slice_in_dim(jnp.zeros(router.shape, F32), groute, me * lsegs, 0)

time: 326 us -> 214 us (0.66)
  waiting for transfers between devices: 90.4 us -> 0 us
  starting transfers between devices: 22 us -> 0 us
  Pallas kernels: 173 us -> 178 us
  local copies, waits for them, and re-layouts: 19.6 us -> 16.1 us
    all_to_all x4 -> x0, waiting for transfers between devices: 90.4 us -> none  [exchange(): lax.all_to_all(parts, 'var', 1, 1, tiled=True).reshape(batch, rows, width)]
    all_to_all x4 -> x0, starting transfers between devices: 22 us -> none  [exchange(): lax.all_to_all(parts, 'var', 1, 1, tiled=True).reshape(batch, rows, width)]
    reshape x4 -> x0, local copies, waits for them, and re-layouts: 6.87 us -> none  [exchange(): parts = x.reshape(batch, var_size, rows // var_size, width)]
    all_to_all x4 -> x0, local copies, waits for them, and re-layouts: 4.25 us -> none  [exchange(): lax.all_to_all(parts, 'var', 1, 1, tiled=True).reshape(batch, rows, width)]
    unnamed x36 -> x19, local copies, waits for them, and re-layouts: 1.32 us -> 5.22 us
    pallas_call x3 -> x1, Pallas kernels: 110 us -> 113 us  [on_device(): pl.pallas_call(functools.partial(layer_kernel, lvars, lsegs, nvars, route...]
  transfers between devices with their start and end apart: 4 -> 0, of which waited for: 4 -> 0; matrix products, arithmetic and copies ran while one was open for 2% -> 0% of each run, Pallas kernels for 0% -> 0%
where the time goes in v2:
time: 214 us; the launch traced here: 212 us
  Pallas kernels  178 us (83%)
  other arithmetic  17 us (8%)
  local copies, waits for them, and re-layouts  16.1 us (8%)
    pallas_call x1, Pallas kernels, on_device(): pl.pallas_call(functools.partial(layer_kernel, lvars, lsegs, nvars, route...  113 us
    pallas_call x1, Pallas kernels, all_reduce(): pl.pallas_call(kernel, out_shape=jax.ShapeDtypeStruct((padded, width), LO...  65.1 us
    unnamed x19, local copies, waits for them, and re-layouts  5.22 us
    concatenate x1, other arithmetic, on_device(): jnp.concatenate([grads_b, grads_c, routes], axis=0)  4.3 us

profile of v2, /device:TPU:29, one launch (start us, length us, event | category | flops | bytes accessed | tf_op | source)
XLA Modules:
  0.0 212.3 jit_solution(4212299890525615964)
XLA Ops:
  0.7 0.8 select_reduce_fusion.2
  1.5 0.7 iota_compare_fusion.1
  2.1 0.7 broadcast_in_dim.71.lim_ref
  2.8 0.8 select_reduce_fusion
  4.8 0.6 pad.8.clone
  5.5 113.3 %layer.1 = (bf16[8,8,32,256]{3,2,1,0:T(8,128)(2,1)}, f32[8,4,64,256]{3,2,1,0:T(8,128)}, f32[3088,256]{1,0:T(8,128)}, f32[2064,256]{1,0:T(8,128)}, f32[128,256]{1,0:T(8,128)}) custom-call(bf16[8,4,64,256]{3,2,1,0:T(8,128)(2,1)} %tok_ref.1, bf16[8,4,64,256]{3,2,1,0:T(8,128)(2,1)} %cot_ref.1, f32[8,1,256]{2,1,0:T(1,128)} %broadcast_in_dim.66.off_ref, ...), custom_call_target="tpu_custom_call" | custom-call | tf_op jit(solution)/shard_map/layer/pallas_call | solution.py:631
  118.9 1.0 slice_dynamic-update-slice_fusion
  120.0 1.6 copy_bitcast_fusion
  121.6 0.7 copy-done.2
  122.3 4.3 %select_maximum_fusion.refs_0_ = f32[6144,256]{1,0:T(8,128)} fusion(f32[640,256]{1,0:T(8,128)S(1)} %reshape.82, f32[2064,256]{1,0:T(8,128)S(1)} %copy-done.2, f32[3088,256]{1,0:T(8,128)} %get-tuple-element.19), kind=kLoop, calls=%fused_computation | loop fusion | flops 9437184 | bytes 12222464 | tf_op jit(solution)/shard_map/concatenate | solution.py:677
  126.6 65.1 %reduce.1 = bf16[6144,256]{1,0:T(8,128)(2,1)} custom-call(f32[6144,256]{1,0:T(8,128)} %select_maximum_fusion.refs_0_), custom_call_target="tpu_custom_call" | custom-call | tf_op jit(solution)/shard_map/reduce/pallas_call | solution.py:552
  191.7 2.3 %slice_convert_fusion = f32[5792,256]{1,0:T(8,128)S(1)} fusion(bf16[6144,256]{1,0:T(8,128)(2,1)} %reduce.1), kind=kLoop, calls=%fused_computation.3 | loop fusion | flops 1482752 | bytes 8896512 | tf_op jit(solution)/shard_map/convert_element_type | solution.py:677
  194.7 1.9 copy-done.1
  197.2 0.8 fusion
  199.2 2.0 slice.143
  201.2 1.3 reshape.86
  202.5 1.2 copy.46
  203.7 1.5 fusion.2
  205.4 1.0 pad_maximum_fusion.1
  206.6 1.0 pad_maximum_fusion.2
  207.6 0.8 slice-done.3
  208.5 1.6 pad_maximum_fusion
  210.0 0.9 pad_maximum_fusion.3
  211.0 1.3 copy.53
  (35 shorter events, 4.3 us)
Async XLA Ops:
  0.6 4.2 %copy-start = (bf16[64,10,256]{2,0,1:T(8,128)(2,1)S(1)}, bf16[64,10,256]{2,0,1:T(8,128)(2,1)}, u32[]{:S(2)}) copy-start(bf16[64,10,256]{2,0,1:T(8,128)(2,1)} %param.40) | copy-start | bytes 983044
  118.7 1.3 copy-start.4
  120.0 2.3 %copy-start.2 = (f32[2064,256]{1,0:T(8,128)S(1)}, f32[2064,256]{1,0:T(8,128)}, u32[]{:S(2)}) copy-start(f32[2064,256]{1,0:T(8,128)} %get-tuple-element.20) | copy-start | bytes 6340612
  194.1 2.5 %copy-start.1 = (f32[5792,256]{1,0:T(8,128)}, f32[5792,256]{1,0:T(8,128)S(1)}, u32[]{:S(2)}) copy-start(f32[5792,256]{1,0:T(8,128)S(1)} %slice_convert_fusion) | copy-start | bytes 17793028
  201.2 5.2 %slice-start = ((s8[5931008]{0:T(1024)(128)(4,1)}), s8[1736704]{0:T(1024)(128)(4,1)S(1)}, s32[]{:S(2)}) async-start(s8[5931008]{0:T(1024)(128)(4,1)} %bitcast.29), calls=%async_computation | async-start | bytes 3473408
  203.7 2.7 %slice-start.1 = ((s8[5931008]{0:T(1024)(128)(4,1)}), s8[4194304]{0:T(1024)(128)(4,1)S(1)}, s32[]{:S(2)}) async-start(s8[5931008]{0:T(1024)(128)(4,1)} %bitcast.29), calls=%async_computation.1 | async-start | bytes 8388608
  206.4 1.2 slice-start.2
  206.4 2.0 slice-start.3
  208.5 2.5 %copy-start.3 = (f32[8,4,64,256]{3,2,1,0:T(8,128)S(1)}, f32[8,4,64,256]{3,2,1,0:T(8,128)}, u32[]{:S(2)}) copy-start(f32[8,4,64,256]{3,2,1,0:T(8,128)} %get-tuple-element.93) | copy-start | bytes 6291460

commit v3 on v2

v3 whole, which is shorter than its diff:
```python
import functools

import jax
import jax.numpy as jnp
import numpy as np
from jax import lax
from jax.experimental import pallas as pl
from jax.experimental.pallas import tpu as pltpu
from jax.sharding import PartitionSpec as P

HEADS = 8
SLOTS = 16
EPS = 1e-05
MASKED = -1e30
MESH = pl.DeviceIdType.MESH
F32 = jnp.float32
LOW = jnp.bfloat16
VMEM_LIMIT = 56 * 1024 * 1024


def mm(a, b):
    return jnp.dot(a, b, preferred_element_type=F32)


def mm_nt(a, b):
    return lax.dot_general(a, b, (((1,), (1,)), ((), ())), preferred_element_type=F32)


def mm_tn(a, b):
    return lax.dot_general(a, b, (((0,), (0,)), ((), ())), preferred_element_type=F32)


def ln_stats(a):
    mean = jnp.mean(a, axis=1, keepdims=True)
    center = a - mean
    var = jnp.mean(center * center, axis=1, keepdims=True)
    rstd = lax.rsqrt(var + EPS)
    return center * rstd, rstd


def ln_back(g, xhat, rstd, gain):
    gy = g * gain
    first = jnp.mean(gy, axis=1, keepdims=True)
    second = jnp.mean(gy * xhat, axis=1, keepdims=True)
    return rstd * (gy - first - xhat * second)


def gelu_both(z):
    k0 = np.float32(np.sqrt(2.0 / np.pi))
    k1 = np.float32(0.044715)
    square = z * z
    t = jnp.tanh(k0 * z * (1.0 + k1 * square))
    half = 0.5 * (1.0 + t)
    slope = half + 0.5 * z * (1.0 - t * t) * (k0 * (1.0 + 3.0 * k1 * square))
    return z * half, slope


def col_sum(x):
    return jnp.sum(x.astype(F32), axis=0, keepdims=True)


def spread_heads(x, heads_ref):
    return jnp.concatenate([x * heads_ref[h : h + 1, :] for h in range(HEADS)], axis=0)


def gather_heads(x, headsf_ref, rows):
    total = x[:rows] * headsf_ref[0:1, :]
    for h in range(1, HEADS):
        total = total + x[h * rows : (h + 1) * rows] * headsf_ref[h : h + 1, :]
    return total


def time_forward(
    lvars, b, tok_ref, offset, factor, wi_ref, wo_ref, ab_ref, win_ref, bin_ref, wout_ref, bout_ref,
    gain_ref, shift_ref, heads_ref, headsf_ref, kept,
):
    q_ref, k_ref, v_ref, p_ref, tc_ref, x1_ref, r1_ref, f1_ref, s1_ref, x2_ref, r2_ref = kept
    segs, width = tok_ref.shape[2:]
    rows = lvars * segs
    scale = np.float32((width // HEADS) ** (-0.5))
    tok = tok_ref[0].reshape(rows, width).astype(F32)
    start = (tok - offset) * factor
    low = start.astype(LOW)
    q_ref[b] = (mm(low, wi_ref[0, 0]) + ab_ref[0, 0:1, :]).astype(LOW)
    k_ref[b] = mm(low, wi_ref[0, 1]).astype(LOW)
    v_ref[b] = (mm(low, wi_ref[0, 2]) + ab_ref[0, 1:2, :]).astype(LOW)
    for v in range(lvars):
        part = slice(v * segs, (v + 1) * segs)
        spread = spread_heads(q_ref[b, part, :], heads_ref)
        scores = mm_nt(k_ref[b, part, :], spread)
        top = jnp.max(scores, axis=0, keepdims=True)
        expo = jnp.exp((scores - top) * scale)
        prob = (expo / jnp.sum(expo, axis=0, keepdims=True)).astype(LOW)
        p_ref[b, part, :] = prob
        tc_ref[b, part, :] = gather_heads(mm_tn(prob, v_ref[b, part, :]), headsf_ref, segs).astype(LOW)
    a1 = start + mm(tc_ref[b], wo_ref[0]) + ab_ref[0, 2:3, :]
    x1, r1 = ln_stats(a1)
    x1_ref[b] = x1.astype(LOW)
    r1_ref[b] = jnp.broadcast_to(r1, (rows, 128))
    t1 = x1 * gain_ref[0:1, :] + shift_ref[0:1, :]
    act, slope = gelu_both(mm(t1.astype(LOW), win_ref[0]) + bin_ref[0:1, :])
    f1_ref[b] = act.astype(LOW)
    s1_ref[b] = slope.astype(LOW)
    a2 = t1 + mm(f1_ref[b], wout_ref[0]) + bout_ref[0:1, :]
    x2, r2 = ln_stats(a2)
    x2_ref[b] = x2.astype(LOW)
    r2_ref[b] = jnp.broadcast_to(r2, (rows, 128))
    return (x2 * gain_ref[1:2, :] + shift_ref[1:2, :]).astype(LOW)


B_SQ, B_SK, B_SV, B_RQ, B_RK, B_RV, B_O1, B_O2, B_IN, B_OUT, B_ROUTE = [256 * i for i in (0, 1, 2, 3, 4, 5, 6, 7, 8, 10, 12)]
M_IN, M_OUT, M_ROWS = [256 * i for i in (0, 2, 4)]
T_Q, T_K, T_V, T_O, T_ROWS = [256 * i for i in (0, 1, 2, 3, 4)]
S_BIAS, S_IN, S_OUT, S_GAIN, S_SHIFT, S_ROWS = 0, 9, 13, 15, 19, 32


def router_part(
    lsegs, nvars, routers, steps, b, arrived, leaving,
    limit, router_ref, wi1_ref, wi2_ref, wo_ref, ab_ref, win_ref, bin_ref, wout_ref, bout_ref,
    gain_ref, shift_ref, mask_ref, grow_ref, shrink_ref, sumr_ref, perm_ref, back_ref,
    grads_ref, small_ref, qx_ref, kq_ref, first_route,
):
    rows, width = perm_ref.shape[0], wo_ref.shape[1]
    lanes = SLOTS * HEADS
    scale = np.float32((width // HEADS) ** (-0.5))

    def expand(x):
        return (mm(grow_ref[...], x).astype(LOW).reshape(-1, 16, width) * mask_ref[...][None]).reshape(-1, width)

    def contract(x):
        return mm(shrink_ref[...], (x.astype(LOW).reshape(-1, 16, width) * mask_ref[...][None]).reshape(-1, width))

    @pl.when(b == 0)
    def _():
        grads_ref[...] = jnp.zeros_like(grads_ref)
        kq_ref[...] = jnp.zeros_like(kq_ref)
        sq = (mm(router_ref[...], wi1_ref[0, 0]) + ab_ref[1, 0:1, :]).astype(LOW)
        qx_ref[...] = expand(sq)

    def per_segment(f):
        return [f(slice(s * nvars, (s + 1) * nvars), slice(s * lanes, (s + 1) * lanes)) for s in range(lsegs)]

    t2 = mm(perm_ref[...], arrived(0).reshape(rows, width)).astype(LOW)
    sk = mm(t2, wi1_ref[0, 1]).astype(LOW)
    sv = (mm(t2, wi1_ref[0, 2]) + ab_ref[1, 1:2, :]).astype(LOW)
    rq = (mm(t2, wi2_ref[0, 0]) + ab_ref[2, 0:1, :]).astype(LOW)
    valid = lax.broadcasted_iota(jnp.int32, (nvars, lanes), 0).astype(F32) < limit

    def send_prob(n, l):
        scores = jnp.where(valid, mm_nt(sk[n], qx_ref[l, :]), MASKED)
        top = jnp.max(scores, axis=0, keepdims=True)
        expo = jnp.where(valid, jnp.exp((scores - top) * scale), 0.0)
        return expo / jnp.sum(expo, axis=0, keepdims=True)

    sp = per_segment(send_prob)
    sp_low = [x.astype(LOW) for x in sp]
    pre = contract(jnp.concatenate([mm_tn(sp_low[s], sv[s * nvars : (s + 1) * nvars]) for s in range(lsegs)], axis=0))
    pre_low = pre.astype(LOW)
    buffer = (mm(pre_low, wo_ref[1]) + ab_ref[1, 2:3, :]).astype(LOW)
    rkx = expand(mm(buffer, wi2_ref[0, 1]).astype(LOW))
    rvx = expand((mm(buffer, wi2_ref[0, 2]) + ab_ref[2, 1:2, :]).astype(LOW))
    scores = jnp.concatenate(per_segment(lambda n, l: mm_nt(rq[n], rkx[l])), axis=0)
    real = lax.broadcasted_iota(jnp.int32, (rows, lanes), 1) < routers * HEADS
    scores = jnp.where(real, scores, MASKED)
    top = scores
    shift = lanes // 2
    while shift >= HEADS:
        top = jnp.maximum(top, pltpu.roll(top, shift, 1))
        shift //= 2
    expo = jnp.where(real, jnp.exp((scores - top) * scale), 0.0)
    rp = expo / mm(expo.astype(LOW), sumr_ref[...])
    rp_low = rp.astype(LOW)
    rc = jnp.concatenate(per_segment(lambda n, l: mm(rp_low[n], rvx[l])), axis=0).astype(LOW)
    a3 = t2.astype(F32) + mm(rc, wo_ref[2]) + ab_ref[2, 2:3, :]
    x3, r3 = ln_stats(a3)
    t3 = x3 * gain_ref[2:3, :] + shift_ref[2:3, :]
    t3_low = t3.astype(LOW)
    act, slope = gelu_both(mm(t3_low, win_ref[0]) + bin_ref[1:2, :])
    f2 = act.astype(LOW)
    a4 = t3 + mm(f2, wout_ref[0]) + bout_ref[1:2, :]
    x4, r4 = ln_stats(a4)
    out = (x4 * gain_ref[3:4, :] + shift_ref[3:4, :]).astype(LOW)
    leaving(3, mm(back_ref[...], out).astype(LOW))

    def add(row, value):
        grads_ref[row : row + value.shape[0], :] += value

    def add_small(row, value):
        small_ref[row : row + 1, :] += value

    cot = mm(perm_ref[...], arrived(1).reshape(rows, width))
    add_small(S_GAIN + 3, col_sum(cot * x4))
    add_small(S_SHIFT + 3, col_sum(cot))
    g4 = ln_back(cot, x4, r4, gain_ref[3:4, :])
    e4 = g4.astype(LOW)
    add(B_OUT, mm_tn(f2, e4))
    add_small(S_OUT + 1, col_sum(e4))
    e3 = (slope * mm_nt(e4, wout_ref[0])).astype(LOW)
    add(B_IN, mm_tn(t3_low, e3[:, :width]))
    add(B_IN + width, mm_tn(t3_low, e3[:, width:]))
    e3_sum = col_sum(e3)
    add_small(S_IN + 2, e3_sum[:, :width])
    add_small(S_IN + 3, e3_sum[:, width:])
    g3 = g4 + mm_nt(e3, win_ref[0])
    add_small(S_GAIN + 2, col_sum(g3 * x3))
    add_small(S_SHIFT + 2, col_sum(g3))
    g3 = ln_back(g3, x3, r3, gain_ref[2:3, :])
    eo = g3.astype(LOW)
    add(B_O2, mm_tn(rc, eo))
    add_small(S_BIAS + 8, col_sum(eo))
    ec = mm_nt(eo, wo_ref[2]).astype(LOW)
    dp = jnp.concatenate(per_segment(lambda n, l: mm_nt(ec[n], rvx[l])), axis=0)
    ds = (scale * rp * (dp - mm((rp * dp).astype(LOW), sumr_ref[...]))).astype(LOW)
    erq = jnp.concatenate(per_segment(lambda n, l: mm(ds[n], rkx[l])), axis=0).astype(LOW)
    erk = contract(jnp.concatenate(per_segment(lambda n, l: mm_tn(ds[n], rq[n])), axis=0)).astype(LOW)
    erv = contract(jnp.concatenate(per_segment(lambda n, l: mm_tn(rp_low[n], ec[n])), axis=0)).astype(LOW)
    add(B_RQ, mm_tn(t2, erq))
    add_small(S_BIAS + 6, col_sum(erq))
    add(B_RK, mm_tn(buffer, erk))
    add(B_RV, mm_tn(buffer, erv))
    add_small(S_BIAS + 7, col_sum(erv))
    eb = (mm_nt(erk, wi2_ref[0, 1]) + mm_nt(erv, wi2_ref[0, 2])).astype(LOW)
    add(B_O1, mm_tn(pre_low, eb))
    add_small(S_BIAS + 5, col_sum(eb))
    epx = expand(mm_nt(eb, wo_ref[1]).astype(LOW))
    dss = []
    for s in range(lsegs):
        dps = mm_nt(sv[s * nvars : (s + 1) * nvars], epx[s * lanes : (s + 1) * lanes])
        weighted = sp[s] * dps
        center = jnp.sum(weighted, axis=0, keepdims=True)
        dss.append((scale * (weighted - sp[s] * center)).astype(LOW))
    esv = jnp.concatenate([mm(sp_low[s], epx[s * lanes : (s + 1) * lanes]) for s in range(lsegs)], axis=0).astype(LOW)
    esk = jnp.concatenate([mm(dss[s], qx_ref[s * lanes : (s + 1) * lanes, :]) for s in range(lsegs)], axis=0).astype(LOW)
    for s in range(lsegs):
        kq_ref[s * lanes : (s + 1) * lanes, :] += mm_tn(dss[s], sk[s * nvars : (s + 1) * nvars])
    add(B_SK, mm_tn(t2, esk))
    add(B_SV, mm_tn(t2, esv))
    add_small(S_BIAS + 4, col_sum(esv))
    g2 = g3 + mm_nt(erq, wi2_ref[0, 0]) + mm_nt(esk, wi1_ref[0, 1]) + mm_nt(esv, wi1_ref[0, 2])
    leaving(2, mm(back_ref[...], g2.astype(LOW)).astype(LOW))

    @pl.when(b == steps - 1)
    def _():
        kq = contract(kq_ref[...])
        kq_low = kq.astype(LOW)
        grads_ref[B_SQ : B_SQ + width, :] = mm_tn(router_ref[...], kq_low)
        add_small(S_BIAS + 3, col_sum(kq))
        grads_ref[pl.ds(first_route, lsegs * SLOTS), :] = mm_nt(kq_low, wi1_ref[0, 0])


def feed_backward(
    rows, b, arrived, wo_ref, win_ref, wout_ref, gain_ref, shift_ref, perm_ref, kept, feeds_ref, times_ref, small_ref,
    etc_ref, g1_ref,
):
    q_ref, k_ref, v_ref, p_ref, tc_ref, x1_ref, r1_ref, f1_ref, s1_ref, x2_ref, r2_ref = kept
    width = wo_ref.shape[1]

    @pl.when(b == 0)
    def _():
        feeds_ref[...] = jnp.zeros_like(feeds_ref)
        times_ref[...] = jnp.zeros_like(times_ref)

    def add(ref, row, value):
        ref[row : row + value.shape[0], :] += value

    def wide(ref):
        return jnp.concatenate([ref[b]] * (width // 128), axis=1)

    g2 = mm(perm_ref[...], arrived(2).reshape(rows, width))
    x2 = x2_ref[b].astype(F32)
    add(small_ref, S_GAIN + 1, col_sum(g2 * x2))
    add(small_ref, S_SHIFT + 1, col_sum(g2))
    g2 = ln_back(g2, x2, wide(r2_ref), gain_ref[1:2, :])
    e2 = g2.astype(LOW)
    add(feeds_ref, M_OUT, mm_tn(f1_ref[b], e2))
    add(small_ref, S_OUT, col_sum(e2))
    e1 = (s1_ref[b].astype(F32) * mm_nt(e2, wout_ref[0])).astype(LOW)
    x1 = x1_ref[b].astype(F32)
    t1 = (x1 * gain_ref[0:1, :] + shift_ref[0:1, :]).astype(LOW)
    add(feeds_ref, M_IN, mm_tn(t1, e1[:, :width]))
    add(feeds_ref, M_IN + width, mm_tn(t1, e1[:, width:]))
    e1_sum = col_sum(e1)
    add(small_ref, S_IN, e1_sum[:, :width])
    add(small_ref, S_IN + 1, e1_sum[:, width:])
    g1 = g2 + mm_nt(e1, win_ref[0])
    add(small_ref, S_GAIN, col_sum(g1 * x1))
    add(small_ref, S_SHIFT, col_sum(g1))
    g1 = ln_back(g1, x1, wide(r1_ref), gain_ref[0:1, :])
    g1_ref[b] = g1
    et = g1.astype(LOW)
    add(times_ref, T_O, mm_tn(tc_ref[b], et))
    add(small_ref, S_BIAS + 2, col_sum(et))
    etc_ref[b] = mm_nt(et, wo_ref[0]).astype(LOW)


def time_backward(lvars, b, tok_ref, offset, factor, heads_ref, headsf_ref, kept, times_ref, small_ref, etc_ref):
    q_ref, k_ref, v_ref, p_ref = kept[:4]
    segs, width = tok_ref.shape[2:]
    rows = lvars * segs
    scale = np.float32((width // HEADS) ** (-0.5))

    def add(ref, row, value):
        ref[row : row + value.shape[0], :] += value

    for v in range(lvars):
        part = slice(v * segs, (v + 1) * segs)
        ex = spread_heads(etc_ref[b, part, :], heads_ref)
        prob_low = p_ref[b, part, :]
        prob = prob_low.astype(F32)
        weighted = prob * mm_nt(v_ref[b, part, :], ex)
        ets = (weighted - prob * jnp.sum(weighted, axis=0, keepdims=True)).astype(LOW)
        v_ref[b, part, :] = mm(prob_low, ex).astype(LOW)
        gk = (scale * mm(ets, spread_heads(q_ref[b, part, :], heads_ref))).astype(LOW)
        q_ref[b, part, :] = (scale * gather_heads(mm_tn(ets, k_ref[b, part, :]), headsf_ref, segs)).astype(LOW)
        k_ref[b, part, :] = gk
    low = ((tok_ref[0].reshape(rows, width).astype(F32) - offset) * factor).astype(LOW)
    add(times_ref, T_Q, mm_tn(low, q_ref[b]))
    add(times_ref, T_K, mm_tn(low, k_ref[b]))
    add(times_ref, T_V, mm_tn(low, v_ref[b]))
    add(small_ref, S_BIAS, col_sum(q_ref[b]))
    add(small_ref, S_BIAS + 1, col_sum(v_ref[b]))


class Sum:
    def __init__(self, axes, direct, acc, send, total, recv, sems):
        self.axes, self.acc, self.send, self.total, self.recv, self.sems = axes, acc, send, total, recv, sems
        self.direct = direct
        self.plan = []
        half = acc.shape[0] // 2
        for part, order in enumerate(self.orders({name: axis[1] for name, axis in axes.items()})):
            start, size, levels = part * half, half, []
            for depth, name in enumerate(order):
                index, count, _ = axes[name]
                whole = direct and depth == len(order) - 1
                size = size if whole else size // count
                levels.append((name, start, size))
                start = start if whole else start + index * size
            self.plan.append(levels)
        self.levels = len(self.plan[0])
        self.last = 2 * self.levels - (1 if direct else 0)

    @staticmethod
    def orders(counts):
        names = [name for name in counts if counts[name] > 1]
        if len(names) < 4:
            return [names, names]
        return [names, [names[0], names[2], names[1], names[3]]]

    @classmethod
    def scratch(cls, rows, width, counts, direct):
        recv, copies = [], 0
        for order in cls.orders(counts):
            size = rows // 2
            for depth, name in enumerate(order):
                whole = direct and depth == len(order) - 1
                size = size if whole else size // counts[name]
                recv.append(pltpu.VMEM((counts[name] if whole else counts[name] - 1, size, width), LOW))
                copies += counts[name] - 1
        return [
            pltpu.VMEM((rows, width), F32), pltpu.VMEM((rows, width), LOW), pltpu.VMEM((rows, width), LOW),
            *[pltpu.SemaphoreType.DMA((copies,))] * 4, *recv,
        ]

    def rows(self, start, size):
        return pl.ds(start if isinstance(start, int) else pl.multiple_of(start, 16), size)

    def whole(self, level):
        return self.direct and level == self.levels - 1

    def copies(self, level, gather):
        send_sem, recv_sem = self.sems[2:] if gather else self.sems[:2]
        found, counter = [], 0
        for part, levels in enumerate(self.plan):
            for depth, (name, start, size) in enumerate(levels):
                index, count, target = self.axes[name]
                for k in range(1, count):
                    if depth == level:
                        peer = lax.rem(index + k, count)
                        recv = self.recv[part * self.levels + level]
                        if self.whole(level):
                            rows, where = self.rows(start, size), recv.at[index]
                        else:
                            rows = self.rows(start + (index if gather else peer) * size, size)
                            where = self.total.at[rows, :] if gather else recv.at[k - 1]
                        source = self.total if gather else self.send
                        copy = pltpu.make_async_remote_copy(
                            src_ref=source.at[rows, :],
                            dst_ref=where,
                            send_sem=send_sem.at[counter],
                            recv_sem=recv_sem.at[counter],
                            device_id=target(peer),
                            device_id_type=MESH,
                        )
                        found.append((copy, rows))
                    counter += 1
        return found

    def advance(self, turn):
        levels = self.levels
        if 0 < turn <= levels:
            for copy, _ in self.copies(turn - 1, False):
                copy.wait()
            for part, plan in enumerate(self.plan):
                name, start, size = plan[turn - 1]
                index, count, _ = self.axes[name]
                recv = self.recv[part * levels + turn - 1]
                if self.whole(turn - 1):
                    mine = self.rows(start, size)
                    value = recv[0].astype(F32)
                    others = range(1, count)
                else:
                    mine = self.rows(start + index * size, size)
                    value = self.acc[mine, :]
                    others = range(count - 1)
                for k in others:
                    value = value + recv[k].astype(F32)
                if turn < levels:
                    self.acc[mine, :] = value
                else:
                    self.total[mine, :] = value.astype(LOW)
        elif turn > levels:
            for copy, _ in self.copies(self.last - turn, True):
                copy.wait()
        if turn < levels:
            if self.whole(turn):
                for part, plan in enumerate(self.plan):
                    name, start, size = plan[turn]
                    mine = self.rows(start, size)
                    value = self.acc[mine, :].astype(LOW)
                    self.send[mine, :] = value
                    self.recv[part * levels + turn][self.axes[name][0]] = value
            for copy, rows in self.copies(turn, False):
                if not self.whole(turn):
                    self.send[rows, :] = self.acc[rows, :].astype(LOW)
                copy.start()
        elif turn < self.last:
            for copy, _ in self.copies(self.last - 1 - turn, True):
                copy.start()

    @property
    def turns(self):
        return self.last + 1


class SmallSum:
    def __init__(self, acc, sent, recvs, sems, places):
        self.acc, self.sent, self.recvs, self.sems, self.places = acc, sent, recvs, sems, places

    @staticmethod
    def scratch(rows, width, sizes):
        return [
            pltpu.VMEM((rows, width), F32), pltpu.VMEM((len(sizes), rows, width), LOW),
            *[pltpu.VMEM((size, rows, width), LOW) for size in sizes],
            *[pltpu.SemaphoreType.DMA((size,)) for size in sizes for _ in range(2)],
        ]

    def copies(self, stage):
        name, me, size = self.places[stage]
        send_sem, recv_sem = self.sems[2 * stage : 2 * stage + 2]
        return [
            pltpu.make_async_remote_copy(
                src_ref=self.sent.at[stage],
                dst_ref=self.recvs[stage].at[me],
                send_sem=send_sem.at[k],
                recv_sem=recv_sem.at[k],
                device_id={name: lax.rem(me + k, size)},
                device_id_type=MESH,
            )
            for k in range(1, size)
        ]

    def start(self, stage):
        value = self.acc[...].astype(LOW)
        self.sent[stage] = value
        self.recvs[stage][self.places[stage][1]] = value
        for copy in self.copies(stage):
            copy.start()

    def finish(self, stage):
        for copy in self.copies(stage):
            copy.wait()
        value = self.recvs[stage][0].astype(F32)
        for k in range(1, self.places[stage][2]):
            value = value + self.recvs[stage][k].astype(F32)
        self.acc[...] = value


def layer_kernel(
    lvars, lsegs, nvars, routers, steps, var_size, seg_size, counts, directs,
    dom_ref, cnt_ref, tok_ref, cot_ref, mean_ref, scale_ref, router_ref, wi0_ref, wi1_ref, wi2_ref, wo_ref, ab_ref,
    win0_ref, win1_ref, bin_ref, wout0_ref, wout1_ref, bout_ref, gain_ref, shift_ref,
    heads_ref, headsf_ref, split_ref, join_ref, mask_ref, grow_ref, shrink_ref, sumr_ref, swap_ref, back_ref,
    out_ref, gin_ref, small_out_ref, inner_ref, outer_ref, up_ref, down_ref, route_ref,
    sent_ref, came_ref, qx_ref, kq_ref, etc_ref, g1_ref, send_sem, recv_sem, out_sem, *scratch,
):
    step = pl.program_id(0)
    me = lax.axis_index("var")
    seg = lax.axis_index("seg")
    width = tok_ref.shape[3]
    rows = lvars * tok_ref.shape[2]
    block = rows // var_size
    kept, scratch = scratch[:11], scratch[11:]
    cores, xs, ys = counts["core"], counts["x"], counts["y"]
    core, xi = lax.rem(seg, cores), lax.div(seg, cores)
    yi, zi = lax.rem(me, ys), lax.div(me, ys)
    axes = {
        "core": (core, cores, lambda i: {"seg": xi * cores + i}),
        "x": (xi, xs, lambda i: {"seg": i * cores + core}),
        "y": (yi, ys, lambda i: {"var": zi * ys + i}),
        "z": (zi, counts["z"], lambda i: {"var": i * ys + yi}),
    }
    sums = []
    for direct in directs:
        used = 7 + 2 * len([name for name in counts if counts[name] > 1])
        group, scratch = scratch[:used], scratch[used:]
        sums.append(Sum(axes, direct, group[0], group[1], group[2], group[7:], group[3:7]))
    routes, feeds, times = sums
    small = SmallSum(scratch[0], scratch[1], scratch[2:4], scratch[4:8], [("seg", seg, seg_size), ("var", me, var_size)])

    def copy(kind, b, k):
        target = lax.rem(me + k, var_size)
        return pltpu.make_async_remote_copy(
            src_ref=sent_ref.at[kind, b, target],
            dst_ref=came_ref.at[kind, b, me],
            send_sem=send_sem.at[kind, b],
            recv_sem=recv_sem.at[kind, b],
            device_id={"var": target},
            device_id_type=MESH,
        )

    def whole(kind, b):
        others = pl.ds(0, var_size - 1)
        return pltpu.make_async_remote_copy(
            src_ref=sent_ref.at[kind, b, others],
            dst_ref=came_ref.at[kind, b, others],
            send_sem=send_sem.at[kind, b],
            recv_sem=recv_sem.at[kind, b],
            device_id={"var": lax.rem(me + 1, var_size)},
            device_id_type=MESH,
        )

    def store(kind, b, value):
        value = value.reshape(var_size, block, width)
        sent_ref[kind, b] = value
        came_ref[kind, b, me] = sent_ref[kind, b, me]

    def send(kind, b):
        for k in range(1, var_size):
            copy(kind, b, k).start()

    def pick(b, ref):
        total = jnp.zeros((1, width), F32)
        for d in range(ref.shape[0]):
            total = total + jnp.where(dom_ref[b] == d, ref[d : d + 1, :], 0.0)
        return total

    def arrived(kind, b):
        whole(kind, b).wait_recv()
        return came_ref[kind, b]

    pieces = [
        (times, T_Q, 3 * width, inner_ref, 0), (routes, B_SQ, 6 * width, inner_ref, 3 * width),
        (times, T_O, width, outer_ref, 0), (routes, B_O1, 2 * width, outer_ref, width),
        (feeds, M_IN, 2 * width, up_ref, 0), (routes, B_IN, 2 * width, up_ref, 2 * width),
        (feeds, M_OUT, 2 * width, down_ref, 0), (routes, B_OUT, 2 * width, down_ref, 2 * width),
        (routes, B_ROUTE, route_ref.shape[0], route_ref, 0),
    ]

    def deliver(which):
        return [
            pltpu.make_async_copy(
                total.total.at[pl.ds(row, count), :], ref.at[pl.ds(there, count), :], out_sem.at[index]
            )
            for index, (total, row, count, ref, there) in enumerate(pieces)
            if total is which
        ]

    @pl.when(step < steps)
    def _():
        b = step

        @pl.when(b == 0)
        def _():
            barrier = pltpu.get_barrier_semaphore()
            for k in range(1, var_size):
                pl.semaphore_signal(barrier, inc=1, device_id={"var": lax.rem(me + k, var_size)}, device_id_type=MESH)
            for k in range(1, seg_size):
                pl.semaphore_signal(barrier, inc=1, device_id={"seg": lax.rem(seg + k, seg_size)}, device_id_type=MESH)
            small.acc[...] = jnp.zeros_like(small.acc)

        store(1, b, mm(split_ref[...], cot_ref[0].reshape(rows, width)).astype(LOW))
        t2 = time_forward(
            lvars, b, tok_ref, pick(b, mean_ref), pick(b, scale_ref), wi0_ref, wo_ref, ab_ref, win0_ref, bin_ref,
            wout0_ref, bout_ref, gain_ref, shift_ref, heads_ref, headsf_ref, kept,
        )
        store(0, b, mm(split_ref[...], t2).astype(LOW))

        @pl.when(b == 0)
        def _():
            pl.semaphore_wait(pltpu.get_barrier_semaphore(), var_size + seg_size - 2)

        send(0, b)
        send(1, b)

    @pl.when((step >= steps) & (step < 2 * steps))
    def _():
        b = step - steps

        def leaving(kind, value):
            store(kind, b, value)
            if kind == 2:
                send(kind, b)

        limit = jnp.int32(0)
        for d in range(cnt_ref.shape[0]):
            limit = limit + jnp.where(dom_ref[b] == d, cnt_ref[d], 0)
        router_part(
            lsegs, nvars, routers, steps, b, lambda kind: arrived(kind, b), leaving,
            limit, router_ref, wi1_ref, wi2_ref, wo_ref, ab_ref, win1_ref, bin_ref, wout1_ref, bout_ref,
            gain_ref, shift_ref, mask_ref, grow_ref, shrink_ref, sumr_ref, swap_ref, back_ref,
            routes.acc, small.acc, qx_ref, kq_ref, B_ROUTE + me * (lsegs * SLOTS),
        )

    @pl.when((step >= 2 * steps) & (step < 3 * steps))
    def _():
        b = step - 2 * steps
        send(3, b)
        feed_backward(
            rows, b, lambda kind: arrived(kind, b), wo_ref, win0_ref, wout0_ref, gain_ref, shift_ref, join_ref, kept,
            feeds.acc, times.acc, small.acc, etc_ref, g1_ref,
        )

    @pl.when((step >= 3 * steps) & (step < 4 * steps))
    def _():
        b = step - 3 * steps
        time_backward(
            lvars, b, tok_ref, pick(b, mean_ref), pick(b, scale_ref), heads_ref, headsf_ref, kept, times.acc, small.acc,
            etc_ref,
        )

    def at(turn_step, run):
        pl.when(step == turn_step)(run)

    for total, first_step, last_step in ((routes, 2 * steps, 4 * steps), (feeds, 3 * steps, 4 * steps)):
        for turn in range(total.turns):
            at(first_step + (last_step - first_step) * turn // (total.turns - 1), functools.partial(total.advance, turn))
    spread = [min(turn * steps // (times.turns - 1), steps - 1) for turn in range(times.turns)]

    @pl.when(step >= 4 * steps)
    def _():
        b = step - 4 * steps

        @pl.when(b == 0)
        def _():
            small.start(0)
            for total in (routes, feeds):
                for copy in deliver(total):
                    copy.start()

        for turn in range(times.turns - 1):
            pl.when(b == spread[turn])(functools.partial(times.advance, turn))

        @pl.when(b == steps // 2)
        def _():
            small.finish(0)
            small.start(1)

        grad = g1_ref[b] + mm_nt(kept[0][b], wi0_ref[0, 0]) + mm_nt(kept[1][b], wi0_ref[0, 1])
        grad = (grad + mm_nt(kept[2][b], wi0_ref[0, 2])) * pick(b, scale_ref)
        gin_ref[0] = grad.reshape(gin_ref.shape[1:])

    @pl.when(step == 5 * steps - 1)
    def _():
        small.finish(1)
        small_out_ref[...] = small.acc[...]
        for b in range(steps):
            whole(3, b).wait_recv()
            for kind in range(4):
                whole(kind, b).wait_send()
        out_ref[...] = came_ref[3]
        times.advance(times.turns - 1)
        for copy in deliver(times):
            copy.start()
        for total in sums:
            for copy in deliver(total):
                copy.wait()


def finish_kernel(
    width, segs, lvars, out_ref, inner_ref, outer_ref, up_ref, down_ref, route_ref, join_ref,
    output_ref, ginner_ref, gouter_ref, gup_ref, gdown_ref, groute_ref,
):
    routers = groute_ref.shape[1]
    output_ref[0] = mm(join_ref[...], out_ref[0].reshape(lvars * segs, width)).reshape(lvars, segs, width)
    ginner_ref[...] = inner_ref[...].astype(F32)
    gouter_ref[...] = outer_ref[...].astype(F32)
    gup_ref[0, :, :width] = up_ref[0, 0].astype(F32)
    gup_ref[0, :, width:] = up_ref[0, 1].astype(F32)
    gdown_ref[...] = down_ref[...].astype(F32)
    groute_ref[...] = route_ref[...].astype(F32)[:, :routers, :]


def fixed(shape, index=None):
    index = (0,) * len(shape) if index is None else index
    return pl.BlockSpec(shape, lambda b: index)


def on_device(
    var_size, seg_size,
    tokens, domain, counts, domain_mean, domain_scale, attn_inner, attn_outer, attn_bias,
    mlp_in, mlp_in_bias, mlp_out, mlp_out_bias, norm_gain, norm_bias, router, cotangent,
):
    batch, lvars, segs, width = tokens.shape
    routers = router.shape[1]
    hidden = mlp_in.shape[2]
    lsegs = segs // var_size
    nvars = lvars * var_size
    rows = lvars * segs
    lanes = SLOTS * HEADS
    me = lax.axis_index("var")

    heads = (np.arange(width)[None, :] // (width // HEADS) == np.arange(HEADS)[:, None]).astype(np.float32)
    heads_low = jnp.asarray(heads, LOW)
    heads_f = jnp.asarray(heads, F32)
    mask = jnp.asarray(np.concatenate([heads, heads], axis=0), LOW)
    order = np.arange(rows).reshape(lvars, var_size, lsegs).transpose(1, 0, 2).reshape(-1)
    split = np.eye(rows, dtype=np.float32)[order]
    order = np.arange(rows).reshape(nvars, lsegs).transpose(1, 0).reshape(-1)
    swap = np.eye(rows, dtype=np.float32)[order]
    group = np.arange(lsegs * lanes) // HEADS
    grow = (group[:, None] == np.arange(lsegs * SLOTS)[None, :]).astype(np.float32)
    sumr = (np.arange(lanes)[:, None] % HEADS == np.arange(lanes)[None, :] % HEADS).astype(np.float32)

    kept = [
        ((rows, width), LOW), ((rows, width), LOW), ((rows, width), LOW), ((rows, HEADS * segs), LOW),
        ((rows, width), LOW), ((rows, width), LOW), ((rows, 128), F32), ((rows, hidden), LOW),
        ((rows, hidden), LOW), ((rows, width), LOW), ((rows, 128), F32),
    ]
    mine = lax.dynamic_slice_in_dim(router, me * lsegs, lsegs, 0)
    mine = jnp.pad(mine, ((0, 0), (0, SLOTS - routers), (0, 0))).reshape(lsegs * SLOTS, width)
    inner = [fixed((1,) + attn_inner.shape[1:], (i, 0, 0, 0)) for i in range(3)]
    up0, up1 = [fixed((1,) + mlp_in.shape[1:], (i, 0, 0)) for i in range(2)]
    down0, down1 = [fixed((1,) + mlp_out.shape[1:], (i, 0, 0)) for i in range(2)]
    consts = [jnp.asarray(x, LOW) for x in (split, split.T)] + [mask]
    consts += [jnp.asarray(x, LOW) for x in (grow, grow.T, sumr, swap, swap.T)]

    def first_third(i):
        return jnp.where(i < batch, i, jnp.clip(i - 3 * batch, 0, batch - 1))

    def first(i):
        return jnp.minimum(i, batch - 1)

    def last(i):
        return jnp.clip(i - 4 * batch, 0, batch - 1)

    cores = 2 if seg_size % 2 == 0 else 1
    xs = seg_size // cores
    ys = xs if var_size % xs == 0 else 1
    sizes = {"core": cores, "x": xs, "y": ys, "z": var_size // ys}
    directs = [var_size * seg_size > 32] * 3
    quantum = 32 * var_size * seg_size
    sum_rows = []
    for count, direct in zip((B_ROUTE + segs * SLOTS, M_ROWS, T_ROWS), directs):
        unit = quantum // sizes["z"] if direct else quantum
        sum_rows.append(-(-count // unit) * unit)
    whole = lambda x: fixed(x.shape)
    scalars = pl.BlockSpec(memory_space=pltpu.SMEM)
    anywhere = pl.BlockSpec(memory_space=pl.ANY)
    block = (1, lvars, segs, width)
    out_shapes = [
        jax.ShapeDtypeStruct((batch, var_size, rows // var_size, width), LOW),
        jax.ShapeDtypeStruct(tokens.shape, F32),
        jax.ShapeDtypeStruct((S_ROWS, width), F32),
        jax.ShapeDtypeStruct((9 * width, width), LOW),
        jax.ShapeDtypeStruct((3 * width, width), LOW),
        jax.ShapeDtypeStruct((4 * width, width), LOW),
        jax.ShapeDtypeStruct((2 * hidden, width), LOW),
        jax.ShapeDtypeStruct((segs * SLOTS, width), LOW),
    ]
    arrived, input_grad, small, inner_low, outer_low, up_low, down_low, route_low = pl.pallas_call(
        functools.partial(layer_kernel, lvars, lsegs, nvars, routers, batch, var_size, seg_size, sizes, directs),
        grid=(5 * batch,),
        in_specs=[
            scalars, scalars,
            pl.BlockSpec(block, lambda i: (first_third(i), 0, 0, 0)),
            pl.BlockSpec(block, lambda i: (first(i), 0, 0, 0)),
            whole(domain_mean), whole(domain_scale), whole(mine), *inner, whole(attn_outer), whole(attn_bias),
            up0, up1, whole(mlp_in_bias), down0, down1, whole(mlp_out_bias), whole(norm_gain), whole(norm_bias),
            whole(heads_low), whole(heads_f),
        ]
        + [whole(c) for c in consts],
        out_specs=[
            whole(out_shapes[0]),
            pl.BlockSpec(block, lambda i: (last(i), 0, 0, 0)),
            whole(out_shapes[2]),
            *[anywhere] * 5,
        ],
        out_shape=out_shapes,
        scratch_shapes=[
            pltpu.VMEM((4, batch, var_size, rows // var_size, width), LOW),
            pltpu.VMEM((4, batch, var_size, rows // var_size, width), LOW),
            pltpu.VMEM((lsegs * lanes, width), LOW),
            pltpu.VMEM((lsegs * lanes, width), F32),
            pltpu.VMEM((batch, rows, width), LOW),
            pltpu.VMEM((batch, rows, width), F32),
            pltpu.SemaphoreType.DMA((4, batch)),
            pltpu.SemaphoreType.DMA((4, batch)),
            pltpu.SemaphoreType.DMA((9,)),
            *[pltpu.VMEM((batch,) + shape, dtype) for shape, dtype in kept],
            *[x for count, direct in zip(sum_rows, directs) for x in Sum.scratch(count, width, sizes, direct)],
            *SmallSum.scratch(S_ROWS, width, (seg_size, var_size)),
        ],
        compiler_params=pltpu.CompilerParams(
            dimension_semantics=("arbitrary",), vmem_limit_bytes=VMEM_LIMIT, collective_id=0, has_side_effects=True
        ),
        name="layer",
    )(
        domain, counts, tokens, cotangent, domain_mean, domain_scale, mine, attn_inner, attn_inner, attn_inner,
        attn_outer, attn_bias, mlp_in, mlp_in, mlp_in_bias, mlp_out, mlp_out, mlp_out_bias, norm_gain, norm_bias,
        heads_low, heads_f, *consts,
    )

    def shares(*shape):
        shape = (shape[0] // batch,) + shape[1:]
        return pl.BlockSpec(shape, lambda i: (i,) + (0,) * (len(shape) - 1))

    quarter = width * 2 // batch
    per = batch // 2
    output, grad_inner, grad_outer, grad_up, grad_down, grad_router = pl.pallas_call(
        functools.partial(finish_kernel, width, segs, lvars),
        grid=(batch,),
        in_specs=[
            shares(batch, var_size, rows // var_size, width),
            shares(*inner_low.shape), shares(*outer_low.shape),
            pl.BlockSpec((1, 2, quarter, width), lambda i: (i // per, 0, i % per, 0)),
            shares(*down_low.shape), shares(segs, SLOTS, width), whole(consts[1]),
        ],
        out_specs=[
            pl.BlockSpec(block, lambda i: (i, 0, 0, 0)),
            shares(*inner_low.shape), shares(*outer_low.shape),
            pl.BlockSpec((1, quarter, hidden), lambda i: (i // per, i % per, 0)),
            shares(*down_low.shape), shares(*router.shape),
        ],
        out_shape=[
            jax.ShapeDtypeStruct(tokens.shape, F32),
            jax.ShapeDtypeStruct(inner_low.shape, F32),
            jax.ShapeDtypeStruct(outer_low.shape, F32),
            jax.ShapeDtypeStruct(mlp_in.shape, F32),
            jax.ShapeDtypeStruct(down_low.shape, F32),
            jax.ShapeDtypeStruct(router.shape, F32),
        ],
        compiler_params=pltpu.CompilerParams(dimension_semantics=("arbitrary",), vmem_limit_bytes=VMEM_LIMIT),
        name="finish",
    )(
        arrived, inner_low, outer_low, up_low.reshape(2, 2, width, width), down_low,
        route_low.reshape(segs, SLOTS, width), consts[1],
    )
    return (
        output, input_grad, grad_inner.reshape(attn_inner.shape), grad_outer.reshape(attn_outer.shape),
        small[S_BIAS : S_BIAS + 9].reshape(attn_bias.shape), grad_up, small[S_IN : S_IN + 4].reshape(mlp_in_bias.shape),
        grad_down.reshape(mlp_out.shape), small[S_OUT : S_OUT + 2], small[S_GAIN : S_GAIN + 4],
        small[S_SHIFT : S_SHIFT + 4], grad_router,
    )


def solution(mesh):
    split = P("seg", "var", None, None)
    in_specs = (split, P("seg")) + (P(),) * 13 + (split,)
    out_specs = (split, split) + (P(),) * 10
    var_size, seg_size = mesh.shape["var"], mesh.shape["seg"]
    return jax.shard_map(
        functools.partial(on_device, var_size, seg_size),
        mesh=mesh, in_specs=in_specs, out_specs=out_specs, check_vma=False,
    )
```

time: 214 us -> 194 us (0.907)
  other arithmetic: 17 us -> 0 us
  local copies, waits for them, and re-layouts: 16.1 us -> 9.98 us
    pallas_call x1, Pallas kernels: 113 us -> 172 us  [on_device(): pl.pallas_call(functools.partial(layer_kernel, lvars, lsegs, nvars, route...]
    pallas_call x1, Pallas kernels: 65.1 us -> 8.41 us  [on_device(): pl.pallas_call(functools.partial(finish_kernel, width, segs, lvars), grid...]
    concatenate x5 -> x0, other arithmetic: 7.4 us -> none  [the longest x1 4.3 us: on_device(): jnp.concatenate([grads_b, grads_c, routes], axis=0)]
    convert_element_type x3 -> x0, other arithmetic: 3.89 us -> none  [the longest x1 2.3 us: on_device(): all_reduce(jnp.concatenate([grads_b, grads_c, routes], axis=0), var_size,...]
    another operation x5 -> x0, other arithmetic: 3.47 us -> none  [the longest x2 1.19 us: on_device(): grad_up = jnp.stack([up(gc[C_IN:]), up(gb[B_IN:])])]
    slice x10 -> x3, local copies, waits for them, and re-layouts: 5.12 us -> 3.37 us  [the longest x1 1.37 us: on_device(): small[S_SHIFT:S_SHIFT + 4]]
    unnamed x19 -> x7, local copies, waits for them, and re-layouts: 5.22 us -> 4.75 us
where the time goes in v3:
time: 194 us; the launch traced here: 191 us
  Pallas kernels  180 us (93%)
  local copies, waits for them, and re-layouts  9.98 us (5%)
    pallas_call x1, Pallas kernels, on_device(): pl.pallas_call(functools.partial(layer_kernel, lvars, lsegs, nvars, route...  172 us
    pallas_call x1, Pallas kernels, on_device(): pl.pallas_call(functools.partial(finish_kernel, width, segs, lvars), grid...  8.41 us
    unnamed x7, local copies, waits for them, and re-layouts  4.75 us

profile of v3, /device:TPU:29, one launch (start us, length us, event | category | flops | bytes accessed | tf_op | source)
XLA Modules:
  0.0 190.8 jit_solution(5788981254262328619)
XLA Ops:
  0.6 0.0 copy-start
  0.7 1.0 copy-done
  1.6 0.6 pad.4.clone
  2.3 171.7 %layer.1 = (bf16[8,8,32,256]{3,2,1,0:T(8,128)(2,1)}, f32[8,4,64,256]{3,2,1,0:T(8,128)}, f32[32,256]{1,0:T(8,128)}, bf16[2304,256]{1,0:T(8,128)(2,1)}, bf16[768,2...) custom-call(s32[8]{0:T(128)} %dom_ref.1, s32[4]{0:T(128)} %cnt_ref.1, ...), custom_call_target="tpu_custom_call" | custom-call | tf_op jit(solution)/shard_map/layer/pallas_call | solution.py:780
  174.0 1.3 slice.17
  175.3 1.4 fusion
  176.7 0.7 slice.15
  177.4 0.6 reshape.53
  178.0 0.6 reshape.54
  178.6 0.0 copy-start.1
  178.6 8.4 %finish.1 = (f32[8,4,64,256]{3,2,1,0:T(8,128)}, f32[2304,256]{1,0:T(8,128)}, f32[768,256]{1,0:T(8,128)}, f32[2,256,512]{2,1,0:T(8,128)}, f32[1024,256]{1,0:T(8,128)}, /*index=5*/f32[64,10,256]{2,1,0:T(8,128)}) custom-call(bf16[8,8,32,256]{3,2,1,0:T(8,128)(2,1)} %get-tuple-element.26.out_ref, bf16[2304,256]{1,0:T(8,128)(2,1)} %get-tuple-element.27.inner_ref, ...), custom_call_target="tpu_custom_call" | custom-call | tf_op jit(solution)/shard_map/finish/pallas_call | solution.py:829
  187.0 2.4 %copy.39 = f32[64,10,256]{2,0,1:T(8,128)} copy(f32[64,10,256]{2,1,0:T(8,128)} %get-tuple-element.51) | data formatting | bytes 1310720
  189.5 0.0 copy-done.1
  189.5 1.3 copy.42
  (2 shorter events, 0.0 us)
Async XLA Ops:
  0.6 1.0 copy-start
  178.6 10.9 %copy-start.1 = (f32[8,4,64,256]{3,2,1,0:T(8,128)S(1)}, f32[8,4,64,256]{3,2,1,0:T(8,128)}, u32[]{:S(2)}) copy-start(f32[8,4,64,256]{3,2,1,0:T(8,128)} %get-tuple-element.68) | copy-start | bytes 6291460

commit v4 on v3

v4 whole, which is shorter than its diff:
```python
import functools

import jax
import jax.numpy as jnp
import numpy as np
from jax import lax
from jax.experimental import pallas as pl
from jax.experimental.pallas import tpu as pltpu
from jax.sharding import PartitionSpec as P

HEADS = 8
SLOTS = 16
EPS = 1e-05
MASKED = -1e30
MESH = pl.DeviceIdType.MESH
F32 = jnp.float32
LOW = jnp.bfloat16
VMEM_LIMIT = 60 * 1024 * 1024


OUT_ROUNDS = (-7, -6, -5, -4, -3, -2, -1, 0)
ATTN_ROUNDS = (0, 2, 9, 14, 17, 19, 21)
ROUTE_ROUNDS = (1, 3, 12, 16, 18, 20, 22)
FEED_ROUNDS = (9, 11, 16, 18, 20, 22, 24)
TIME_ROUNDS = (16, 17, 19, 22, 23)


def mm(a, b):
    return jnp.dot(a, b, preferred_element_type=F32)


def mm_nt(a, b):
    return lax.dot_general(a, b, (((1,), (1,)), ((), ())), preferred_element_type=F32)


def mm_tn(a, b):
    return lax.dot_general(a, b, (((0,), (0,)), ((), ())), preferred_element_type=F32)


def ln_stats(a):
    mean = jnp.mean(a, axis=1, keepdims=True)
    center = a - mean
    var = jnp.mean(center * center, axis=1, keepdims=True)
    rstd = lax.rsqrt(var + EPS)
    return center * rstd, rstd


def ln_back(g, xhat, rstd, gain):
    gy = g * gain
    first = jnp.mean(gy, axis=1, keepdims=True)
    second = jnp.mean(gy * xhat, axis=1, keepdims=True)
    return rstd * (gy - first - xhat * second)


def gelu_both(z):
    k0 = np.float32(np.sqrt(2.0 / np.pi))
    k1 = np.float32(0.044715)
    square = z * z
    t = jnp.tanh(k0 * z * (1.0 + k1 * square))
    half = 0.5 * (1.0 + t)
    slope = half + 0.5 * z * (1.0 - t * t) * (k0 * (1.0 + 3.0 * k1 * square))
    return z * half, slope


def col_sum(x):
    return jnp.sum(x.astype(F32), axis=0, keepdims=True)


def spread_heads(x, heads_ref):
    return jnp.concatenate([x * heads_ref[h : h + 1, :] for h in range(HEADS)], axis=0)


def gather_heads(x, headsf_ref, rows):
    total = x[:rows] * headsf_ref[0:1, :]
    for h in range(1, HEADS):
        total = total + x[h * rows : (h + 1) * rows] * headsf_ref[h : h + 1, :]
    return total


def time_forward(
    lvars, b, tok_ref, offset, factor, wi_ref, wo_ref, ab_ref, win_ref, bin_ref, wout_ref, bout_ref,
    gain_ref, shift_ref, heads_ref, headsf_ref, kept,
):
    q_ref, k_ref, v_ref, p_ref, tc_ref, x1_ref, r1_ref, f1_ref, s1_ref, x2_ref, r2_ref = kept
    segs, width = tok_ref.shape[2:]
    rows = lvars * segs
    scale = np.float32((width // HEADS) ** (-0.5))
    tok = tok_ref[b].reshape(rows, width).astype(F32)
    start = (tok - offset) * factor
    low = start.astype(LOW)
    q_ref[b] = (mm(low, wi_ref[0, 0]) + ab_ref[0, 0:1, :]).astype(LOW)
    k_ref[b] = mm(low, wi_ref[0, 1]).astype(LOW)
    v_ref[b] = (mm(low, wi_ref[0, 2]) + ab_ref[0, 1:2, :]).astype(LOW)
    for v in range(lvars):
        part = slice(v * segs, (v + 1) * segs)
        spread = spread_heads(q_ref[b, part, :], heads_ref)
        scores = mm_nt(k_ref[b, part, :], spread)
        top = jnp.max(scores, axis=0, keepdims=True)
        expo = jnp.exp((scores - top) * scale)
        prob = (expo / jnp.sum(expo, axis=0, keepdims=True)).astype(LOW)
        p_ref[b, part, :] = prob
        tc_ref[b, part, :] = gather_heads(mm_tn(prob, v_ref[b, part, :]), headsf_ref, segs).astype(LOW)
    a1 = start + mm(tc_ref[b], wo_ref[0]) + ab_ref[0, 2:3, :]
    x1, r1 = ln_stats(a1)
    x1_ref[b] = x1.astype(LOW)
    r1_ref[b] = jnp.broadcast_to(r1, (rows, 128))
    t1 = x1 * gain_ref[0:1, :] + shift_ref[0:1, :]
    act, slope = gelu_both(mm(t1.astype(LOW), win_ref[0]) + bin_ref[0:1, :])
    f1_ref[b] = act.astype(LOW)
    s1_ref[b] = slope.astype(LOW)
    a2 = t1 + mm(f1_ref[b], wout_ref[0]) + bout_ref[0:1, :]
    x2, r2 = ln_stats(a2)
    x2_ref[b] = x2.astype(LOW)
    r2_ref[b] = jnp.broadcast_to(r2, (rows, 128))
    return (x2 * gain_ref[1:2, :] + shift_ref[1:2, :]).astype(LOW)


B_SQ, B_SK, B_SV, B_RQ, B_RK, B_RV, B_O1, B_O2, B_ROWS = [256 * i for i in range(9)]
R_IN, R_OUT, R_ROUTE = [256 * i for i in (0, 2, 4)]
M_IN, M_OUT, M_V, M_O, M_ROWS = [256 * i for i in (0, 2, 4, 5, 6)]
T_Q, T_K, T_ROWS = [256 * i for i in (0, 1, 2)]
S_BIAS, S_IN, S_OUT, S_GAIN, S_SHIFT, S_ROWS = 0, 9, 13, 15, 19, 32


def router_part(
    lsegs, nvars, routers, steps, b, arrived, leaving,
    limit, router_ref, wi_ref, wo_ref, ab_ref, win_ref, bin_ref, wout_ref, bout_ref,
    gain_ref, shift_ref, mask_ref, grow_ref, shrink_ref, sumr_ref, perm_ref, back_ref,
    attn_ref, rest_ref, small_ref, qx_ref, kq_ref, first_seg, var_size,
):
    rows, width = perm_ref.shape[0], wo_ref.shape[1]
    lanes = SLOTS * HEADS
    scale = np.float32((width // HEADS) ** (-0.5))

    def expand(x):
        return (mm(grow_ref[...], x).astype(LOW).reshape(-1, 16, width) * mask_ref[...][None]).reshape(-1, width)

    def contract(x):
        return mm(shrink_ref[...], (x.astype(LOW).reshape(-1, 16, width) * mask_ref[...][None]).reshape(-1, width))

    @pl.when(b == 0)
    def _():
        attn_ref[...] = jnp.zeros(attn_ref.shape, F32)
        rest_ref[...] = jnp.zeros(rest_ref.shape, F32)
        kq_ref[...] = jnp.zeros_like(kq_ref)
        sq = (mm(router_ref[...], wi_ref[1, 0]) + ab_ref[1, 0:1, :]).astype(LOW)
        qx_ref[...] = expand(sq)

    def per_segment(f):
        return [f(slice(s * nvars, (s + 1) * nvars), slice(s * lanes, (s + 1) * lanes)) for s in range(lsegs)]

    t2 = mm(perm_ref[...], arrived(0).reshape(rows, width)).astype(LOW)
    sk = mm(t2, wi_ref[1, 1]).astype(LOW)
    sv = (mm(t2, wi_ref[1, 2]) + ab_ref[1, 1:2, :]).astype(LOW)
    rq = (mm(t2, wi_ref[2, 0]) + ab_ref[2, 0:1, :]).astype(LOW)
    valid = lax.broadcasted_iota(jnp.int32, (nvars, lanes), 0).astype(F32) < limit

    def send_prob(n, l):
        scores = jnp.where(valid, mm_nt(sk[n], qx_ref[l, :]), MASKED)
        top = jnp.max(scores, axis=0, keepdims=True)
        expo = jnp.where(valid, jnp.exp((scores - top) * scale), 0.0)
        return expo / jnp.sum(expo, axis=0, keepdims=True)

    sp = per_segment(send_prob)
    sp_low = [x.astype(LOW) for x in sp]
    pre = contract(jnp.concatenate([mm_tn(sp_low[s], sv[s * nvars : (s + 1) * nvars]) for s in range(lsegs)], axis=0))
    pre_low = pre.astype(LOW)
    buffer = (mm(pre_low, wo_ref[1]) + ab_ref[1, 2:3, :]).astype(LOW)
    rkx = expand(mm(buffer, wi_ref[2, 1]).astype(LOW))
    rvx = expand((mm(buffer, wi_ref[2, 2]) + ab_ref[2, 1:2, :]).astype(LOW))
    scores = jnp.concatenate(per_segment(lambda n, l: mm_nt(rq[n], rkx[l])), axis=0)
    real = lax.broadcasted_iota(jnp.int32, (rows, lanes), 1) < routers * HEADS
    scores = jnp.where(real, scores, MASKED)
    top = scores
    shift = lanes // 2
    while shift >= HEADS:
        top = jnp.maximum(top, pltpu.roll(top, shift, 1))
        shift //= 2
    expo = jnp.where(real, jnp.exp((scores - top) * scale), 0.0)
    rp = expo / mm(expo.astype(LOW), sumr_ref[...])
    rp_low = rp.astype(LOW)
    rc = jnp.concatenate(per_segment(lambda n, l: mm(rp_low[n], rvx[l])), axis=0).astype(LOW)
    a3 = t2.astype(F32) + mm(rc, wo_ref[2]) + ab_ref[2, 2:3, :]
    x3, r3 = ln_stats(a3)
    t3 = x3 * gain_ref[2:3, :] + shift_ref[2:3, :]
    t3_low = t3.astype(LOW)
    act, slope = gelu_both(mm(t3_low, win_ref[1]) + bin_ref[1:2, :])
    f2 = act.astype(LOW)
    a4 = t3 + mm(f2, wout_ref[1]) + bout_ref[1:2, :]
    x4, r4 = ln_stats(a4)
    out = (x4 * gain_ref[3:4, :] + shift_ref[3:4, :]).astype(LOW)
    leaving(3, mm(back_ref[...], out).astype(LOW))

    def add(row, value, ref=attn_ref):
        ref[row : row + value.shape[0], :] += value

    def add_small(row, value):
        small_ref[row : row + 1, :] += value

    cot = mm(perm_ref[...], arrived(1).reshape(rows, width))
    add_small(S_GAIN + 3, col_sum(cot * x4))
    add_small(S_SHIFT + 3, col_sum(cot))
    g4 = ln_back(cot, x4, r4, gain_ref[3:4, :])
    e4 = g4.astype(LOW)
    add(R_OUT, mm_tn(f2, e4), rest_ref)
    add_small(S_OUT + 1, col_sum(e4))
    e3 = (slope * mm_nt(e4, wout_ref[1])).astype(LOW)
    add(R_IN, mm_tn(t3_low, e3[:, :width]), rest_ref)
    add(R_IN + width, mm_tn(t3_low, e3[:, width:]), rest_ref)
    e3_sum = col_sum(e3)
    add_small(S_IN + 2, e3_sum[:, :width])
    add_small(S_IN + 3, e3_sum[:, width:])
    g3 = g4 + mm_nt(e3, win_ref[1])
    add_small(S_GAIN + 2, col_sum(g3 * x3))
    add_small(S_SHIFT + 2, col_sum(g3))
    g3 = ln_back(g3, x3, r3, gain_ref[2:3, :])
    eo = g3.astype(LOW)
    add(B_O2, mm_tn(rc, eo))
    add_small(S_BIAS + 8, col_sum(eo))
    ec = mm_nt(eo, wo_ref[2]).astype(LOW)
    dp = jnp.concatenate(per_segment(lambda n, l: mm_nt(ec[n], rvx[l])), axis=0)
    ds = (scale * rp * (dp - mm((rp * dp).astype(LOW), sumr_ref[...]))).astype(LOW)
    erq = jnp.concatenate(per_segment(lambda n, l: mm(ds[n], rkx[l])), axis=0).astype(LOW)
    erk = contract(jnp.concatenate(per_segment(lambda n, l: mm_tn(ds[n], rq[n])), axis=0)).astype(LOW)
    erv = contract(jnp.concatenate(per_segment(lambda n, l: mm_tn(rp_low[n], ec[n])), axis=0)).astype(LOW)
    add(B_RQ, mm_tn(t2, erq))
    add_small(S_BIAS + 6, col_sum(erq))
    add(B_RK, mm_tn(buffer, erk))
    add(B_RV, mm_tn(buffer, erv))
    add_small(S_BIAS + 7, col_sum(erv))
    eb = (mm_nt(erk, wi_ref[2, 1]) + mm_nt(erv, wi_ref[2, 2])).astype(LOW)
    add(B_O1, mm_tn(pre_low, eb))
    add_small(S_BIAS + 5, col_sum(eb))
    epx = expand(mm_nt(eb, wo_ref[1]).astype(LOW))
    dss = []
    for s in range(lsegs):
        dps = mm_nt(sv[s * nvars : (s + 1) * nvars], epx[s * lanes : (s + 1) * lanes])
        weighted = sp[s] * dps
        center = jnp.sum(weighted, axis=0, keepdims=True)
        dss.append((scale * (weighted - sp[s] * center)).astype(LOW))
    esv = jnp.concatenate([mm(sp_low[s], epx[s * lanes : (s + 1) * lanes]) for s in range(lsegs)], axis=0).astype(LOW)
    esk = jnp.concatenate([mm(dss[s], qx_ref[s * lanes : (s + 1) * lanes, :]) for s in range(lsegs)], axis=0).astype(LOW)
    for s in range(lsegs):
        kq_ref[s * lanes : (s + 1) * lanes, :] += mm_tn(dss[s], sk[s * nvars : (s + 1) * nvars])
    add(B_SK, mm_tn(t2, esk))
    add(B_SV, mm_tn(t2, esv))
    add_small(S_BIAS + 4, col_sum(esv))
    g2 = g3 + mm_nt(erq, wi_ref[2, 0]) + mm_nt(esk, wi_ref[1, 1]) + mm_nt(esv, wi_ref[1, 2])
    leaving(2, mm(back_ref[...], g2.astype(LOW)).astype(LOW))

    @pl.when(b == steps - 1)
    def _():
        kq = contract(kq_ref[...])
        kq_low = kq.astype(LOW)
        attn_ref[B_SQ : B_SQ + width, :] = mm_tn(router_ref[...], kq_low)
        add_small(S_BIAS + 3, col_sum(kq))
        places = routers * lsegs * var_size
        there = lax.broadcasted_iota(jnp.int32, (places, lsegs * SLOTS), 0)
        here = lax.broadcasted_iota(jnp.int32, (places, lsegs * SLOTS), 1)
        here = lax.div(here, lsegs) * (lsegs * var_size) + lax.rem(here, lsegs) + first_seg
        here = jnp.where(there == here, 1.0, 0.0).astype(LOW)
        rest_ref[R_ROUTE : R_ROUTE + places, :] = mm(here, mm_nt(kq_low, wi_ref[1, 0]).astype(LOW))


def feed_backward(
    lvars, b, arrived, tok_ref, offset, factor, wo_ref, win_ref, wout_ref, gain_ref, shift_ref, heads_ref, perm_ref, kept,
    feeds_ref, small_ref, etc_ref, g1_ref,
):

    q_ref, k_ref, v_ref, p_ref, tc_ref, x1_ref, r1_ref, f1_ref, s1_ref, x2_ref, r2_ref = kept
    segs, width = tok_ref.shape[2:]
    rows = lvars * segs

    @pl.when(b == 0)
    def _():
        feeds_ref[...] = jnp.zeros(feeds_ref.shape, F32)

    def add(ref, row, value):
        ref[row : row + value.shape[0], :] += value

    def wide(ref):
        return jnp.concatenate([ref[b]] * (width // 128), axis=1)

    g2 = mm(perm_ref[...], arrived(2).reshape(rows, width))
    x2 = x2_ref[b].astype(F32)
    add(small_ref, S_GAIN + 1, col_sum(g2 * x2))
    add(small_ref, S_SHIFT + 1, col_sum(g2))
    g2 = ln_back(g2, x2, wide(r2_ref), gain_ref[1:2, :])
    e2 = g2.astype(LOW)
    add(feeds_ref, M_OUT, mm_tn(f1_ref[b], e2))
    add(small_ref, S_OUT, col_sum(e2))
    e1 = (s1_ref[b].astype(F32) * mm_nt(e2, wout_ref[0])).astype(LOW)
    x1 = x1_ref[b].astype(F32)
    t1 = (x1 * gain_ref[0:1, :] + shift_ref[0:1, :]).astype(LOW)
    add(feeds_ref, M_IN, mm_tn(t1, e1[:, :width]))
    add(feeds_ref, M_IN + width, mm_tn(t1, e1[:, width:]))
    e1_sum = col_sum(e1)
    add(small_ref, S_IN, e1_sum[:, :width])
    add(small_ref, S_IN + 1, e1_sum[:, width:])
    g1 = g2 + mm_nt(e1, win_ref[0])
    add(small_ref, S_GAIN, col_sum(g1 * x1))
    add(small_ref, S_SHIFT, col_sum(g1))
    g1 = ln_back(g1, x1, wide(r1_ref), gain_ref[0:1, :])
    g1_ref[b] = g1
    et = g1.astype(LOW)
    add(feeds_ref, M_O, mm_tn(tc_ref[b], et))
    add(small_ref, S_BIAS + 2, col_sum(et))
    etc_ref[b] = mm_nt(et, wo_ref[0]).astype(LOW)
    for v in range(lvars):
        part = slice(v * segs, (v + 1) * segs)
        tc_ref[b, part, :] = mm(p_ref[b, part, :], spread_heads(etc_ref[b, part, :], heads_ref)).astype(LOW)
    low = ((tok_ref[b].reshape(rows, width).astype(F32) - offset) * factor).astype(LOW)
    add(feeds_ref, M_V, mm_tn(low, tc_ref[b]))
    add(small_ref, S_BIAS + 1, col_sum(tc_ref[b]))


def time_backward(lvars, b, tok_ref, offset, factor, heads_ref, headsf_ref, kept, times_ref, small_ref, etc_ref):
    q_ref, k_ref, v_ref, p_ref = kept[:4]
    segs, width = tok_ref.shape[2:]
    rows = lvars * segs
    scale = np.float32((width // HEADS) ** (-0.5))

    @pl.when(b == 0)
    def _():
        times_ref[...] = jnp.zeros(times_ref.shape, F32)

    def add(ref, row, value):
        ref[row : row + value.shape[0], :] += value

    for v in range(lvars):
        part = slice(v * segs, (v + 1) * segs)
        ex = spread_heads(etc_ref[b, part, :], heads_ref)
        prob = p_ref[b, part, :].astype(F32)
        weighted = prob * mm_nt(v_ref[b, part, :], ex)
        ets = (weighted - prob * jnp.sum(weighted, axis=0, keepdims=True)).astype(LOW)
        gk = (scale * mm(ets, spread_heads(q_ref[b, part, :], heads_ref))).astype(LOW)
        q_ref[b, part, :] = (scale * gather_heads(mm_tn(ets, k_ref[b, part, :]), headsf_ref, segs)).astype(LOW)
        k_ref[b, part, :] = gk
    low = ((tok_ref[b].reshape(rows, width).astype(F32) - offset) * factor).astype(LOW)
    add(times_ref, T_Q, mm_tn(low, q_ref[b]))
    add(times_ref, T_K, mm_tn(low, k_ref[b]))
    add(small_ref, S_BIAS, col_sum(q_ref[b]))


class Sum:
    def __init__(self, axes, acc, send, total, recv, sems):
        self.acc, self.send, self.total, self.recv, self.sems = acc, send, total, recv, sems
        self.plan = []
        start, size = 0, acc.shape[0]
        for index, count, target in axes:
            size //= count
            self.plan.append((index, count, target, start, size))
            start = start + index * size
        self.levels = len(self.plan)
        self.last = 2 * self.levels

    @staticmethod
    def scratch(rows, width, counts):
        recv, size = [], rows
        for count in counts:
            size //= count
            recv.append(pltpu.VMEM((count - 1, size, width), LOW))
        copies = sum(counts) - len(counts)
        return [
            pltpu.VMEM((rows, width), F32), pltpu.VMEM((rows, width), LOW), pltpu.VMEM((rows, width), LOW),
            *[pltpu.SemaphoreType.DMA((copies,))] * 4, *recv,
        ]

    def rows(self, start, size):
        return pl.ds(start if isinstance(start, int) else pl.multiple_of(start, 16), size)

    def copies(self, level, gather):
        send_sem, recv_sem = self.sems[2:] if gather else self.sems[:2]
        index, count, target, start, size = self.plan[level]
        first = sum(entry[1] - 1 for entry in self.plan[:level])
        found = []
        for k in range(1, count):
            peer = lax.rem(index + k, count)
            rows = self.rows(start + (index if gather else peer) * size, size)
            copy = pltpu.make_async_remote_copy(
                src_ref=(self.total if gather else self.send).at[rows, :],
                dst_ref=self.total.at[rows, :] if gather else self.recv[level].at[k - 1],
                send_sem=send_sem.at[first + k - 1],
                recv_sem=recv_sem.at[first + k - 1],
                device_id=target(peer),
                device_id_type=MESH,
            )
            found.append((copy, rows))
        return found

    def advance(self, turn):
        levels = self.levels
        if 0 < turn <= levels:
            for copy, _ in self.copies(turn - 1, False):
                copy.wait()
            index, count, _, start, size = self.plan[turn - 1]
            mine = self.rows(start + index * size, size)
            value = self.acc[mine, :]
            for k in range(count - 1):
                value = value + self.recv[turn - 1][k].astype(F32)
            if turn < levels:
                self.acc[mine, :] = value
            else:
                self.total[mine, :] = value.astype(LOW)
        elif turn > levels:
            for copy, _ in self.copies(self.last - turn, True):
                copy.wait()
        if turn < levels:
            for copy, rows in self.copies(turn, False):
                self.send[rows, :] = self.acc[rows, :].astype(LOW)
                copy.start()
        elif turn < self.last:
            for copy, _ in self.copies(self.last - 1 - turn, True):
                copy.start()

    @property
    def turns(self):
        return self.last + 1


class SmallSum:
    def __init__(self, acc, sent, recvs, sems, places):
        self.acc, self.sent, self.recvs, self.sems, self.places = acc, sent, recvs, sems, places

    @staticmethod
    def scratch(rows, width, sizes):
        return [
            pltpu.VMEM((rows, width), F32), pltpu.VMEM((len(sizes), rows, width), LOW),
            *[pltpu.VMEM((size, rows, width), LOW) for size in sizes],
            *[pltpu.SemaphoreType.DMA((size,)) for size in sizes for _ in range(2)],
        ]

    def copies(self, stage):
        name, me, size = self.places[stage]
        send_sem, recv_sem = self.sems[2 * stage : 2 * stage + 2]
        return [
            pltpu.make_async_remote_copy(
                src_ref=self.sent.at[stage],
                dst_ref=self.recvs[stage].at[me],
                send_sem=send_sem.at[k],
                recv_sem=recv_sem.at[k],
                device_id={name: lax.rem(me + k, size)},
                device_id_type=MESH,
            )
            for k in range(1, size)
        ]

    def start(self, stage):
        value = self.acc[...].astype(LOW)
        self.sent[stage] = value
        self.recvs[stage][self.places[stage][1]] = value
        for copy in self.copies(stage):
            copy.start()

    def finish(self, stage):
        for copy in self.copies(stage):
            copy.wait()
        value = self.recvs[stage][0].astype(F32)
        for k in range(1, self.places[stage][2]):
            value = value + self.recvs[stage][k].astype(F32)
        self.acc[...] = value


def layer_kernel(
    lvars, lsegs, nvars, routers, steps, var_size, seg_size, sizes, groups, shares,
    dom_ref, cnt_ref, tok_ref, cot_ref, mean_ref, scale_ref, router_ref, wi_ref, wo_ref, ab_ref,
    win_ref, bin_ref, wout_ref, bout_ref, gain_ref, shift_ref, heads_ref, headsf_ref, split_ref, join_ref, mask_ref, grow_ref, shrink_ref, sumr_ref, swap_ref, back_ref,
    small_out_ref, out_ref, gin_ref, inner_ref, outer_ref, up_ref, down_ref, route_ref,
    sent_ref, came_ref, qx_ref, kq_ref, etc_ref, g1_ref, send_sem, recv_sem, out_sem, *scratch,
):
    me = lax.axis_index("var")
    seg = lax.axis_index("seg")
    width = tok_ref.shape[3]
    rows = lvars * tok_ref.shape[2]
    block = rows // var_size
    kept, scratch = scratch[:11], scratch[11:]
    cores, xs, ys, zs = sizes
    core, xi = lax.rem(seg, cores), lax.div(seg, cores)
    yi, zi = lax.rem(me, ys), lax.div(me, ys)

    def space(i):
        return {"seg": lax.rem(i, xs) * cores + core, "var": lax.div(i, xs)}

    axes = {
        "core": (core, cores, lambda i: {"seg": xi * cores + i}),
        "plane": (yi * xs + xi, xs * ys, lambda i: space(zi * (xs * ys) + i)),
        "z": (zi, zs, lambda i: {"var": i * ys + yi}),
        "space": (me * xs + xi, var_size * xs, space),
    }
    sums = []
    for _, names in groups:
        used = 7 + len(names)
        group, scratch = scratch[:used], scratch[used:]
        sums.append(Sum([axes[name] for name in names], group[0], group[1], group[2], group[7:], group[3:7]))
    parts = []
    for index, base, count in shares:
        parts.append((sums[index], base, sums[index].acc.at[pl.ds(base, count), :]))
    attns, routes, feeds, times = parts
    small = SmallSum(scratch[0], scratch[1], scratch[2:4], scratch[4:8], [("seg", seg, seg_size), ("var", me, var_size)])

    def copy(kind, b, k):
        target = lax.rem(me + k, var_size)
        return pltpu.make_async_remote_copy(
            src_ref=sent_ref.at[kind, b, target],
            dst_ref=came_ref.at[kind, b, me],
            send_sem=send_sem.at[kind, b],
            recv_sem=recv_sem.at[kind, b],
            device_id={"var": target},
            device_id_type=MESH,
        )

    def whole(kind, b):
        others = pl.ds(0, var_size - 1)
        return pltpu.make_async_remote_copy(
            src_ref=sent_ref.at[kind, b, others],
            dst_ref=came_ref.at[kind, b, others],
            send_sem=send_sem.at[kind, b],
            recv_sem=recv_sem.at[kind, b],
            device_id={"var": lax.rem(me + 1, var_size)},
            device_id_type=MESH,
        )

    def store(kind, b, value):
        value = value.reshape(var_size, block, width)
        sent_ref[kind, b] = value
        came_ref[kind, b, me] = sent_ref[kind, b, me]

    def send(kind, b):
        for k in range(1, var_size):
            copy(kind, b, k).start()

    def pick(b, ref):
        total = jnp.zeros((1, width), F32)
        for d in range(ref.shape[0]):
            total = total + jnp.where(dom_ref[b] == d, ref[d : d + 1, :], 0.0)
        return total

    def arrived(kind, b):
        whole(kind, b).wait_recv()
        return came_ref[kind, b]

    pieces = [
        (times, T_Q, 2 * width, inner_ref, 0), (feeds, M_V, width, inner_ref, 2 * width), (attns, B_SQ, 6 * width, inner_ref, 3 * width),
        (feeds, M_O, width, outer_ref, 0), (attns, B_O1, 2 * width, outer_ref, width),
        (feeds, M_IN, 2 * width, up_ref, 0), (routes, R_IN, 2 * width, up_ref, 2 * width),
        (feeds, M_OUT, 2 * width, down_ref, 0), (routes, R_OUT, 2 * width, down_ref, 2 * width),
        (routes, R_ROUTE, route_ref.shape[0], route_ref, 0),
    ]

    def deliver(which):
        return [
            pltpu.make_async_copy(
                which.total.at[pl.ds(base + row, count), :], ref.at[pl.ds(there, count), :], out_sem.at[index]
            )
            for index, ((total, base, _), row, count, ref, there) in enumerate(pieces)
            if total is which
        ]

    def series_out(kind, b):
        source, ref = ((came_ref.at[3, b], out_ref), (g1_ref.at[b], gin_ref))[kind]
        return pltpu.make_async_copy(source, ref.at[b], out_sem.at[len(pieces) + kind * steps + b])

    barrier = pltpu.get_barrier_semaphore()
    _, spaces, _ = axes["space"]
    for k in range(1, spaces):
        pl.semaphore_signal(barrier, inc=1, device_id=space(lax.rem(axes["space"][0] + k, spaces)), device_id_type=MESH)
    for k in range(1, cores):
        for i in range(xs):
            peer = {"seg": i * cores + lax.rem(core + k, cores)}
            pl.semaphore_signal(barrier, inc=1, device_id=peer, device_id_type=MESH)
    small.acc[...] = jnp.zeros_like(small.acc)

    def forward(b):
        store(1, b, mm(split_ref[...], cot_ref[b].reshape(rows, width)).astype(LOW))
        t2 = time_forward(
            lvars, b, tok_ref, pick(b, mean_ref), pick(b, scale_ref), wi_ref, wo_ref, ab_ref, win_ref, bin_ref,
            wout_ref, bout_ref, gain_ref, shift_ref, heads_ref, headsf_ref, kept,
        )
        store(0, b, mm(split_ref[...], t2).astype(LOW))

        @pl.when(b == 0)
        def _():
            pl.semaphore_wait(barrier, spaces - 1 + (cores - 1) * xs)

        send(0, b)
        send(1, b)

    def middle(b):
        def leaving(kind, value):
            store(kind, b, value)
            if kind == 2:
                send(2, b)

        limit = jnp.int32(0)
        for d in range(cnt_ref.shape[0]):
            limit = limit + jnp.where(dom_ref[b] == d, cnt_ref[d], 0)
        router_part(
            lsegs, nvars, routers, steps, b, lambda kind: arrived(kind, b), leaving,
            limit, router_ref, wi_ref, wo_ref, ab_ref, win_ref, bin_ref, wout_ref, bout_ref,
            gain_ref, shift_ref, mask_ref, grow_ref, shrink_ref, sumr_ref, swap_ref, back_ref,
            attns[2], routes[2], small.acc, qx_ref, kq_ref, me * lsegs, var_size,
        )

    def back_feed(b):
        feed_backward(
            lvars, b, lambda kind: arrived(kind, b), tok_ref, pick(b, mean_ref), pick(b, scale_ref), wo_ref, win_ref,
            wout_ref, gain_ref, shift_ref, heads_ref, join_ref, kept, feeds[2], small.acc, etc_ref, g1_ref,
        )

    def back_time(b):
        time_backward(
            lvars, b, tok_ref, pick(b, mean_ref), pick(b, scale_ref), heads_ref, headsf_ref, kept, times[2], small.acc,
            etc_ref,
        )

    def back_input(b):
        grad = g1_ref[b] + mm_nt(kept[0][b], wi_ref[0, 0]) + mm_nt(kept[1][b], wi_ref[0, 1])
        g1_ref[b] = (grad + mm_nt(kept[4][b], wi_ref[0, 2])) * pick(b, scale_ref)
        series_out(1, b).start()

    todo = {}

    def plan(total, *rounds):
        for turn in range(total.turns):
            todo.setdefault(rounds[min(turn, len(rounds) - 1)], []).append(functools.partial(total.advance, turn))

    for b, round_ in enumerate(OUT_ROUNDS):
        todo.setdefault(round_, []).append(functools.partial(send, 3, b))
    rounds_of = (ATTN_ROUNDS, ROUTE_ROUNDS, FEED_ROUNDS, TIME_ROUNDS) if len(sums) > 1 else ((2 * steps, 3 * steps),)
    for total, rounds in zip(sums, rounds_of):
        plan(total, *rounds)
    todo.setdefault(2 * steps, []).append(functools.partial(small.start, 0))
    todo.setdefault(2 * steps + steps // 2, []).append(lambda: (small.finish(0), small.start(1)))

    def sweep(run, first):
        def body(b, carry):
            for round_, acts in sorted(todo.items()):
                if first <= round_ < first + steps:

                    @pl.when(b == round_ - first)
                    def _(acts=acts):
                        for act in acts:
                            act()

            run(b)
            return carry

        lax.fori_loop(0, steps, body, 0)

    sweep(forward, -2 * steps)
    sweep(middle, -steps)
    sweep(back_feed, 0)
    sweep(back_time, steps)
    sweep(back_input, 2 * steps)
    last = [max(rounds[: total.turns]) for total, rounds in zip(sums, rounds_of)]
    for round_ in range(3 * steps, max(max(todo), *last) + 1):
        for act in todo.get(round_, []):
            act()
        for total, end in zip(sums, last):
            if round_ == max(end, 3 * steps):
                for copy in deliver(total):
                    copy.start()
    small.finish(1)
    small_out_ref[...] = small.acc[...]
    for b in range(steps):
        whole(3, b).wait_recv()
        series_out(0, b).start()
    for b in range(steps):
        for kind in range(4):
            whole(kind, b).wait_send()
    for total in sums:
        for copy in deliver(total):
            copy.wait()
    for b in range(steps):
        series_out(0, b).wait()
        series_out(1, b).wait()


def finish_kernel(
    segs, lvars, out_ref, gin_ref, small_ref, inner_ref, outer_ref, up_ref, down_ref, route_ref, join_ref,
    output_ref, gin_out_ref, ginner_ref, gouter_ref, gbias_ref, gup_ref, gupb_ref, gdown_ref, gdownb_ref, ggain_ref,
    gshift_ref, groute_ref,
):
    width = inner_ref.shape[1]

    @pl.when(pl.program_id(0) == 0)
    def _():
        for i in range(3):
            gbias_ref[i] = small_ref[S_BIAS + 3 * i : S_BIAS + 3 * i + 3, :]
        for i in range(2):
            for j in range(2):
                row = S_IN + 2 * i + j
                gupb_ref[i : i + 1, j * width : (j + 1) * width] = small_ref[row : row + 1, :]
        gdownb_ref[...] = small_ref[S_OUT : S_OUT + 2, :]
        ggain_ref[...] = small_ref[S_GAIN : S_GAIN + 4, :]
        gshift_ref[...] = small_ref[S_SHIFT : S_SHIFT + 4, :]

    for i in range(out_ref.shape[0]):
        output_ref[i] = mm(join_ref[...], out_ref[i].reshape(lvars * segs, width)).reshape(lvars, segs, width)
    gin_out_ref[...] = gin_ref[...]
    ginner_ref[...] = inner_ref[...].astype(F32)
    gouter_ref[...] = outer_ref[...].astype(F32)
    gup_ref[0, :, :width] = up_ref[0, 0].astype(F32)
    gup_ref[0, :, width:] = up_ref[0, 1].astype(F32)
    gdown_ref[...] = down_ref[...].astype(F32)
    groute_ref[...] = route_ref[...].astype(F32)


def fixed(shape, index=None):
    index = (0,) * len(shape) if index is None else index
    return pl.BlockSpec(shape, lambda b: index)


def on_device(
    var_size, seg_size,
    tokens, domain, counts, domain_mean, domain_scale, attn_inner, attn_outer, attn_bias,
    mlp_in, mlp_in_bias, mlp_out, mlp_out_bias, norm_gain, norm_bias, router, cotangent,
):
    batch, lvars, segs, width = tokens.shape
    routers = router.shape[1]
    hidden = mlp_in.shape[2]
    lsegs = segs // var_size
    nvars = lvars * var_size
    rows = lvars * segs
    lanes = SLOTS * HEADS
    me = lax.axis_index("var")

    heads = (np.arange(width)[None, :] // (width // HEADS) == np.arange(HEADS)[:, None]).astype(np.float32)
    heads_low = jnp.asarray(heads, LOW)
    heads_f = jnp.asarray(heads, F32)
    mask = jnp.asarray(np.concatenate([heads, heads], axis=0), LOW)
    order = np.arange(rows).reshape(lvars, var_size, lsegs).transpose(1, 0, 2).reshape(-1)
    split = np.eye(rows, dtype=np.float32)[order]
    order = np.arange(rows).reshape(nvars, lsegs).transpose(1, 0).reshape(-1)
    swap = np.eye(rows, dtype=np.float32)[order]
    group = np.arange(lsegs * lanes) // HEADS
    group = group % SLOTS * lsegs + group // SLOTS
    grow = (group[:, None] == np.arange(lsegs * SLOTS)[None, :]).astype(np.float32)
    sumr = (np.arange(lanes)[:, None] % HEADS == np.arange(lanes)[None, :] % HEADS).astype(np.float32)

    kept = [
        ((rows, width), LOW), ((rows, width), LOW), ((rows, width), LOW), ((rows, HEADS * segs), LOW),
        ((rows, width), LOW), ((rows, width), LOW), ((rows, 128), F32), ((rows, hidden), LOW),
        ((rows, hidden), LOW), ((rows, width), LOW), ((rows, 128), F32),
    ]
    mine = lax.dynamic_slice_in_dim(router.transpose(1, 0, 2), me * lsegs, lsegs, 1)
    mine = jnp.pad(mine, ((0, SLOTS - routers), (0, 0), (0, 0))).reshape(SLOTS * lsegs, width)
    consts = [jnp.asarray(x, LOW) for x in (split, split.T)] + [mask]
    consts += [jnp.asarray(x, LOW) for x in (grow, grow.T, sumr, swap, swap.T)]

    cores = 2 if seg_size % 2 == 0 else 1
    xs = seg_size // cores
    ys = xs if var_size % xs == 0 else 1
    zs = var_size // ys
    sizes = (cores, xs, ys, zs)
    counts_of = {"core": cores, "plane": xs * ys, "z": zs, "space": var_size * xs}
    far = ("core", "plane", "z")
    near = ("core", "space") if var_size * xs <= 16 else far
    unit = 16 * var_size * seg_size
    wanted = [(B_ROWS, far), (R_ROUTE + segs * routers, far), (M_ROWS, far), (T_ROWS, near)]
    if unit > 1024:
        starts = np.cumsum([0] + [count for count, _ in wanted])
        parts = [(0, int(start), count) for start, (count, _) in zip(starts, wanted)]
        wanted = [(int(starts[-1]), far)]
    else:
        parts = [(index, 0, count) for index, (count, _) in enumerate(wanted)]
    groups = []
    for count, names in wanted:
        groups.append((-(-count // unit) * unit, [name for name in names if counts_of[name] > 1]))
    scalars = pl.BlockSpec(memory_space=pltpu.SMEM)
    anywhere = pl.BlockSpec(memory_space=pl.ANY)
    out_shapes = [
        jax.ShapeDtypeStruct((S_ROWS, width), F32),
        jax.ShapeDtypeStruct((batch, var_size, rows // var_size, width), LOW),
        jax.ShapeDtypeStruct((batch, rows, width), F32),
        jax.ShapeDtypeStruct((9 * width, width), LOW),
        jax.ShapeDtypeStruct((3 * width, width), LOW),
        jax.ShapeDtypeStruct((4 * width, width), LOW),
        jax.ShapeDtypeStruct((2 * hidden, width), LOW),
        jax.ShapeDtypeStruct((routers * segs, width), LOW),
    ]
    in_vmem = pl.BlockSpec(memory_space=pltpu.VMEM)
    small, arrived, input_grad, inner_low, outer_low, up_low, down_low, route_low = pl.pallas_call(
        functools.partial(layer_kernel, lvars, lsegs, nvars, routers, batch, var_size, seg_size, sizes, groups, parts),
        in_specs=[scalars] * 2 + [in_vmem] * (16 + len(consts)),
        out_specs=[in_vmem] + [anywhere] * 7,
        out_shape=out_shapes,
        scratch_shapes=[
            pltpu.VMEM((4, batch, var_size, rows // var_size, width), LOW),
            pltpu.VMEM((4, batch, var_size, rows // var_size, width), LOW),
            pltpu.VMEM((lsegs * lanes, width), LOW),
            pltpu.VMEM((lsegs * lanes, width), F32),
            pltpu.VMEM((batch, rows, width), LOW),
            pltpu.VMEM((batch, rows, width), F32),
            pltpu.SemaphoreType.DMA((4, batch)),
            pltpu.SemaphoreType.DMA((4, batch)),
            pltpu.SemaphoreType.DMA((10 + 2 * batch,)),
            *[pltpu.VMEM((batch,) + shape, dtype) for shape, dtype in kept],
            *[x for count, names in groups for x in Sum.scratch(count, width, [counts_of[name] for name in names])],
            *SmallSum.scratch(S_ROWS, width, (seg_size, var_size)),
        ],
        compiler_params=pltpu.CompilerParams(
            vmem_limit_bytes=VMEM_LIMIT, collective_id=0, has_side_effects=True
        ),
        name="layer",
    )(
        domain, counts, tokens, cotangent, domain_mean, domain_scale, mine, attn_inner, attn_outer, attn_bias, mlp_in,
        mlp_in_bias, mlp_out, mlp_out_bias, norm_gain, norm_bias, heads_low, heads_f, *consts,
    )

    turns = 4

    def shares(*shape):
        shape = (shape[0] // turns,) + shape[1:]
        return pl.BlockSpec(shape, lambda i: (i,) + (0,) * (len(shape) - 1))

    piece = width * 2 // turns
    per = turns // 2
    whole = lambda x: fixed(x.shape)
    f32 = lambda x: jax.ShapeDtypeStruct(x.shape, F32)
    output, input_grad, grad_inner, grad_outer, grad_bias, grad_up, grad_up_bias, grad_down, *rest = pl.pallas_call(
        functools.partial(finish_kernel, segs, lvars),
        grid=(turns,),
        in_specs=[
            shares(*arrived.shape), shares(*input_grad.shape), whole(small),
            shares(*inner_low.shape), shares(*outer_low.shape),
            pl.BlockSpec((1, 2, piece, width), lambda i: (i // per, 0, i % per, 0)),
            shares(*down_low.shape), shares(*route_low.shape), whole(consts[1]),
        ],
        out_specs=[
            shares(*tokens.shape), shares(*input_grad.shape), shares(*inner_low.shape), shares(*outer_low.shape), whole(attn_bias),
            pl.BlockSpec((1, piece, hidden), lambda i: (i // per, i % per, 0)), whole(mlp_in_bias),
            shares(*down_low.shape), whole(mlp_out_bias), whole(norm_gain), whole(norm_bias), shares(*route_low.shape),
        ],
        out_shape=[
            f32(tokens), f32(input_grad), f32(inner_low), f32(outer_low), f32(attn_bias), f32(mlp_in), f32(mlp_in_bias),
            f32(down_low), f32(mlp_out_bias), f32(norm_gain), f32(norm_bias), f32(route_low),
        ],
        compiler_params=pltpu.CompilerParams(dimension_semantics=("arbitrary",), vmem_limit_bytes=VMEM_LIMIT),
        name="finish",
    )(
        arrived, input_grad, small, inner_low, outer_low, up_low.reshape(2, 2, width, width), down_low,
        route_low, consts[1],
    )
    grad_down_bias, grad_gain, grad_shift, grad_router = rest
    return (
        output, input_grad.reshape(tokens.shape), grad_inner.reshape(attn_inner.shape),
        grad_outer.reshape(attn_outer.shape), grad_bias, grad_up, grad_up_bias, grad_down.reshape(mlp_out.shape),
        grad_down_bias, grad_gain, grad_shift, grad_router.reshape(routers, segs, width).transpose(1, 0, 2),
    )


def solution(mesh):
    split = P("seg", "var", None, None)
    in_specs = (split, P("seg")) + (P(),) * 13 + (split,)
    out_specs = (split, split) + (P(),) * 10
    var_size, seg_size = mesh.shape["var"], mesh.shape["seg"]
    return jax.shard_map(
        functools.partial(on_device, var_size, seg_size),
        mesh=mesh, in_specs=in_specs, out_specs=out_specs, check_vma=False,
    )
```

time: 194 us -> 154 us (0.79)
  the two profiles are of different devices: /device:TPU:29 before, /device:TPU:0 now
where the time goes in v4:
time: 154 us
  Pallas kernels  151 us (98%)
  local copies, waits for them, and re-layouts  1.61 us (1%)
    pallas_call x1, Pallas kernels, on_device(): pl.pallas_call(functools.partial(layer_kernel, lvars, lsegs, nvars, route...  145 us
    pallas_call x1, Pallas kernels, on_device(): pl.pallas_call(functools.partial(finish_kernel, segs, lvars), grid=(turns...  6.8 us

profile of v4, /device:TPU:0, one launch (start us, length us, event | category | flops | bytes accessed | tf_op | source)
XLA Modules:
  0.0 153.8 jit_solution(12734554613601961916)
XLA Ops:
  0.6 0.0 copy-start
  0.7 1.0 copy-done
  1.6 0.6 pad_bitcast_fusion.router_ref
  2.3 144.7 %layer.1 = (f32[32,256]{1,0:T(8,128)}, bf16[8,8,32,256]{3,2,1,0:T(8,128)(2,1)}, f32[8,256,256]{2,1,0:T(8,128)}, bf16[2304,256]{1,0:T(8,128)(2,1)}, bf16[768,256]...) custom-call(s32[8]{0:T(128)} %dom_ref.1, s32[4]{0:T(128)} %cnt_ref.1, ...), custom_call_target="tpu_custom_call" | custom-call | tf_op jit(solution)/shard_map/layer/pallas_call | solution.py:783
  147.0 6.8 %finish.1 = (f32[8,4,64,256]{3,2,1,0:T(8,128)}, f32[8,256,256]{2,1,0:T(8,128)}, f32[2304,256]{1,0:T(8,128)}, f32[768,256]{1,0:T(8,128)}, f32[3,3,256]{2,1,0:T(4,...) custom-call(bf16[8,8,32,256]{3,2,1,0:T(8,128)(2,1)} %get-tuple-eleme, ...), custom_call_target="tpu_custom_call" | custom-call | tf_op jit(solution)/shard_map/finish/pallas_call | solution.py:821
  (1 shorter events, 0.0 us)
Async XLA Ops:
  0.6 1.0 copy-start

commit v5 on v4

--- a/solution.py
+++ b/solution.py
@@ -18,11 +18,13 @@
 VMEM_LIMIT = 60 * 1024 * 1024
 
 
-OUT_ROUNDS = (-7, -6, -5, -4, -3, -2, -1, 0)
+OUT_ROUNDS = (-2, -2, 0, 2, 4, 8, 12, 14)
 ATTN_ROUNDS = (0, 2, 9, 14, 17, 19, 21)
 ROUTE_ROUNDS = (1, 3, 12, 16, 18, 20, 22)
-FEED_ROUNDS = (9, 11, 16, 18, 20, 22, 24)
+FEED_ROUNDS = (12, 14, 16, 18, 20, 22, 24)
 TIME_ROUNDS = (16, 17, 19, 22, 23)
+TOGETHER = (2, 2, 2, 2, 2)
+AHEAD = 1
 
 
 def mm(a, b):
@@ -78,40 +80,52 @@
 
 
 def time_forward(
-    lvars, b, tok_ref, offset, factor, wi_ref, wo_ref, ab_ref, win_ref, bin_ref, wout_ref, bout_ref,
+    lvars, b, several, tok_ref, offsets, factors, wi_ref, wo_ref, ab_ref, win_ref, bin_ref, wout_ref, bout_ref,
     gain_ref, shift_ref, heads_ref, headsf_ref, kept,
 ):
     q_ref, k_ref, v_ref, p_ref, tc_ref, x1_ref, r1_ref, f1_ref, s1_ref, x2_ref, r2_ref = kept
     segs, width = tok_ref.shape[2:]
     rows = lvars * segs
     scale = np.float32((width // HEADS) ** (-0.5))
-    tok = tok_ref[b].reshape(rows, width).astype(F32)
-    start = (tok - offset) * factor
+
+    def keep(ref, value):
+        ref[pl.ds(b, several)] = value.reshape(several, rows, value.shape[1])
+
+    start = jnp.concatenate(
+        [(tok_ref[b + i].reshape(rows, width).astype(F32) - offsets[i]) * factors[i] for i in range(several)], axis=0
+    )
     low = start.astype(LOW)
-    q_ref[b] = (mm(low, wi_ref[0, 0]) + ab_ref[0, 0:1, :]).astype(LOW)
-    k_ref[b] = mm(low, wi_ref[0, 1]).astype(LOW)
-    v_ref[b] = (mm(low, wi_ref[0, 2]) + ab_ref[0, 1:2, :]).astype(LOW)
-    for v in range(lvars):
+    query = (mm(low, wi_ref[0, 0]) + ab_ref[0, 0:1, :]).astype(LOW)
+    key = mm(low, wi_ref[0, 1]).astype(LOW)
+    value = (mm(low, wi_ref[0, 2]) + ab_ref[0, 1:2, :]).astype(LOW)
+    keep(q_ref, query)
+    keep(k_ref, key)
+    keep(v_ref, value)
+    probs, contexts = [], []
+    for v in range(several * lvars):
         part = slice(v * segs, (v + 1) * segs)
-        spread = spread_heads(q_ref[b, part, :], heads_ref)
-        scores = mm_nt(k_ref[b, part, :], spread)
+        scores = mm_nt(key[part], spread_heads(query[part], heads_ref))
         top = jnp.max(scores, axis=0, keepdims=True)
         expo = jnp.exp((scores - top) * scale)
         prob = (expo / jnp.sum(expo, axis=0, keepdims=True)).astype(LOW)
-        p_ref[b, part, :] = prob
-        tc_ref[b, part, :] = gather_heads(mm_tn(prob, v_ref[b, part, :]), headsf_ref, segs).astype(LOW)
-    a1 = start + mm(tc_ref[b], wo_ref[0]) + ab_ref[0, 2:3, :]
+        probs.append(prob)
+        contexts.append(gather_heads(mm_tn(prob, value[part]), headsf_ref, segs).astype(LOW))
+    keep(p_ref, jnp.concatenate(probs, axis=0))
+    context = jnp.concatenate(contexts, axis=0)
+    keep(tc_ref, context)
+    a1 = start + mm(context, wo_ref[0]) + ab_ref[0, 2:3, :]
     x1, r1 = ln_stats(a1)
-    x1_ref[b] = x1.astype(LOW)
-    r1_ref[b] = jnp.broadcast_to(r1, (rows, 128))
+    keep(x1_ref, x1.astype(LOW))
+    keep(r1_ref, jnp.broadcast_to(r1, (several * rows, 128)))
     t1 = x1 * gain_ref[0:1, :] + shift_ref[0:1, :]
     act, slope = gelu_both(mm(t1.astype(LOW), win_ref[0]) + bin_ref[0:1, :])
-    f1_ref[b] = act.astype(LOW)
-    s1_ref[b] = slope.astype(LOW)
-    a2 = t1 + mm(f1_ref[b], wout_ref[0]) + bout_ref[0:1, :]
+    f1 = act.astype(LOW)
+    keep(f1_ref, f1)
+    keep(s1_ref, slope.astype(LOW))
+    a2 = t1 + mm(f1, wout_ref[0]) + bout_ref[0:1, :]
     x2, r2 = ln_stats(a2)
-    x2_ref[b] = x2.astype(LOW)
-    r2_ref[b] = jnp.broadcast_to(r2, (rows, 128))
+    keep(x2_ref, x2.astype(LOW))
+    keep(r2_ref, jnp.broadcast_to(r2, (several * rows, 128)))
     return (x2 * gain_ref[1:2, :] + shift_ref[1:2, :]).astype(LOW)
 
 
@@ -122,53 +136,90 @@
 S_BIAS, S_IN, S_OUT, S_GAIN, S_SHIFT, S_ROWS = 0, 9, 13, 15, 19, 32
 
 
+def router_start(router_ref, wi_ref, ab_ref, grow_ref, mask_ref, attn_ref, rest_ref, qx_ref, kq_ref):
+    attn_ref[...] = jnp.zeros(attn_ref.shape, F32)
+    rest_ref[...] = jnp.zeros(rest_ref.shape, F32)
+    kq_ref[...] = jnp.zeros(kq_ref.shape, F32)
+    sq = (mm(router_ref[...], wi_ref[1, 0]) + ab_ref[1, 0:1, :]).astype(LOW)
+    qx_ref[...] = expand(sq, grow_ref, mask_ref)
+
+
+def router_end(lsegs, routers, var_size, first_seg, router_ref, wi_ref, shrink_ref, mask_ref, attn_ref, rest_ref, small_ref, kq_ref):
+    width = router_ref.shape[1]
+    kq = contract(kq_ref[...], shrink_ref, mask_ref)
+    kq_low = kq.astype(LOW)
+    attn_ref[B_SQ : B_SQ + width, :] = mm_tn(router_ref[...], kq_low)
+    small_ref[S_BIAS + 3 : S_BIAS + 4, :] = col_sum(kq)
+    places = routers * lsegs * var_size
+    there = lax.broadcasted_iota(jnp.int32, (places, lsegs * SLOTS), 0)
+    here = lax.broadcasted_iota(jnp.int32, (places, lsegs * SLOTS), 1)
+    here = lax.div(here, lsegs) * (lsegs * var_size) + lax.rem(here, lsegs) + first_seg
+    here = jnp.where(there == here, 1.0, 0.0).astype(LOW)
+    rest_ref[R_ROUTE : R_ROUTE + places, :] = mm(here, mm_nt(kq_low, wi_ref[1, 0]).astype(LOW))
+
+
+def expand(x, grow_ref, mask_ref):
+    width = x.shape[1]
+    return (mm(grow_ref[...], x).astype(LOW).reshape(-1, 16, width) * mask_ref[...][None]).reshape(-1, width)
+
+
+def contract(x, shrink_ref, mask_ref):
+    width = x.shape[1]
+    return mm(shrink_ref[...], (x.astype(LOW).reshape(-1, 16, width) * mask_ref[...][None]).reshape(-1, width))
+
+
 def router_part(
-    lsegs, nvars, routers, steps, b, arrived, leaving,
-    limit, router_ref, wi_ref, wo_ref, ab_ref, win_ref, bin_ref, wout_ref, bout_ref,
+    lsegs, nvars, routers, several, arrived, leaving,
+    limits, wi_ref, wo_ref, ab_ref, win_ref, bin_ref, wout_ref, bout_ref,
     gain_ref, shift_ref, mask_ref, grow_ref, shrink_ref, sumr_ref, perm_ref, back_ref,
-    attn_ref, rest_ref, small_ref, qx_ref, kq_ref, first_seg, var_size,
+    attn_ref, rest_ref, small_ref, qx_ref, kq_ref,
 ):
-    rows, width = perm_ref.shape[0], wo_ref.shape[1]
+    series, width = perm_ref.shape[0], wo_ref.shape[1]
+    rows = several * series
     lanes = SLOTS * HEADS
     scale = np.float32((width // HEADS) ** (-0.5))
-
-    def expand(x):
-        return (mm(grow_ref[...], x).astype(LOW).reshape(-1, 16, width) * mask_ref[...][None]).reshape(-1, width)
-
-    def contract(x):
-        return mm(shrink_ref[...], (x.astype(LOW).reshape(-1, 16, width) * mask_ref[...][None]).reshape(-1, width))
-
-    @pl.when(b == 0)
-    def _():
-        attn_ref[...] = jnp.zeros(attn_ref.shape, F32)
-        rest_ref[...] = jnp.zeros(rest_ref.shape, F32)
-        kq_ref[...] = jnp.zeros_like(kq_ref)
-        sq = (mm(router_ref[...], wi_ref[1, 0]) + ab_ref[1, 0:1, :]).astype(LOW)
-        qx_ref[...] = expand(sq)
-
-    def per_segment(f):
-        return [f(slice(s * nvars, (s + 1) * nvars), slice(s * lanes, (s + 1) * lanes)) for s in range(lsegs)]
-
-    t2 = mm(perm_ref[...], arrived(0).reshape(rows, width)).astype(LOW)
+    parts = range(several * lsegs)
+    ns = [slice(j * nvars, (j + 1) * nvars) for j in parts]
+    ls = [slice(j * lanes, (j + 1) * lanes) for j in parts]
+    qs = [slice(j % lsegs * lanes, (j % lsegs + 1) * lanes) for j in parts]
+
+    def cat(blocks):
+        return jnp.concatenate(list(blocks), axis=0)
+
+    def each(f, x):
+        size = x.shape[0] // several
+        return cat(f(x[i * size : (i + 1) * size]) for i in range(several))
+
+    def grown(x):
+        return each(lambda y: expand(y, grow_ref, mask_ref), x)
+
+    def shrunk(blocks):
+        return cat(contract(cat(blocks[i * lsegs : (i + 1) * lsegs]), shrink_ref, mask_ref) for i in range(several))
+
+    def permuted(ref, x):
+        return each(lambda y: mm(ref[...], y), x)
+
+    t2 = permuted(perm_ref, arrived(0)).astype(LOW)
     sk = mm(t2, wi_ref[1, 1]).astype(LOW)
     sv = (mm(t2, wi_ref[1, 2]) + ab_ref[1, 1:2, :]).astype(LOW)
     rq = (mm(t2, wi_ref[2, 0]) + ab_ref[2, 0:1, :]).astype(LOW)
-    valid = lax.broadcasted_iota(jnp.int32, (nvars, lanes), 0).astype(F32) < limit
-
-    def send_prob(n, l):
-        scores = jnp.where(valid, mm_nt(sk[n], qx_ref[l, :]), MASKED)
+    var = lax.broadcasted_iota(jnp.int32, (nvars, lanes), 0)
+    valid = [var < limit for limit in limits]
+
+    def send_prob(j):
+        real = valid[j // lsegs]
+        scores = jnp.where(real, mm_nt(sk[ns[j]], qx_ref[qs[j], :]), MASKED)
         top = jnp.max(scores, axis=0, keepdims=True)
-        expo = jnp.where(valid, jnp.exp((scores - top) * scale), 0.0)
+        expo = jnp.where(real, jnp.exp((scores - top) * scale), 0.0)
         return expo / jnp.sum(expo, axis=0, keepdims=True)
 
-    sp = per_segment(send_prob)
+    sp = [send_prob(j) for j in parts]
     sp_low = [x.astype(LOW) for x in sp]
-    pre = contract(jnp.concatenate([mm_tn(sp_low[s], sv[s * nvars : (s + 1) * nvars]) for s in range(lsegs)], axis=0))
-    pre_low = pre.astype(LOW)
+    pre_low = shrunk([mm_tn(sp_low[j], sv[ns[j]]) for j in parts]).astype(LOW)
     buffer = (mm(pre_low, wo_ref[1]) + ab_ref[1, 2:3, :]).astype(LOW)
-    rkx = expand(mm(buffer, wi_ref[2, 1]).astype(LOW))
-    rvx = expand((mm(buffer, wi_ref[2, 2]) + ab_ref[2, 1:2, :]).astype(LOW))
-    scores = jnp.concatenate(per_segment(lambda n, l: mm_nt(rq[n], rkx[l])), axis=0)
+    rkx = grown(mm(buffer, wi_ref[2, 1]).astype(LOW))
+    rvx = grown((mm(buffer, wi_ref[2, 2]) + ab_ref[2, 1:2, :]).astype(LOW))
+    scores = cat(mm_nt(rq[ns[j]], rkx[ls[j]]) for j in parts)
     real = lax.broadcasted_iota(jnp.int32, (rows, lanes), 1) < routers * HEADS
     scores = jnp.where(real, scores, MASKED)
     top = scores
@@ -179,7 +230,7 @@
     expo = jnp.where(real, jnp.exp((scores - top) * scale), 0.0)
     rp = expo / mm(expo.astype(LOW), sumr_ref[...])
     rp_low = rp.astype(LOW)
-    rc = jnp.concatenate(per_segment(lambda n, l: mm(rp_low[n], rvx[l])), axis=0).astype(LOW)
+    rc = cat(mm(rp_low[ns[j]], rvx[ls[j]]) for j in parts).astype(LOW)
     a3 = t2.astype(F32) + mm(rc, wo_ref[2]) + ab_ref[2, 2:3, :]
     x3, r3 = ln_stats(a3)
     t3 = x3 * gain_ref[2:3, :] + shift_ref[2:3, :]
@@ -189,7 +240,7 @@
     a4 = t3 + mm(f2, wout_ref[1]) + bout_ref[1:2, :]
     x4, r4 = ln_stats(a4)
     out = (x4 * gain_ref[3:4, :] + shift_ref[3:4, :]).astype(LOW)
-    leaving(3, mm(back_ref[...], out).astype(LOW))
+    leaving(3, permuted(back_ref, out).astype(LOW))
 
     def add(row, value, ref=attn_ref):
         ref[row : row + value.shape[0], :] += value
@@ -197,7 +248,7 @@
     def add_small(row, value):
         small_ref[row : row + 1, :] += value
 
-    cot = mm(perm_ref[...], arrived(1).reshape(rows, width))
+    cot = permuted(perm_ref, arrived(1))
     add_small(S_GAIN + 3, col_sum(cot * x4))
     add_small(S_SHIFT + 3, col_sum(cot))
     g4 = ln_back(cot, x4, r4, gain_ref[3:4, :])
@@ -218,79 +269,70 @@
     add(B_O2, mm_tn(rc, eo))
     add_small(S_BIAS + 8, col_sum(eo))
     ec = mm_nt(eo, wo_ref[2]).astype(LOW)
-    dp = jnp.concatenate(per_segment(lambda n, l: mm_nt(ec[n], rvx[l])), axis=0)
+    dp = cat(mm_nt(ec[ns[j]], rvx[ls[j]]) for j in parts)
     ds = (scale * rp * (dp - mm((rp * dp).astype(LOW), sumr_ref[...]))).astype(LOW)
-    erq = jnp.concatenate(per_segment(lambda n, l: mm(ds[n], rkx[l])), axis=0).astype(LOW)
-    erk = contract(jnp.concatenate(per_segment(lambda n, l: mm_tn(ds[n], rq[n])), axis=0)).astype(LOW)
-    erv = contract(jnp.concatenate(per_segment(lambda n, l: mm_tn(rp_low[n], ec[n])), axis=0)).astype(LOW)
+    erk = shrunk([mm_tn(ds[ns[j]], rq[ns[j]]) for j in parts]).astype(LOW)
+    erv = shrunk([mm_tn(rp_low[ns[j]], ec[ns[j]]) for j in parts]).astype(LOW)
+    erq = cat(mm(ds[ns[j]], rkx[ls[j]]) for j in parts).astype(LOW)
+    eb = (mm_nt(erk, wi_ref[2, 1]) + mm_nt(erv, wi_ref[2, 2])).astype(LOW)
+    epx = grown(mm_nt(eb, wo_ref[1]).astype(LOW))
     add(B_RQ, mm_tn(t2, erq))
     add_small(S_BIAS + 6, col_sum(erq))
     add(B_RK, mm_tn(buffer, erk))
     add(B_RV, mm_tn(buffer, erv))
     add_small(S_BIAS + 7, col_sum(erv))
-    eb = (mm_nt(erk, wi_ref[2, 1]) + mm_nt(erv, wi_ref[2, 2])).astype(LOW)
     add(B_O1, mm_tn(pre_low, eb))
     add_small(S_BIAS + 5, col_sum(eb))
-    epx = expand(mm_nt(eb, wo_ref[1]).astype(LOW))
     dss = []
+    for j in parts:
+        weighted = sp[j] * mm_nt(sv[ns[j]], epx[ls[j]])
+        center = jnp.sum(weighted, axis=0, keepdims=True)
+        dss.append((scale * (weighted - sp[j] * center)).astype(LOW))
+    esv = cat(mm(sp_low[j], epx[ls[j]]) for j in parts).astype(LOW)
+    esk = cat(mm(dss[j], qx_ref[qs[j], :]) for j in parts).astype(LOW)
+    g2 = g3 + mm_nt(erq, wi_ref[2, 0]) + mm_nt(esk, wi_ref[1, 1]) + mm_nt(esv, wi_ref[1, 2])
+    leaving(2, permuted(back_ref, g2.astype(LOW)).astype(LOW))
     for s in range(lsegs):
-        dps = mm_nt(sv[s * nvars : (s + 1) * nvars], epx[s * lanes : (s + 1) * lanes])
-        weighted = sp[s] * dps
-        center = jnp.sum(weighted, axis=0, keepdims=True)
-        dss.append((scale * (weighted - sp[s] * center)).astype(LOW))
-    esv = jnp.concatenate([mm(sp_low[s], epx[s * lanes : (s + 1) * lanes]) for s in range(lsegs)], axis=0).astype(LOW)
-    esk = jnp.concatenate([mm(dss[s], qx_ref[s * lanes : (s + 1) * lanes, :]) for s in range(lsegs)], axis=0).astype(LOW)
-    for s in range(lsegs):
-        kq_ref[s * lanes : (s + 1) * lanes, :] += mm_tn(dss[s], sk[s * nvars : (s + 1) * nvars])
+        total = mm_tn(dss[s], sk[ns[s]])
+        for i in range(1, several):
+            total = total + mm_tn(dss[i * lsegs + s], sk[ns[i * lsegs + s]])
+        kq_ref[qs[s], :] += total
     add(B_SK, mm_tn(t2, esk))
     add(B_SV, mm_tn(t2, esv))
     add_small(S_BIAS + 4, col_sum(esv))
-    g2 = g3 + mm_nt(erq, wi_ref[2, 0]) + mm_nt(esk, wi_ref[1, 1]) + mm_nt(esv, wi_ref[1, 2])
-    leaving(2, mm(back_ref[...], g2.astype(LOW)).astype(LOW))
-
-    @pl.when(b == steps - 1)
-    def _():
-        kq = contract(kq_ref[...])
-        kq_low = kq.astype(LOW)
-        attn_ref[B_SQ : B_SQ + width, :] = mm_tn(router_ref[...], kq_low)
-        add_small(S_BIAS + 3, col_sum(kq))
-        places = routers * lsegs * var_size
-        there = lax.broadcasted_iota(jnp.int32, (places, lsegs * SLOTS), 0)
-        here = lax.broadcasted_iota(jnp.int32, (places, lsegs * SLOTS), 1)
-        here = lax.div(here, lsegs) * (lsegs * var_size) + lax.rem(here, lsegs) + first_seg
-        here = jnp.where(there == here, 1.0, 0.0).astype(LOW)
-        rest_ref[R_ROUTE : R_ROUTE + places, :] = mm(here, mm_nt(kq_low, wi_ref[1, 0]).astype(LOW))
 
 
 def feed_backward(
-    lvars, b, arrived, tok_ref, offset, factor, wo_ref, win_ref, wout_ref, gain_ref, shift_ref, heads_ref, perm_ref, kept,
-    feeds_ref, small_ref, etc_ref, g1_ref,
+    lvars, b, several, arrived, tok_ref, offsets, factors, wo_ref, win_ref, wout_ref, gain_ref, shift_ref, heads_ref,
+    perm_ref, kept, feeds_ref, small_ref, etc_ref, g1_ref,
 ):
-
     q_ref, k_ref, v_ref, p_ref, tc_ref, x1_ref, r1_ref, f1_ref, s1_ref, x2_ref, r2_ref = kept
     segs, width = tok_ref.shape[2:]
     rows = lvars * segs
 
-    @pl.when(b == 0)
-    def _():
-        feeds_ref[...] = jnp.zeros(feeds_ref.shape, F32)
-
     def add(ref, row, value):
         ref[row : row + value.shape[0], :] += value
 
+    def held(ref):
+        return ref[pl.ds(b, several)].reshape(several * rows, ref.shape[2])
+
+    def keep(ref, value):
+        ref[pl.ds(b, several)] = value.reshape(several, rows, value.shape[1])
+
     def wide(ref):
-        return jnp.concatenate([ref[b]] * (width // 128), axis=1)
-
-    g2 = mm(perm_ref[...], arrived(2).reshape(rows, width))
-    x2 = x2_ref[b].astype(F32)
+        return jnp.concatenate([held(ref)] * (width // 128), axis=1)
+
+    g2 = arrived(2)
+    g2 = jnp.concatenate([mm(perm_ref[...], g2[i * rows : (i + 1) * rows]) for i in range(several)], axis=0)
+    x2 = held(x2_ref).astype(F32)
     add(small_ref, S_GAIN + 1, col_sum(g2 * x2))
     add(small_ref, S_SHIFT + 1, col_sum(g2))
     g2 = ln_back(g2, x2, wide(r2_ref), gain_ref[1:2, :])
     e2 = g2.astype(LOW)
-    add(feeds_ref, M_OUT, mm_tn(f1_ref[b], e2))
+    add(feeds_ref, M_OUT, mm_tn(held(f1_ref), e2))
     add(small_ref, S_OUT, col_sum(e2))
-    e1 = (s1_ref[b].astype(F32) * mm_nt(e2, wout_ref[0])).astype(LOW)
-    x1 = x1_ref[b].astype(F32)
+    e1 = (held(s1_ref).astype(F32) * mm_nt(e2, wout_ref[0])).astype(LOW)
+    x1 = held(x1_ref).astype(F32)
     t1 = (x1 * gain_ref[0:1, :] + shift_ref[0:1, :]).astype(LOW)
     add(feeds_ref, M_IN, mm_tn(t1, e1[:, :width]))
     add(feeds_ref, M_IN + width, mm_tn(t1, e1[:, width:]))
@@ -301,45 +343,64 @@
     add(small_ref, S_GAIN, col_sum(g1 * x1))
     add(small_ref, S_SHIFT, col_sum(g1))
     g1 = ln_back(g1, x1, wide(r1_ref), gain_ref[0:1, :])
-    g1_ref[b] = g1
+    keep(g1_ref, g1)
     et = g1.astype(LOW)
-    add(feeds_ref, M_O, mm_tn(tc_ref[b], et))
+    add(feeds_ref, M_O, mm_tn(held(tc_ref), et))
     add(small_ref, S_BIAS + 2, col_sum(et))
-    etc_ref[b] = mm_nt(et, wo_ref[0]).astype(LOW)
-    for v in range(lvars):
+    etc = mm_nt(et, wo_ref[0]).astype(LOW)
+    keep(etc_ref, etc)
+    prob = held(p_ref)
+    grads = []
+    for v in range(several * lvars):
         part = slice(v * segs, (v + 1) * segs)
-        tc_ref[b, part, :] = mm(p_ref[b, part, :], spread_heads(etc_ref[b, part, :], heads_ref)).astype(LOW)
-    low = ((tok_ref[b].reshape(rows, width).astype(F32) - offset) * factor).astype(LOW)
-    add(feeds_ref, M_V, mm_tn(low, tc_ref[b]))
-    add(small_ref, S_BIAS + 1, col_sum(tc_ref[b]))
-
-
-def time_backward(lvars, b, tok_ref, offset, factor, heads_ref, headsf_ref, kept, times_ref, small_ref, etc_ref):
+        grads.append(mm(prob[part], spread_heads(etc[part], heads_ref)).astype(LOW))
+    gv = jnp.concatenate(grads, axis=0)
+    keep(tc_ref, gv)
+    low = start_low(lvars, b, several, tok_ref, offsets, factors)
+    add(feeds_ref, M_V, mm_tn(low, gv))
+    add(small_ref, S_BIAS + 1, col_sum(gv))
+
+
+def start_low(lvars, b, several, tok_ref, offsets, factors):
+    segs, width = tok_ref.shape[2:]
+    tok = [tok_ref[b + i].reshape(lvars * segs, width).astype(F32) for i in range(several)]
+    return jnp.concatenate([((tok[i] - offsets[i]) * factors[i]).astype(LOW) for i in range(several)], axis=0)
+
+
+def time_backward(
+    lvars, b, several, tok_ref, offsets, factors, heads_ref, headsf_ref, kept, times_ref, small_ref, etc_ref
+):
     q_ref, k_ref, v_ref, p_ref = kept[:4]
     segs, width = tok_ref.shape[2:]
     rows = lvars * segs
     scale = np.float32((width // HEADS) ** (-0.5))
 
-    @pl.when(b == 0)
-    def _():
-        times_ref[...] = jnp.zeros(times_ref.shape, F32)
-
     def add(ref, row, value):
         ref[row : row + value.shape[0], :] += value
 
-    for v in range(lvars):
+    def held(ref):
+        return ref[pl.ds(b, several)].reshape(several * rows, ref.shape[2])
+
+    def keep(ref, value):
+        ref[pl.ds(b, several)] = value.reshape(several, rows, value.shape[1])
+
+    etc, query, key, value, probs = held(etc_ref), held(q_ref), held(k_ref), held(v_ref), held(p_ref)
+    grads_q, grads_k = [], []
+    for v in range(several * lvars):
         part = slice(v * segs, (v + 1) * segs)
-        ex = spread_heads(etc_ref[b, part, :], heads_ref)
-        prob = p_ref[b, part, :].astype(F32)
-        weighted = prob * mm_nt(v_ref[b, part, :], ex)
+        prob = probs[part].astype(F32)
+        weighted = prob * mm_nt(value[part], spread_heads(etc[part], heads_ref))
         ets = (weighted - prob * jnp.sum(weighted, axis=0, keepdims=True)).astype(LOW)
-        gk = (scale * mm(ets, spread_heads(q_ref[b, part, :], heads_ref))).astype(LOW)
-        q_ref[b, part, :] = (scale * gather_heads(mm_tn(ets, k_ref[b, part, :]), headsf_ref, segs)).astype(LOW)
-        k_ref[b, part, :] = gk
-    low = ((tok_ref[b].reshape(rows, width).astype(F32) - offset) * factor).astype(LOW)
-    add(times_ref, T_Q, mm_tn(low, q_ref[b]))
-    add(times_ref, T_K, mm_tn(low, k_ref[b]))
-    add(small_ref, S_BIAS, col_sum(q_ref[b]))
+        grads_k.append((scale * mm(ets, spread_heads(query[part], heads_ref))).astype(LOW))
+        grads_q.append((scale * gather_heads(mm_tn(ets, key[part]), headsf_ref, segs)).astype(LOW))
+    gq = jnp.concatenate(grads_q, axis=0)
+    gk = jnp.concatenate(grads_k, axis=0)
+    keep(q_ref, gq)
+    keep(k_ref, gk)
+    low = start_low(lvars, b, several, tok_ref, offsets, factors)
+    add(times_ref, T_Q, mm_tn(low, gq))
+    add(times_ref, T_K, mm_tn(low, gk))
+    add(small_ref, S_BIAS, col_sum(gq))
 
 
 class Sum:
@@ -520,14 +581,16 @@
             device_id_type=MESH,
         )
 
-    def store(kind, b, value):
-        value = value.reshape(var_size, block, width)
-        sent_ref[kind, b] = value
-        came_ref[kind, b, me] = sent_ref[kind, b, me]
-
-    def send(kind, b):
-        for k in range(1, var_size):
-            copy(kind, b, k).start()
+    def store(kind, b, several, value):
+        value = value.reshape(several, var_size, block, width)
+        sent_ref[kind, pl.ds(b, several)] = value
+        for i in range(several):
+            came_ref[kind, b + i, me] = sent_ref[kind, b + i, me]
+
+    def send(kind, b, several=1):
+        for i in range(several):
+            for k in range(1, var_size):
+                copy(kind, b + i, k).start()
 
     def pick(b, ref):
         total = jnp.zeros((1, width), F32)
@@ -535,9 +598,13 @@
             total = total + jnp.where(dom_ref[b] == d, ref[d : d + 1, :], 0.0)
         return total
 
-    def arrived(kind, b):
-        whole(kind, b).wait_recv()
-        return came_ref[kind, b]
+    def picks(b, several, ref):
+        return [pick(b + i, ref) for i in range(several)]
+
+    def arrived(kind, b, several):
+        for i in range(several):
+            whole(kind, b + i).wait_recv()
+        return came_ref[kind, pl.ds(b, several)].reshape(several * rows, width)
 
     pieces = [
         (times, T_Q, 2 * width, inner_ref, 0), (feeds, M_V, width, inner_ref, 2 * width), (attns, B_SQ, 6 * width, inner_ref, 3 * width),
@@ -569,54 +636,66 @@
             peer = {"seg": i * cores + lax.rem(core + k, cores)}
             pl.semaphore_signal(barrier, inc=1, device_id=peer, device_id_type=MESH)
     small.acc[...] = jnp.zeros_like(small.acc)
-
-    def forward(b):
-        store(1, b, mm(split_ref[...], cot_ref[b].reshape(rows, width)).astype(LOW))
+    router_start(
+        router_ref, wi_ref, ab_ref, grow_ref, mask_ref, attns[2], routes[2], qx_ref, kq_ref
+    )
+    feeds[2][...] = jnp.zeros(feeds[2].shape, F32)
+    times[2][...] = jnp.zeros(times[2].shape, F32)
+    pl.semaphore_wait(barrier, spaces - 1 + (cores - 1) * xs)
+
+    def forward(b, several):
+        for i in range(several):
+            store(1, b + i, 1, mm(split_ref[...], cot_ref[b + i].reshape(rows, width)).astype(LOW))
+        send(1, b, several)
         t2 = time_forward(
-            lvars, b, tok_ref, pick(b, mean_ref), pick(b, scale_ref), wi_ref, wo_ref, ab_ref, win_ref, bin_ref,
-            wout_ref, bout_ref, gain_ref, shift_ref, heads_ref, headsf_ref, kept,
+            lvars, b, several, tok_ref, picks(b, several, mean_ref), picks(b, several, scale_ref), wi_ref, wo_ref,
+            ab_ref, win_ref, bin_ref, wout_ref, bout_ref, gain_ref, shift_ref, heads_ref, headsf_ref, kept,
         )
-        store(0, b, mm(split_ref[...], t2).astype(LOW))
-
-        @pl.when(b == 0)
-        def _():
-            pl.semaphore_wait(barrier, spaces - 1 + (cores - 1) * xs)
-
-        send(0, b)
-        send(1, b)
-
-    def middle(b):
+        for i in range(several):
+            store(0, b + i, 1, mm(split_ref[...], t2[i * rows : (i + 1) * rows]).astype(LOW))
+        send(0, b, several)
+
+    def middle(b, several):
         def leaving(kind, value):
-            store(kind, b, value)
+            store(kind, b, several, value)
             if kind == 2:
-                send(2, b)
-
-        limit = jnp.int32(0)
-        for d in range(cnt_ref.shape[0]):
-            limit = limit + jnp.where(dom_ref[b] == d, cnt_ref[d], 0)
+                send(2, b, several)
+
+        limits = []
+        for i in range(several):
+            limit = jnp.int32(0)
+            for d in range(cnt_ref.shape[0]):
+                limit = limit + jnp.where(dom_ref[b + i] == d, cnt_ref[d], 0)
+            limits.append(limit)
         router_part(
-            lsegs, nvars, routers, steps, b, lambda kind: arrived(kind, b), leaving,
-            limit, router_ref, wi_ref, wo_ref, ab_ref, win_ref, bin_ref, wout_ref, bout_ref,
+            lsegs, nvars, routers, several, lambda kind: arrived(kind, b, several), leaving,
+            limits, wi_ref, wo_ref, ab_ref, win_ref, bin_ref, wout_ref, bout_ref,
             gain_ref, shift_ref, mask_ref, grow_ref, shrink_ref, sumr_ref, swap_ref, back_ref,
-            attns[2], routes[2], small.acc, qx_ref, kq_ref, me * lsegs, var_size,
+            attns[2], routes[2], small.acc, qx_ref, kq_ref,
         )
 
-    def back_feed(b):
+    def back_feed(b, several):
         feed_backward(
-            lvars, b, lambda kind: arrived(kind, b), tok_ref, pick(b, mean_ref), pick(b, scale_ref), wo_ref, win_ref,
-            wout_ref, gain_ref, shift_ref, heads_ref, join_ref, kept, feeds[2], small.acc, etc_ref, g1_ref,
+            lvars, b, several, lambda kind: arrived(kind, b, several), tok_ref, picks(b, several, mean_ref),
+            picks(b, several, scale_ref), wo_ref, win_ref, wout_ref, gain_ref, shift_ref, heads_ref, join_ref, kept,
+            feeds[2], small.acc, etc_ref, g1_ref,
         )
 
-    def back_time(b):
+    def back_time(b, several):
         time_backward(
-            lvars, b, tok_ref, pick(b, mean_ref), pick(b, scale_ref), heads_ref, headsf_ref, kept, times[2], small.acc,
-            etc_ref,
+            lvars, b, several, tok_ref, picks(b, several, mean_ref), picks(b, several, scale_ref), heads_ref, headsf_ref,
+            kept, times[2], small.acc, etc_ref,
         )
 
-    def back_input(b):
-        grad = g1_ref[b] + mm_nt(kept[0][b], wi_ref[0, 0]) + mm_nt(kept[1][b], wi_ref[0, 1])
-        g1_ref[b] = (grad + mm_nt(kept[4][b], wi_ref[0, 2])) * pick(b, scale_ref)
-        series_out(1, b).start()
+    def back_input(b, several):
+        def held(ref):
+            return ref[pl.ds(b, several)].reshape(several * rows, width)
+
+        grad = held(g1_ref) + mm_nt(held(kept[0]), wi_ref[0, 0]) + mm_nt(held(kept[1]), wi_ref[0, 1])
+        grad = grad + mm_nt(held(kept[4]), wi_ref[0, 2])
+        for i in range(several):
+            g1_ref[b + i] = grad[i * rows : (i + 1) * rows] * pick(b + i, scale_ref)
+            series_out(1, b + i).start()
 
     todo = {}
 
@@ -632,26 +711,57 @@
     todo.setdefault(2 * steps, []).append(functools.partial(small.start, 0))
     todo.setdefault(2 * steps + steps // 2, []).append(lambda: (small.finish(0), small.start(1)))
 
-    def sweep(run, first):
-        def body(b, carry):
+    def sweep(run, first, several):
+        def body(i, carry):
+            b = i * several
             for round_, acts in sorted(todo.items()):
                 if first <= round_ < first + steps:
 
-                    @pl.when(b == round_ - first)
+                    @pl.when(i == (round_ - first) // several)
                     def _(acts=acts):
                         for act in acts:
                             act()
 
-            run(b)
+            run(b, several)
             return carry
 
-        lax.fori_loop(0, steps, body, 0)
-
-    sweep(forward, -2 * steps)
-    sweep(middle, -steps)
-    sweep(back_feed, 0)
-    sweep(back_time, steps)
-    sweep(back_input, 2 * steps)
+        lax.fori_loop(0, steps // several, body, 0)
+
+    together = TOGETHER if len(sums) > 1 else (1,) * 5
+    sweep(forward, -2 * steps, together[0])
+    sweep(middle, -steps, together[1])
+    router_end(
+        lsegs, routers, var_size, me * lsegs, router_ref, wi_ref, shrink_ref, mask_ref, attns[2], routes[2], small.acc,
+        kq_ref,
+    )
+    several = together[2]
+    count = steps // several
+    early = max(count - AHEAD, 1)
+
+    def backward(i, carry):
+        for round_, acts in sorted(todo.items()):
+            if 0 <= round_ < 2 * steps:
+
+                @pl.when(i == round_ // several)
+                def _(acts=acts):
+                    for act in acts:
+                        act()
+
+        lead = early + early - 1
+        feed = (i < early) | ((i >= lead) & (i < lead + count - early))
+
+        @pl.when(feed)
+        def _():
+            back_feed(jnp.where(i < early, i, i - lead + early) * several, several)
+
+        @pl.when(jnp.logical_not(feed))
+        def _():
+            back_time(jnp.where(i < lead, i - early, i - count) * several, several)
+
+        return carry
+
+    lax.fori_loop(0, 2 * count, backward, 0)
+    sweep(back_input, 2 * steps, together[4])
     last = [max(rounds[: total.turns]) for total, rounds in zip(sums, rounds_of)]
     for round_ in range(3 * steps, max(max(todo), *last) + 1):
         for act in todo.get(round_, []):

time: 154 us -> 153 us (level)
  the two profiles are of different devices: /device:TPU:0 before, /device:TPU:29 now
where the time goes in v5:
time: 153 us
  Pallas kernels  150 us (98%)
  local copies, waits for them, and re-layouts  1.61 us (1%)
    pallas_call x1, Pallas kernels, on_device(): pl.pallas_call(functools.partial(layer_kernel, lvars, lsegs, nvars, route...  143 us
    pallas_call x1, Pallas kernels, on_device(): pl.pallas_call(functools.partial(finish_kernel, segs, lvars), grid=(turns...  6.8 us

profile of v5, /device:TPU:29, one launch (start us, length us, event | category | flops | bytes accessed | tf_op | source)
XLA Modules:
  0.0 152.5 jit_solution(1211281459312007083)
XLA Ops:
  0.6 0.0 copy-start
  0.7 1.0 copy-done
  1.6 0.6 pad_bitcast_fusion.router_ref
  2.3 143.3 %layer.1 = (f32[32,256]{1,0:T(8,128)}, bf16[8,8,32,256]{3,2,1,0:T(8,128)(2,1)}, f32[8,256,256]{2,1,0:T(8,128)}, bf16[2304,256]{1,0:T(8,128)(2,1)}, bf16[768,256]...) custom-call(s32[8]{0:T(128)} %dom_ref.1, s32[4]{0:T(128)} %cnt_ref.1, ...), custom_call_target="tpu_custom_call" | custom-call | tf_op jit(solution)/shard_map/layer/pallas_call | solution.py:893
  145.5 6.8 %finish.1 = (f32[8,4,64,256]{3,2,1,0:T(8,128)}, f32[8,256,256]{2,1,0:T(8,128)}, f32[2304,256]{1,0:T(8,128)}, f32[768,256]{1,0:T(8,128)}, f32[3,3,256]{2,1,0:T(4,...) custom-call(bf16[8,8,32,256]{3,2,1,0:T(8,128)(2,1)} %get-tuple-eleme, ...), custom_call_target="tpu_custom_call" | custom-call | tf_op jit(solution)/shard_map/finish/pallas_call | solution.py:931
  (1 shorter events, 0.0 us)
Async XLA Ops:
  0.6 1.0 copy-start

commit v6 on v5

--- a/solution.py
+++ b/solution.py
@@ -23,6 +23,9 @@
 ROUTE_ROUNDS = (1, 3, 12, 16, 18, 20, 22)
 FEED_ROUNDS = (12, 14, 16, 18, 20, 22, 24)
 TIME_ROUNDS = (16, 17, 19, 22, 23)
+ATTN_AXES = ("core", "plane", "z")
+ROUTE_AXES = ("core", "plane", "z")
+FEED_AXES = ("core", "plane", "z")
 TOGETHER = (2, 2, 2, 2, 2)
 AHEAD = 1
 
@@ -129,33 +132,36 @@
     return (x2 * gain_ref[1:2, :] + shift_ref[1:2, :]).astype(LOW)
 
 
-B_SQ, B_SK, B_SV, B_RQ, B_RK, B_RV, B_O1, B_O2, B_ROWS = [256 * i for i in range(9)]
-R_IN, R_OUT, R_ROUTE = [256 * i for i in (0, 2, 4)]
+B_SK, B_SV, B_RQ, B_RK, B_RV, B_O1, B_ROWS = [256 * i for i in range(7)]
+R_IN, R_OUT, R_O2, R_KQ = [256 * i for i in (0, 2, 4, 5)]
 M_IN, M_OUT, M_V, M_O, M_ROWS = [256 * i for i in (0, 2, 4, 5, 6)]
 T_Q, T_K, T_ROWS = [256 * i for i in (0, 1, 2)]
 S_BIAS, S_IN, S_OUT, S_GAIN, S_SHIFT, S_ROWS = 0, 9, 13, 15, 19, 32
 
 
-def router_start(router_ref, wi_ref, ab_ref, grow_ref, mask_ref, attn_ref, rest_ref, qx_ref, kq_ref):
+def router_start(places, router_ref, wi_ref, ab_ref, grow_ref, mask_ref, attn_ref, rest_ref, qx_ref, kq_ref):
     attn_ref[...] = jnp.zeros(attn_ref.shape, F32)
     rest_ref[...] = jnp.zeros(rest_ref.shape, F32)
     kq_ref[...] = jnp.zeros(kq_ref.shape, F32)
-    sq = (mm(router_ref[...], wi_ref[1, 0]) + ab_ref[1, 0:1, :]).astype(LOW)
+    mine = mm(places, router_ref[...]).astype(LOW)
+    sq = (mm(mine, wi_ref[1, 0]) + ab_ref[1, 0:1, :]).astype(LOW)
     qx_ref[...] = expand(sq, grow_ref, mask_ref)
 
 
-def router_end(lsegs, routers, var_size, first_seg, router_ref, wi_ref, shrink_ref, mask_ref, attn_ref, rest_ref, small_ref, kq_ref):
-    width = router_ref.shape[1]
+def router_end(lsegs, routers, var_size, first_seg, shrink_ref, mask_ref, rest_ref, small_ref, kq_ref):
     kq = contract(kq_ref[...], shrink_ref, mask_ref)
-    kq_low = kq.astype(LOW)
-    attn_ref[B_SQ : B_SQ + width, :] = mm_tn(router_ref[...], kq_low)
     small_ref[S_BIAS + 3 : S_BIAS + 4, :] = col_sum(kq)
-    places = routers * lsegs * var_size
-    there = lax.broadcasted_iota(jnp.int32, (places, lsegs * SLOTS), 0)
-    here = lax.broadcasted_iota(jnp.int32, (places, lsegs * SLOTS), 1)
+    places = own_places(lsegs, routers, var_size, first_seg, 0)
+    rest_ref[R_KQ : R_KQ + places.shape[0], :] = mm(places, kq.astype(LOW))
+
+
+def own_places(lsegs, routers, var_size, first_seg, whole):
+    shape = [lsegs * SLOTS] * 2
+    shape[whole] = routers * lsegs * var_size
+    there = lax.broadcasted_iota(jnp.int32, shape, whole)
+    here = lax.broadcasted_iota(jnp.int32, shape, 1 - whole)
     here = lax.div(here, lsegs) * (lsegs * var_size) + lax.rem(here, lsegs) + first_seg
-    here = jnp.where(there == here, 1.0, 0.0).astype(LOW)
-    rest_ref[R_ROUTE : R_ROUTE + places, :] = mm(here, mm_nt(kq_low, wi_ref[1, 0]).astype(LOW))
+    return jnp.where(there == here, 1.0, 0.0).astype(LOW)
 
 
 def expand(x, grow_ref, mask_ref):
@@ -266,7 +272,7 @@
     add_small(S_SHIFT + 2, col_sum(g3))
     g3 = ln_back(g3, x3, r3, gain_ref[2:3, :])
     eo = g3.astype(LOW)
-    add(B_O2, mm_tn(rc, eo))
+    add(R_O2, mm_tn(rc, eo), rest_ref)
     add_small(S_BIAS + 8, col_sum(eo))
     ec = mm_nt(eo, wo_ref[2]).astype(LOW)
     dp = cat(mm_nt(ec[ns[j]], rvx[ls[j]]) for j in parts)
@@ -527,7 +533,7 @@
     dom_ref, cnt_ref, tok_ref, cot_ref, mean_ref, scale_ref, router_ref, wi_ref, wo_ref, ab_ref,
     win_ref, bin_ref, wout_ref, bout_ref, gain_ref, shift_ref, heads_ref, headsf_ref, split_ref, join_ref, mask_ref, grow_ref, shrink_ref, sumr_ref, swap_ref, back_ref,
     small_out_ref, out_ref, gin_ref, inner_ref, outer_ref, up_ref, down_ref, route_ref,
-    sent_ref, came_ref, qx_ref, kq_ref, etc_ref, g1_ref, send_sem, recv_sem, out_sem, *scratch,
+    sent_ref, came_ref, qx_ref, kq_ref, etc_ref, g1_ref, made_ref, send_sem, recv_sem, out_sem, *scratch,
 ):
     me = lax.axis_index("var")
     seg = lax.axis_index("seg")
@@ -538,6 +544,8 @@
     cores, xs, ys, zs = sizes
     core, xi = lax.rem(seg, cores), lax.div(seg, cores)
     yi, zi = lax.rem(me, ys), lax.div(me, ys)
+    pairs = 2 if zs % 2 == 0 else 1
+    zl, zh = lax.rem(zi, pairs), lax.div(zi, pairs)
 
     def space(i):
         return {"seg": lax.rem(i, xs) * cores + core, "var": lax.div(i, xs)}
@@ -547,6 +555,10 @@
         "plane": (yi * xs + xi, xs * ys, lambda i: space(zi * (xs * ys) + i)),
         "z": (zi, zs, lambda i: {"var": i * ys + yi}),
         "space": (me * xs + xi, var_size * xs, space),
+        "x": (xi, xs, lambda i: {"seg": i * cores + core}),
+        "y": (yi, ys, lambda i: {"var": zi * ys + i}),
+        "pair": (zl, pairs, lambda i: {"var": (zh * pairs + i) * ys + yi}),
+        "far": (zh, zs // pairs, lambda i: {"var": (i * pairs + zl) * ys + yi}),
     }
     sums = []
     for _, names in groups:
@@ -607,24 +619,33 @@
         return came_ref[kind, pl.ds(b, several)].reshape(several * rows, width)
 
     pieces = [
-        (times, T_Q, 2 * width, inner_ref, 0), (feeds, M_V, width, inner_ref, 2 * width), (attns, B_SQ, 6 * width, inner_ref, 3 * width),
-        (feeds, M_O, width, outer_ref, 0), (attns, B_O1, 2 * width, outer_ref, width),
+        (times, T_Q, 2 * width, inner_ref, 0), (feeds, M_V, width, inner_ref, 2 * width), (None, 0, width, inner_ref, 3 * width),
+        (attns, B_SK, 5 * width, inner_ref, 4 * width),
+        (feeds, M_O, width, outer_ref, 0), (attns, B_O1, width, outer_ref, width), (routes, R_O2, width, outer_ref, 2 * width),
         (feeds, M_IN, 2 * width, up_ref, 0), (routes, R_IN, 2 * width, up_ref, 2 * width),
         (feeds, M_OUT, 2 * width, down_ref, 0), (routes, R_OUT, 2 * width, down_ref, 2 * width),
-        (routes, R_ROUTE, route_ref.shape[0], route_ref, 0),
+        (None, width, route_ref.shape[0], route_ref, 0),
     ]
 
     def deliver(which):
         return [
             pltpu.make_async_copy(
-                which.total.at[pl.ds(base + row, count), :], ref.at[pl.ds(there, count), :], out_sem.at[index]
+                (made_ref if part is None else which.total).at[pl.ds((0 if part is None else part[1]) + row, count), :],
+                ref.at[pl.ds(there, count), :],
+                out_sem.at[index],
             )
-            for index, ((total, base, _), row, count, ref, there) in enumerate(pieces)
-            if total is which
+            for index, (part, row, count, ref, there) in enumerate(pieces)
+            if (routes if part is None else part)[0] is which
         ]
 
+    def make_routes():
+        total, base, _ = routes
+        kq = total.total[base + R_KQ : base + R_KQ + route_ref.shape[0], :]
+        made_ref[:width, :] = mm_tn(router_ref[...], kq).astype(LOW)
+        made_ref[width:, :] = mm_nt(kq, wi_ref[1, 0]).astype(LOW)
+
     def series_out(kind, b):
-        source, ref = ((came_ref.at[3, b], out_ref), (g1_ref.at[b], gin_ref))[kind]
+        source, ref = ((came_ref.at[3, b], out_ref), (etc_ref.at[b], gin_ref))[kind]
         return pltpu.make_async_copy(source, ref.at[b], out_sem.at[len(pieces) + kind * steps + b])
 
     barrier = pltpu.get_barrier_semaphore()
@@ -637,7 +658,7 @@
             pl.semaphore_signal(barrier, inc=1, device_id=peer, device_id_type=MESH)
     small.acc[...] = jnp.zeros_like(small.acc)
     router_start(
-        router_ref, wi_ref, ab_ref, grow_ref, mask_ref, attns[2], routes[2], qx_ref, kq_ref
+        own_places(lsegs, routers, var_size, me * lsegs, 1), router_ref, wi_ref, ab_ref, grow_ref, mask_ref, attns[2], routes[2], qx_ref, kq_ref
     )
     feeds[2][...] = jnp.zeros(feeds[2].shape, F32)
     times[2][...] = jnp.zeros(times[2].shape, F32)
@@ -694,7 +715,7 @@
         grad = held(g1_ref) + mm_nt(held(kept[0]), wi_ref[0, 0]) + mm_nt(held(kept[1]), wi_ref[0, 1])
         grad = grad + mm_nt(held(kept[4]), wi_ref[0, 2])
         for i in range(several):
-            g1_ref[b + i] = grad[i * rows : (i + 1) * rows] * pick(b + i, scale_ref)
+            etc_ref[b + i] = (grad[i * rows : (i + 1) * rows] * pick(b + i, scale_ref)).astype(LOW)
             series_out(1, b + i).start()
 
     todo = {}
@@ -731,8 +752,7 @@
     sweep(forward, -2 * steps, together[0])
     sweep(middle, -steps, together[1])
     router_end(
-        lsegs, routers, var_size, me * lsegs, router_ref, wi_ref, shrink_ref, mask_ref, attns[2], routes[2], small.acc,
-        kq_ref,
+        lsegs, routers, var_size, me * lsegs, shrink_ref, mask_ref, routes[2], small.acc, kq_ref,
     )
     several = together[2]
     count = steps // several
@@ -763,11 +783,13 @@
     lax.fori_loop(0, 2 * count, backward, 0)
     sweep(back_input, 2 * steps, together[4])
     last = [max(rounds[: total.turns]) for total, rounds in zip(sums, rounds_of)]
-    for round_ in range(3 * steps, max(max(todo), *last) + 1):
+    for round_ in range(3 * steps, max(max(todo), 3 * steps, *last) + 1):
         for act in todo.get(round_, []):
             act()
         for total, end in zip(sums, last):
             if round_ == max(end, 3 * steps):
+                if total is routes[0]:
+                    make_routes()
                 for copy in deliver(total):
                     copy.start()
     small.finish(1)
@@ -807,7 +829,7 @@
 
     for i in range(out_ref.shape[0]):
         output_ref[i] = mm(join_ref[...], out_ref[i].reshape(lvars * segs, width)).reshape(lvars, segs, width)
-    gin_out_ref[...] = gin_ref[...]
+    gin_out_ref[...] = gin_ref[...].astype(F32)
     ginner_ref[...] = inner_ref[...].astype(F32)
     gouter_ref[...] = outer_ref[...].astype(F32)
     gup_ref[0, :, :width] = up_ref[0, 0].astype(F32)
@@ -833,8 +855,6 @@
     nvars = lvars * var_size
     rows = lvars * segs
     lanes = SLOTS * HEADS
-    me = lax.axis_index("var")
-
     heads = (np.arange(width)[None, :] // (width // HEADS) == np.arange(HEADS)[:, None]).astype(np.float32)
     heads_low = jnp.asarray(heads, LOW)
     heads_f = jnp.asarray(heads, F32)
@@ -853,8 +873,7 @@
         ((rows, width), LOW), ((rows, width), LOW), ((rows, 128), F32), ((rows, hidden), LOW),
         ((rows, hidden), LOW), ((rows, width), LOW), ((rows, 128), F32),
     ]
-    mine = lax.dynamic_slice_in_dim(router.transpose(1, 0, 2), me * lsegs, lsegs, 1)
-    mine = jnp.pad(mine, ((0, SLOTS - routers), (0, 0), (0, 0))).reshape(SLOTS * lsegs, width)
+    routes = router.transpose(1, 0, 2).reshape(routers * segs, width)
     consts = [jnp.asarray(x, LOW) for x in (split, split.T)] + [mask]
     consts += [jnp.asarray(x, LOW) for x in (grow, grow.T, sumr, swap, swap.T)]
 
@@ -863,11 +882,15 @@
     ys = xs if var_size % xs == 0 else 1
     zs = var_size // ys
     sizes = (cores, xs, ys, zs)
-    counts_of = {"core": cores, "plane": xs * ys, "z": zs, "space": var_size * xs}
+    pairs = 2 if zs % 2 == 0 else 1
+    counts_of = {
+        "core": cores, "plane": xs * ys, "z": zs, "space": var_size * xs, "x": xs, "y": ys, "pair": pairs,
+        "far": zs // pairs,
+    }
     far = ("core", "plane", "z")
     near = ("core", "space") if var_size * xs <= 16 else far
     unit = 16 * var_size * seg_size
-    wanted = [(B_ROWS, far), (R_ROUTE + segs * routers, far), (M_ROWS, far), (T_ROWS, near)]
+    wanted = [(B_ROWS, ATTN_AXES), (R_KQ + segs * routers, ROUTE_AXES), (M_ROWS, FEED_AXES), (T_ROWS, near)]
     if unit > 1024:
         starts = np.cumsum([0] + [count for count, _ in wanted])
         parts = [(0, int(start), count) for start, (count, _) in zip(starts, wanted)]
@@ -882,7 +905,7 @@
     out_shapes = [
         jax.ShapeDtypeStruct((S_ROWS, width), F32),
         jax.ShapeDtypeStruct((batch, var_size, rows // var_size, width), LOW),
-        jax.ShapeDtypeStruct((batch, rows, width), F32),
+        jax.ShapeDtypeStruct((batch, rows, width), LOW),
         jax.ShapeDtypeStruct((9 * width, width), LOW),
         jax.ShapeDtypeStruct((3 * width, width), LOW),
         jax.ShapeDtypeStruct((4 * width, width), LOW),
@@ -902,9 +925,10 @@
             pltpu.VMEM((lsegs * lanes, width), F32),
             pltpu.VMEM((batch, rows, width), LOW),
             pltpu.VMEM((batch, rows, width), F32),
+            pltpu.VMEM((width + routers * segs, width), LOW),
             pltpu.SemaphoreType.DMA((4, batch)),
             pltpu.SemaphoreType.DMA((4, batch)),
-            pltpu.SemaphoreType.DMA((10 + 2 * batch,)),
+            pltpu.SemaphoreType.DMA((12 + 2 * batch,)),
             *[pltpu.VMEM((batch,) + shape, dtype) for shape, dtype in kept],
             *[x for count, names in groups for x in Sum.scratch(count, width, [counts_of[name] for name in names])],
             *SmallSum.scratch(S_ROWS, width, (seg_size, var_size)),
@@ -914,7 +938,7 @@
         ),
         name="layer",
     )(
-        domain, counts, tokens, cotangent, domain_mean, domain_scale, mine, attn_inner, attn_outer, attn_bias, mlp_in,
+        domain, counts, tokens, cotangent, domain_mean, domain_scale, routes, attn_inner, attn_outer, attn_bias, mlp_in,
         mlp_in_bias, mlp_out, mlp_out_bias, norm_gain, norm_bias, heads_low, heads_f, *consts,
     )
 

time: 153 us -> 147 us (0.961)
  Pallas kernels: 150 us -> 146 us
  local copies, waits for them, and re-layouts: 1.61 us -> 0 us
    pallas_call x1, Pallas kernels: 143 us -> 139 us  [on_device(): pl.pallas_call(functools.partial(layer_kernel, lvars, lsegs, nvars, route...]
where the time goes in v6:
time: 147 us
  Pallas kernels  146 us (99%)
    pallas_call x1, Pallas kernels, on_device(): pl.pallas_call(functools.partial(layer_kernel, lvars, lsegs, nvars, route...  139 us
    pallas_call x1, Pallas kernels, on_device(): pl.pallas_call(functools.partial(finish_kernel, segs, lvars), grid=(turns...  6.73 us

profile of v6, /device:TPU:29, one launch (start us, length us, event | category | flops | bytes accessed | tf_op | source)
XLA Modules:
  0.0 147.1 jit_solution(2763165357343030255)
XLA Ops:
  0.7 139.5 %layer.1 = (f32[32,256]{1,0:T(8,128)}, bf16[8,8,32,256]{3,2,1,0:T(8,128)(2,1)}, bf16[8,256,256]{2,1,0:T(8,128)(2,1)}, bf16[2304,256]{1,0:T(8,128)(2,1)}, bf16[76...) custom-call(s32[8]{0:T(128)} %dom_ref.1, s32[4]{0:T(128)} %cnt_ref.1, ...), custom_call_target="tpu_custom_call" | custom-call | tf_op jit(solution)/shard_map/layer/pallas_call | solution.py:916
  140.2 6.7 %finish.1 = (f32[8,4,64,256]{3,2,1,0:T(8,128)}, f32[8,256,256]{2,1,0:T(8,128)}, f32[2304,256]{1,0:T(8,128)}, f32[768,256]{1,0:T(8,128)}, f32[3,3,256]{2,1,0:T(4,...) custom-call(bf16[8,8,32,256]{3,2,1,0:T(8,128)(2,1)} %get-tuple-eleme, ...), custom_call_target="tpu_custom_call" | custom-call | tf_op jit(solution)/shard_map/finish/pallas_call | solution.py:955

commit v7 on v6

--- a/solution.py
+++ b/solution.py
@@ -18,7 +18,7 @@
 VMEM_LIMIT = 60 * 1024 * 1024
 
 
-OUT_ROUNDS = (-2, -2, 0, 2, 4, 8, 12, 14)
+OUT_ROUNDS = (-2, 0, 2, 4, 8, 12, 16, 18)
 ATTN_ROUNDS = (0, 2, 9, 14, 17, 19, 21)
 ROUTE_ROUNDS = (1, 3, 12, 16, 18, 20, 22)
 FEED_ROUNDS = (12, 14, 16, 18, 20, 22, 24)
@@ -26,6 +26,7 @@
 ATTN_AXES = ("core", "plane", "z")
 ROUTE_AXES = ("core", "plane", "z")
 FEED_AXES = ("core", "plane", "z")
+
 TOGETHER = (2, 2, 2, 2, 2)
 AHEAD = 1
 
@@ -410,13 +411,14 @@
 
 
 class Sum:
-    def __init__(self, axes, acc, send, total, recv, sems):
+    def __init__(self, axes, second, acc, send, total, recv, sems):
+        self.second = second
         self.acc, self.send, self.total, self.recv, self.sems = acc, send, total, recv, sems
         self.plan = []
         start, size = 0, acc.shape[0]
-        for index, count, target in axes:
+        for index, count, target, peer, order in axes:
             size //= count
-            self.plan.append((index, count, target, start, size))
+            self.plan.append((index, count, target, start, size, peer, order))
             start = start + index * size
         self.levels = len(self.plan)
         self.last = 2 * self.levels
@@ -438,11 +440,12 @@
 
     def copies(self, level, gather):
         send_sem, recv_sem = self.sems[2:] if gather else self.sems[:2]
-        index, count, target, start, size = self.plan[level]
+        index, count, target, start, size, peer_at, order = self.plan[level]
         first = sum(entry[1] - 1 for entry in self.plan[:level])
         found = []
-        for k in range(1, count):
-            peer = lax.rem(index + k, count)
+        for k, k_second in zip(*order):
+            k = jnp.where(self.second, k_second, k)
+            peer = peer_at(k)
             rows = self.rows(start + (index if gather else peer) * size, size)
             copy = pltpu.make_async_remote_copy(
                 src_ref=(self.total if gather else self.send).at[rows, :],
@@ -460,7 +463,7 @@
         if 0 < turn <= levels:
             for copy, _ in self.copies(turn - 1, False):
                 copy.wait()
-            index, count, _, start, size = self.plan[turn - 1]
+            index, count, _, start, size = self.plan[turn - 1][:5]
             mine = self.rows(start + index * size, size)
             value = self.acc[mine, :]
             for k in range(count - 1):
@@ -544,27 +547,40 @@
     cores, xs, ys, zs = sizes
     core, xi = lax.rem(seg, cores), lax.div(seg, cores)
     yi, zi = lax.rem(me, ys), lax.div(me, ys)
-    pairs = 2 if zs % 2 == 0 else 1
-    zl, zh = lax.rem(zi, pairs), lax.div(zi, pairs)
 
     def space(i):
         return {"seg": lax.rem(i, xs) * cores + core, "var": lax.div(i, xs)}
 
+    def step(i, k, count):
+        return lax.rem(i + k, count)
+
+    def both_ways(count):
+        return list(range(1, count)), list(range(count - 1, 0, -1))
+
+    def line(index, count, target):
+        return index, count, target, lambda k: step(index, k, count), both_ways(count)
+
+    def plane_peer(k):
+        return step(yi, lax.div(k, xs), ys) * xs + step(xi, lax.rem(k, xs), xs)
+
+    def space_peer(k):
+        return step(zi, lax.div(k, xs * ys), zs) * (xs * ys) + plane_peer(lax.rem(k, xs * ys))
+
     axes = {
-        "core": (core, cores, lambda i: {"seg": xi * cores + i}),
-        "plane": (yi * xs + xi, xs * ys, lambda i: space(zi * (xs * ys) + i)),
-        "z": (zi, zs, lambda i: {"var": i * ys + yi}),
-        "space": (me * xs + xi, var_size * xs, space),
-        "x": (xi, xs, lambda i: {"seg": i * cores + core}),
-        "y": (yi, ys, lambda i: {"var": zi * ys + i}),
-        "pair": (zl, pairs, lambda i: {"var": (zh * pairs + i) * ys + yi}),
-        "far": (zh, zs // pairs, lambda i: {"var": (i * pairs + zl) * ys + yi}),
+        "core": line(core, cores, lambda i: {"seg": xi * cores + i}),
+        "plane": (
+            yi * xs + xi, xs * ys, lambda i: space(zi * (xs * ys) + i), plane_peer,
+            [sorted(range(1, xs * ys), key=lambda k: (k // xs > 0 and k % xs > 0, turn * k)) for turn in (1, -1)],
+        ),
+        "z": line(zi, zs, lambda i: {"var": i * ys + yi}),
+        "space": (me * xs + xi, var_size * xs, space, space_peer, both_ways(var_size * xs)),
     }
+    second = core > 0
     sums = []
     for _, names in groups:
         used = 7 + len(names)
         group, scratch = scratch[:used], scratch[used:]
-        sums.append(Sum([axes[name] for name in names], group[0], group[1], group[2], group[7:], group[3:7]))
+        sums.append(Sum([axes[name] for name in names], second, group[0], group[1], group[2], group[7:], group[3:7]))
     parts = []
     for index, base, count in shares:
         parts.append((sums[index], base, sums[index].acc.at[pl.ds(base, count), :]))
@@ -649,7 +665,7 @@
         return pltpu.make_async_copy(source, ref.at[b], out_sem.at[len(pieces) + kind * steps + b])
 
     barrier = pltpu.get_barrier_semaphore()
-    _, spaces, _ = axes["space"]
+    spaces = axes["space"][1]
     for k in range(1, spaces):
         pl.semaphore_signal(barrier, inc=1, device_id=space(lax.rem(axes["space"][0] + k, spaces)), device_id_type=MESH)
     for k in range(1, cores):
@@ -882,11 +898,7 @@
     ys = xs if var_size % xs == 0 else 1
     zs = var_size // ys
     sizes = (cores, xs, ys, zs)
-    pairs = 2 if zs % 2 == 0 else 1
-    counts_of = {
-        "core": cores, "plane": xs * ys, "z": zs, "space": var_size * xs, "x": xs, "y": ys, "pair": pairs,
-        "far": zs // pairs,
-    }
+    counts_of = {"core": cores, "plane": xs * ys, "z": zs, "space": var_size * xs}
     far = ("core", "plane", "z")
     near = ("core", "space") if var_size * xs <= 16 else far
     unit = 16 * var_size * seg_size
@@ -942,7 +954,7 @@
         mlp_in_bias, mlp_out, mlp_out_bias, norm_gain, norm_bias, heads_low, heads_f, *consts,
     )
 
-    turns = 4
+    turns = 2
 
     def shares(*shape):
         shape = (shape[0] // turns,) + shape[1:]

time: 147 us -> 143 us (0.973)
  Pallas kernels: 146 us -> 141 us
    pallas_call x1, Pallas kernels: 139 us -> 135 us  [on_device(): pl.pallas_call(functools.partial(layer_kernel, lvars, lsegs, nvars, route...]
where the time goes in v7:
time: 143 us; the launch traced here: 142 us
  Pallas kernels  141 us (99%)
    pallas_call x1, Pallas kernels, on_device(): pl.pallas_call(functools.partial(layer_kernel, lvars, lsegs, nvars, route...  135 us
    pallas_call x1, Pallas kernels, on_device(): pl.pallas_call(functools.partial(finish_kernel, segs, lvars), grid=(turns...  6.13 us

profile of v7, /device:TPU:29, one launch (start us, length us, event | category | flops | bytes accessed | tf_op | source)
XLA Modules:
  0.0 141.8 jit_solution(6425093346795386200)
XLA Ops:
  0.7 134.8 %layer.1 = (f32[32,256]{1,0:T(8,128)}, bf16[8,8,32,256]{3,2,1,0:T(8,128)(2,1)}, bf16[8,256,256]{2,1,0:T(8,128)(2,1)}, bf16[2304,256]{1,0:T(8,128)(2,1)}, bf16[76...) custom-call(s32[8]{0:T(128)} %dom_ref.1, s32[4]{0:T(128)} %cnt_ref.1, ...), custom_call_target="tpu_custom_call" | custom-call | tf_op jit(solution)/shard_map/layer/pallas_call | solution.py:928
  135.5 6.1 %finish.1 = (f32[8,4,64,256]{3,2,1,0:T(8,128)}, f32[8,256,256]{2,1,0:T(8,128)}, f32[2304,256]{1,0:T(8,128)}, f32[768,256]{1,0:T(8,128)}, f32[3,3,256]{2,1,0:T(4,...) custom-call(bf16[8,8,32,256]{3,2,1,0:T(8,128)(2,1)} %get-tuple-eleme, ...), custom_call_target="tpu_custom_call" | custom-call | tf_op jit(solution)/shard_map/finish/pallas_call | solution.py:967

commit v8 on v7

--- a/solution.py
+++ b/solution.py
@@ -27,7 +27,7 @@
 ROUTE_AXES = ("core", "plane", "z")
 FEED_AXES = ("core", "plane", "z")
 
-TOGETHER = (2, 2, 2, 2, 2)
+TOGETHER = (2, 2, 2, 2, 4)
 AHEAD = 1
 
 
@@ -462,7 +462,7 @@
         levels = self.levels
         if 0 < turn <= levels:
             for copy, _ in self.copies(turn - 1, False):
-                copy.wait()
+                copy.wait_recv()
             index, count, _, start, size = self.plan[turn - 1][:5]
             mine = self.rows(start + index * size, size)
             value = self.acc[mine, :]
@@ -474,7 +474,7 @@
                 self.total[mine, :] = value.astype(LOW)
         elif turn > levels:
             for copy, _ in self.copies(self.last - turn, True):
-                copy.wait()
+                copy.wait_recv()
         if turn < levels:
             for copy, rows in self.copies(turn, False):
                 self.send[rows, :] = self.acc[rows, :].astype(LOW)
@@ -482,6 +482,12 @@
         elif turn < self.last:
             for copy, _ in self.copies(self.last - 1 - turn, True):
                 copy.start()
+
+    def sent(self):
+        for level in range(self.levels):
+            for gather in (False, True):
+                for copy, _ in self.copies(level, gather):
+                    copy.wait_send()
 
     @property
     def turns(self):
@@ -817,6 +823,7 @@
         for kind in range(4):
             whole(kind, b).wait_send()
     for total in sums:
+        total.sent()
         for copy in deliver(total):
             copy.wait()
     for b in range(steps):

time: 143 us -> 143 us (level)
  no operation moved by 1% of the time
where the time goes in v8:
time: 143 us; the launch traced here: 142 us
  Pallas kernels  141 us (99%)
    pallas_call x1, Pallas kernels, on_device(): pl.pallas_call(functools.partial(layer_kernel, lvars, lsegs, nvars, route...  135 us
    pallas_call x1, Pallas kernels, on_device(): pl.pallas_call(functools.partial(finish_kernel, segs, lvars), grid=(turns...  6.13 us

profile of v8, /device:TPU:29, one launch (start us, length us, event | category | flops | bytes accessed | tf_op | source)
XLA Modules:
  0.0 142.2 jit_solution(16503023236433727023)
XLA Ops:
  0.7 135.3 %layer.1 = (f32[32,256]{1,0:T(8,128)}, bf16[8,8,32,256]{3,2,1,0:T(8,128)(2,1)}, bf16[8,256,256]{2,1,0:T(8,128)(2,1)}, bf16[2304,256]{1,0:T(8,128)(2,1)}, bf16[76...) custom-call(s32[8]{0:T(128)} %dom_ref.1, s32[4]{0:T(128)} %cnt_ref.1, ...), custom_call_target="tpu_custom_call" | custom-call | tf_op jit(solution)/shard_map/layer/pallas_call | solution.py:935
  135.9 6.1 %finish.1 = (f32[8,4,64,256]{3,2,1,0:T(8,128)}, f32[8,256,256]{2,1,0:T(8,128)}, f32[2304,256]{1,0:T(8,128)}, f32[768,256]{1,0:T(8,128)}, f32[3,3,256]{2,1,0:T(4,...) custom-call(bf16[8,8,32,256]{3,2,1,0:T(8,128)(2,1)} %get-tuple-eleme, ...), custom_call_target="tpu_custom_call" | custom-call | tf_op jit(solution)/shard_map/finish/pallas_call | solution.py:974
